TPU v7x, 256 devices: a whole 4x4x8 slice. The times are simulated.
256 devices in a mesh: dp: 16 (over y, x), vocab: 16 (over z, core).
Axes of the slice: x: 4, y: 4, z: 8, core: 2. Of those that a mesh axis runs over, the one named last changes fastest.
Arguments:
- hidden: bfloat16 [768, 4096], P(('dp', 'vocab')), may hold values from -240 to 240
- head_weight: bfloat16 [4096, 163840], P(None, ('dp', 'vocab')), may hold values from -0.40625 to 0.40625
- targets: int32 [768], P(('dp', 'vocab')), may hold values from 0 to 163839, as said below
- image_mask: int32 [768], P(('dp', 'vocab')), may hold values from 0 to 1
- lengths: int32 [16], replicated, may hold values from 12 to 48, as said below
- ref_logps: float32 [16], replicated, may hold values from -18 to -13
- pairing: int32 [16], replicated, may hold values from 0 to 15, each once
Outputs:
- grad_hidden: bfloat16 [768, 4096], P(('dp', 'vocab'))
- grad_head: bfloat16 [4096, 163840], P(None, ('dp', 'vocab'))
- mean_loss: float32 [], replicated
Inputs may be any that keep to these rules, and one draw needn't show every extreme that they name: `targets`: each token's target lies in its modality's columns: at least 131072 where image_mask is 1, below it where image_mask is 0. `lengths`: some window is full.
All inputs are finite; a program needn't handle non-finite values.
Results may differ from a plain program's by a relative error of at most 0.0067.
Values may be sent and summed in bfloat16 or wider, within the bound.
No kernel may reach another device: no remote copies, remote signals or barrier semaphores. Data moves between devices by JAX's collectives and lax.ppermute only.
A program may use at most 128 MiB of HBM per device.

v0:
```python
import functools

import jax
import jax.numpy as jnp
from jax import lax
from jax.experimental import pallas as pl
from jax.experimental.pallas import tpu as pltpu
from jax.sharding import Mesh, PartitionSpec as P

V = 163840
CODES = 32768
WIN = 48
NEG = -1e30
BETA = 1.0
LOSS_SCALE = 4096.0

D = 4096
HALF = D // 2
COLS = 640
TOKENS = 768
META = 128
WIDE = HALF + META
NY, NX, NZ, NC = 4, 4, 8, 2
AXES = ("y", "x", "z", "c")
OFF = (0, 1, 3, 2)
bf16 = jnp.bfloat16
f32 = jnp.float32
VMEM = pl.BlockSpec(memory_space=pltpu.VMEM)
SMEM = pl.BlockSpec(memory_space=pltpu.SMEM)
HBM = pl.BlockSpec(memory_space=pltpu.HBM)
MB = 1024 * 1024
PIECE = HALF // 2


def flat(y, x, z, c):
    return ((y % NY * NX + x % NX) * NZ + z % NZ) * NC + c


def fetch(value, source):
    pairs = [
        (flat(*source(y, x, z, c)), flat(y, x, z, c))
        for y in range(NY) for x in range(NX) for z in range(NZ) for c in range(NC)
    ]
    return lax.ppermute(value, AXES, pairs)


def middle(step):
    return lambda y, x, z, c: (y + step, x, z, c) if c == 0 else (y, x + step, z, c)


def final(step):
    return lambda y, x, z, c: (y, x + step, z, c) if c == 0 else (y + step, x, z, c)


def near(q):
    return lambda y, x, z, c: (y, x, z ^ (q >> 1), c ^ (q & 1))


def window(ids, core, s, k):
    y, x = ids[0], ids[1]
    across = core == 0
    last = (jnp.where(across, x, y) + OFF[s]) % 4
    mid = (jnp.where(across, y, x) + OFF[k]) % 4
    return jnp.where(across, mid * NX + last, last * NX + mid)


def call(kernel, outs, ins, scratch=(), vmem=10, **cost):
    return pl.pallas_call(
        kernel,
        out_shape=outs,
        in_specs=ins,
        out_specs=jax.tree.map(lambda _: VMEM, outs),
        scratch_shapes=list(scratch),
        compiler_params=pltpu.CompilerParams(vmem_limit_bytes=vmem * MB),
        cost_estimate=pl.CostEstimate(
            flops=cost.get("flops", 0), bytes_accessed=cost.get("bytes_accessed", 0), transcendentals=0
        ),
    )


def shape(dims, dtype):
    return jax.ShapeDtypeStruct(dims, dtype)


def join_window_kernel(ids, parts, out, tok, meta):
    for dev in range(16):
        tok[dev * 48:(dev + 1) * 48, :] = parts[dev, 0:48, :].astype(f32)
        meta[dev * 16:(dev + 1) * 16, :] = parts[dev, 48:64, :].astype(f32)
    for j in range(3):
        for r in range(16):
            out[j * 16:(j + 1) * 16, r * 128:(r + 1) * 128] = tok[pl.ds(j * 16 + r, 16, stride=48), :].astype(bf16)
        out[j * 16:(j + 1) * 16, HALF:WIDE] = meta[pl.ds(j, 16, stride=16), :].astype(bf16)


def join_window(ids, parts):
    return call(
        join_window_kernel,
        shape((WIN, WIDE), bf16),
        [SMEM, VMEM],
        [pltpu.VMEM((768, 128), f32), pltpu.VMEM((256, 128), f32)],
    )(ids, parts)


def join_blocks_kernel(a, b, c, d, out):
    for k, v in enumerate((a, b, c, d)):
        out[k] = v[...]


def join_blocks(*blocks):
    return call(join_blocks_kernel, shape((4, WIN, WIDE), bf16), [VMEM] * 4)(*blocks)


def gate_kernel(value, first, second, out):
    out[...] = value[...]


def gate(value, first, second):
    return pl.pallas_call(
        gate_kernel,
        out_shape=shape(value.shape, value.dtype),
        in_specs=[VMEM] * 3,
        out_specs=VMEM,
        compiler_params=pltpu.CompilerParams(vmem_limit_bytes=10 * MB),
    )(value, first, second)


def columns_of(rows):
    full = jnp.concatenate([rows, jnp.zeros((128 - rows.shape[0], 128), f32)], axis=0)
    return full.T


def load_kernel(head_hbm, head, mark, sem):
    mark[...] = jnp.zeros_like(mark)
    copy = pltpu.make_async_copy(head_hbm, head, sem)
    copy.start()
    copy.wait()


def load_head(head):
    return call(
        load_kernel,
        (shape((D, COLS), bf16), shape((8, 128), f32)),
        [HBM],
        [pltpu.SemaphoreType.DMA],
        vmem=8,
        bytes_accessed=10 * MB,
    )(head)


def logits_kernel(
    ids, a0, a1, a2, a3, b0, b1, b2, b3, head, hidden, logits, stats, target, meta, cols
):
    rows = 256
    core = ids[3]
    own = pl.multiple_of(core * HALF, HALF)
    oth = pl.multiple_of((1 - core) * HALF, HALF)
    for s, (a, b) in enumerate(((a0, b0), (a1, b1), (a2, b2), (a3, b3))):
        for k in range(4):
            row = pl.multiple_of(window(ids, core, s, k) * WIN, 16)
            hidden[pl.ds(row, WIN), pl.ds(own, HALF)] = a[k, :, 0:HALF]
            meta[pl.ds(row, WIN), :] = a[k, :, HALF:WIDE].astype(f32)
            row = pl.multiple_of(window(ids, 1 - core, s, k) * WIN, 16)
            hidden[pl.ds(row, WIN), pl.ds(oth, HALF)] = b[k, :, 0:HALF]
    first = ids[4] * COLS
    column = first + lax.broadcasted_iota(jnp.int32, (rows, COLS), 1)
    lane = lax.broadcasted_iota(jnp.int32, (rows, 128), 1)
    for i in range(TOKENS // rows):
        at = pl.ds(i * rows, rows)
        part = jnp.dot(hidden[at, :], head[...], preferred_element_type=f32)
        logits[at, :] = part
        digits = meta[at, :]
        goal = (digits[:, 0:1] + 256.0 * digits[:, 1:2] + 65536.0 * digits[:, 2:3]).astype(jnp.int32)
        in_range = (goal >= V - CODES) == (column >= V - CODES)
        masked = jnp.where(in_range, part, NEG)
        peak = jnp.max(masked, axis=1, keepdims=True)
        total = jnp.sum(jnp.where(in_range, jnp.exp(masked - peak), 0.0), axis=1, keepdims=True)
        hit = jnp.sum(jnp.where(column == goal, part, 0.0), axis=1, keepdims=True)
        cols[at, :] = jnp.where(
            lane == 0, peak, jnp.where(lane == 1, total, jnp.where(lane == 2, hit, goal.astype(f32)))
        )
    stats[...] = jnp.zeros_like(stats)
    target[...] = jnp.zeros_like(target)
    for b in range(TOKENS // 128):
        turned = cols[b * 128:(b + 1) * 128, :].T
        for i in range(3):
            stats[i, b:b + 1, :] = turned[i:i + 1, :]
        target[b:b + 1, :] = turned[3:4, :]


def local_logits(ids, own, other, head):
    return pl.pallas_call(
        logits_kernel,
        out_shape=(
            shape((TOKENS, D), bf16),
            shape((TOKENS, COLS), f32),
            shape((3, 8, 128), f32),
            shape((8, 128), f32),
        ),
        in_specs=[SMEM] + [VMEM] * 9,
        out_specs=(VMEM, VMEM, VMEM, VMEM),
        scratch_shapes=[
            pltpu.VMEM((TOKENS, 128), f32),
            pltpu.VMEM((TOKENS, 128), f32),
        ],
        compiler_params=pltpu.CompilerParams(vmem_limit_bytes=25 * MB),
        cost_estimate=pl.CostEstimate(flops=2 * TOKENS * D * COLS, bytes_accessed=20 * MB, transcendentals=0),
    )(ids, *own, *other, head)


def exchange(value, axes):
    return lax.all_to_all(jnp.broadcast_to(value[None], (16,) + value.shape), axes, 0, 0, tiled=True)


def merged(parts):
    peak = parts[0, 0]
    for i in range(1, 16):
        peak = jnp.maximum(peak, parts[i, 0])
    total = jnp.zeros_like(peak)
    hit = jnp.zeros_like(peak)
    for i in range(16):
        total += parts[i, 1] * jnp.exp(parts[i, 0] - peak)
        hit += parts[i, 2]
    return peak, total, hit


def merge_kernel(parts, out):
    for i in range(16):
        out[i, 0], out[i, 1], out[i, 2] = merged(parts)


def merge(parts):
    return call(merge_kernel, shape((16, 3, 8, 128), f32), [VMEM])(parts)


def preference_kernel(parts, lengths, ref_logps, pairing, norm, weight, loss):
    peak, total, hit = merged(parts)
    log_norm = peak + jnp.log(jnp.maximum(total, 1e-37))
    token_lp = hit - log_norm
    rows = lax.broadcasted_iota(jnp.int32, (8, 128), 0) * 128 + lax.broadcasted_iota(jnp.int32, (8, 128), 1)
    inner = rows % WIN
    group, position = rows // WIN, inner % 16 * 3 + inner // 16
    pairs = pairing.shape[0] // 2
    token_weight = jnp.zeros((8, 128), f32)
    losses = jnp.zeros((1, 1), f32)
    for k in range(pairs):
        sides = []
        for g in (pairing[2 * k], pairing[2 * k + 1]):
            count = lengths[g].astype(f32)
            live = (group == g) & (position < lengths[g])
            policy = jnp.sum(jnp.where(live, token_lp, 0.0), keepdims=True) / count
            sides.append((live, count, policy - ref_logps[g]))
        (live_c, count_c, chosen), (live_r, count_r, rejected) = sides
        margin = BETA * (chosen - rejected)
        losses += jnp.maximum(-margin, 0.0) + jnp.log1p(jnp.exp(-jnp.abs(margin)))
        pair_weight = -LOSS_SCALE * BETA * jax.nn.sigmoid(-margin) / pairs
        token_weight += jnp.where(live_c, pair_weight / count_c, 0.0)
        token_weight -= jnp.where(live_r, pair_weight / count_r, 0.0)
    norm[...] = log_norm
    weight[...] = token_weight
    loss[...] = jnp.broadcast_to(losses / pairs, (8, 128))


def preference(parts, lengths, ref_logps, pairing):
    return call(
        preference_kernel,
        [shape((8, 128), f32)] * 3,
        [VMEM, SMEM, SMEM, SMEM],
    )(parts, lengths, ref_logps, pairing)


BLOCK = 512
STEP = 256


def times_head(grad, rows):
    return lax.dot_general(grad, rows, (((1,), (1,)), ((), ())), preferred_element_type=f32)


def head_rows(half, start):
    return pl.ds(pl.multiple_of(half * HALF + start, STEP), STEP)


def other_piece(piece, ids, grad, head, out):
    for i in range(PIECE // STEP):
        rows = head[head_rows(1 - ids[3], piece * PIECE + i * STEP), :]
        out[:, i * STEP:(i + 1) * STEP] = times_head(grad[...], rows).astype(out.dtype)


def grad_other_first_kernel(ids, logits, norm, weight, target, head, grad, out):
    norm_c, weight_c, goal_c = columns_of(norm[...]), columns_of(weight[...]), columns_of(target[...])
    column = ids[4] * COLS + lax.broadcasted_iota(jnp.int32, (128, COLS), 1)
    for b in range(TOKENS // 128):
        goal = goal_c[:, b:b + 1].astype(jnp.int32)
        in_range = (goal >= V - CODES) == (column >= V - CODES)
        at = slice(b * 128, (b + 1) * 128)
        prob = jnp.exp(jnp.where(in_range, logits[at, :] - norm_c[:, b:b + 1], NEG))
        grad[at, :] = (weight_c[:, b:b + 1] * ((column == goal).astype(f32) - prob)).astype(bf16)
    other_piece(0, ids, grad, head, out)


def grad_other_first(ids, logits, norm, weight, target, head):
    return call(
        grad_other_first_kernel,
        (shape((TOKENS, COLS), bf16), shape((TOKENS, PIECE), bf16)),
        [SMEM] + [VMEM] * 5,
        vmem=16,
        flops=TOKENS * PIECE * COLS * 2,
        bytes_accessed=6 * MB,
    )(ids, logits, norm, weight, target, head)


def grad_other_second(ids, grad, head):
    return call(
        functools.partial(other_piece, 1),
        shape((TOKENS, PIECE), bf16),
        [SMEM, VMEM, VMEM],
        vmem=16,
        flops=TOKENS * PIECE * COLS * 4,
        bytes_accessed=16 * MB,
    )(ids, grad, head)


def arrived_kernel(value, mark):
    mark[...] = jnp.zeros_like(mark)


def arrived(value):
    return call(arrived_kernel, shape((8, 128), f32), [VMEM], vmem=4)(value)


def grad_own_kernel(ids, grad, head, other0, other1, after, r0, r1, r2, r3, mark, total):
    mark[...] = jnp.zeros_like(mark)
    for i in range(HALF // STEP):
        at = slice(i * STEP, (i + 1) * STEP)
        other = (other0, other1)[i * STEP // PIECE]
        inner = i * STEP % PIECE
        total[...] = times_head(grad[...], head[head_rows(ids[3], i * STEP), :])
        total[...] += other[:, inner:inner + STEP].astype(f32)
        for s, r in enumerate((r0, r1, r2, r3)):
            for k in range(4):
                row = pl.multiple_of(window(ids, ids[3], s, k) * WIN, 16)
                r[k, :, at] = total[pl.ds(row, WIN), :].astype(r.dtype)


def grad_own(ids, grad, head, other, after):
    return call(
        grad_own_kernel,
        [shape((4, WIN, HALF), f32 if s == 0 else bf16) for s in range(4)] + [shape((8, 128), f32)],
        [SMEM] + [VMEM] * 5,
        [pltpu.VMEM((TOKENS, STEP), f32)],
        vmem=22,
    )(ids, grad, head, *other, after)


def head_kernel(hidden, grad, after, out, mark):
    mark[...] = jnp.zeros_like(mark)
    out[...] = lax.dot_general(
        hidden[...], grad[...], (((0,), (0,)), ((), ())), preferred_element_type=f32
    ).astype(out.dtype)


def grad_head_of(hidden, grad, after):
    return pl.pallas_call(
        head_kernel,
        grid=(D // BLOCK,),
        in_specs=[
            pl.BlockSpec((TOKENS, BLOCK), lambda i: (0, i)),
            pl.BlockSpec((TOKENS, COLS), lambda i: (0, 0)),
            pl.BlockSpec((8, 128), lambda i: (0, 0)),
        ],
        out_specs=(pl.BlockSpec((BLOCK, COLS), lambda i: (i, 0)), pl.BlockSpec((8, 128), lambda i: (0, 0))),
        out_shape=(shape((D, COLS), bf16), shape((8, 128), f32)),
        compiler_params=pltpu.CompilerParams(vmem_limit_bytes=20 * MB),
        cost_estimate=pl.CostEstimate(flops=2 * TOKENS * D * COLS, bytes_accessed=12 * MB, transcendentals=0),
    )(hidden, grad, after)


def add_four(a, b, c, d):
    return (a.astype(f32) + d.astype(f32)) + (b.astype(f32) + c.astype(f32))


def split_middle_kernel(a, b, c, d, after, *outs):
    for k, q in enumerate(outs):
        q[...] = add_four(a[k], b[k], c[k], d[k]).astype(q.dtype)


def split_middle(a, b, c, d, after):
    return call(
        split_middle_kernel,
        [shape((WIN, HALF), f32 if k == 0 else bf16) for k in range(4)],
        [VMEM] * 5,
        bytes_accessed=6 * MB,
    )(a, b, c, d, after)


def split_window_kernel(a, b, c, d, out, tok):
    total = add_four(a[...], b[...], c[...], d[...])
    for j in range(3):
        for r in range(16):
            tok[pl.ds(j * 16 + r, 16, stride=48), :] = total[j * 16:(j + 1) * 16, r * 128:(r + 1) * 128]
    for dev in range(16):
        out[dev] = tok[dev * 48:(dev + 1) * 48, :].astype(out.dtype)


def split_window(a, b, c, d):
    return call(
        split_window_kernel,
        shape((16, 48, 128), bf16),
        [VMEM] * 4,
        [pltpu.VMEM((768, 128), f32)],
    )(a, b, c, d)


def finish_kernel(parts, out, tok):
    for half in range(2):
        total = parts[half].astype(f32)
        for i in range(1, NZ):
            total += parts[2 * i + half].astype(f32)
        tok[...] = total
        for r in range(16):
            at = half * HALF + r * 128
            out[:, at:at + 128] = tok[pl.ds(r, 3, stride=16), :]


def finish(parts):
    return call(finish_kernel, shape((3, D), f32), [VMEM], [pltpu.VMEM((48, 128), f32)])(parts)


def local(hidden, head_weight, targets, image_mask, lengths, ref_logps, pairing):
    y, x, z, c = (lax.axis_index(a) for a in AXES)
    ids = jnp.stack([y, x, z, c, flat(y, x, z, c)]).astype(jnp.int32)

    digits = jnp.stack([targets % 256, targets // 256 % 256, targets // 65536], axis=1)
    meta = jnp.pad(digits.astype(f32).astype(bf16), ((0, 13), (0, 125)))
    halves = hidden.reshape(3, 2, 16, 128)
    first, second = (jnp.concatenate([halves[:, i].reshape(48, 128), meta], axis=0) for i in range(2))
    parts = lax.all_to_all(
        jnp.broadcast_to(jnp.stack([first, second])[None], (NZ, 2, 64, 128)).reshape(16, 64, 128),
        ("z", "c"), 0, 0, tiled=True,
    )
    block = join_window(ids, parts)
    blocks = join_blocks(block, *(fetch(block, middle(o)) for o in OFF[1:]))
    other = [fetch(blocks, near(1))]
    head, mark = load_head(head_weight)
    blocks = gate(blocks, other[0], mark)
    own = [blocks] + [fetch(blocks, final(o)) for o in OFF[1:]]
    other = other + [fetch(v, near(1)) for v in own[1:]]

    rows, logits, stats, target = local_logits(ids, own, other, head)
    stats = merge(exchange(stats, ("z", "c")))
    stats = lax.all_to_all(stats, ("y", "x"), 0, 0, tiled=True)
    log_norm, weight, loss = preference(stats, lengths, ref_logps, pairing)

    logit_grad, send = grad_other_first(ids, logits, log_norm, weight, target, head)
    received = [fetch(send, near(1))]
    received.append(fetch(grad_other_second(ids, logit_grad, head), near(1)))
    *parts, mark = grad_own(ids, logit_grad, head, received, arrived(received[0]))
    grad_head, mark = grad_head_of(rows, logit_grad, mark)
    parts = split_middle(parts[0], *(fetch(parts[s], final(-OFF[s])) for s in (1, 2, 3)), mark)
    parts = split_window(parts[0], *(fetch(parts[s], middle(-OFF[s])) for s in (1, 2, 3)))
    grad_hidden = finish(lax.all_to_all(parts, ("z", "c"), 0, 0, tiled=True))
    return grad_hidden.astype(bf16), grad_head, loss[0, 0]


def solution(mesh):
    fine = Mesh(mesh.devices.reshape(NY, NX, NZ, NC), AXES)
    return jax.shard_map(
        local,
        mesh=fine,
        in_specs=(P(AXES, None), P(None, AXES), P(AXES), P(AXES), P(), P(), P()),
        out_specs=(P(AXES, None), P(None, AXES), P()),
        check_vma=False,
    )
```

profile of v0, /device:TPU:1, one launch (start us, length us, event | category | flops | bytes accessed | tf_op | source)
XLA Modules:
  0.0 161.6 jit_solution(13079927599476991827)
XLA Ops:
  3.0 10.0 %all-to-all-start = ((bf16[16,64,128]{2,1,0:T(8,128)(2,1)}), bf16[16,64,128]{2,1,0:T(8,128)(2,1)S(1)}, u32[]{:S(2)}, u32[]{:S(2)}) async-start(bf16[16,64,128]{2,1,0:T(8,128)(2,1)} %bitcast.12), calls=%async_computation | async-start | bytes 524288 | tf_op jit(solution)/shard_map/all_to_all | solution.py:437
  13.0 11.6 %all-to-all-done.parts = bf16[16,64,128]{2,1,0:T(8,128)(2,1)S(1)} async-done(((bf16[16,64,128]{2,1,0:T(8,128)(2,1)}), bf16[16,64,128]{2,1,0:T(8,128)(2,1)S(1)}, u32[]{:S(2)}, u32[]{:S(2)}) %all-to-all-start) | async-done | bytes 262176 | tf_op jit(solution)/shard_map/all_to_all | solution.py:437
  25.4 2.8 %collective-permute-start.2 = (bf16[48,2176]{1,0:T(8,128)(2,1)S(1)}, bf16[48,2176]{1,0:T(8,128)(2,1)S(1)}, u32[]{:S(2)}, u32[]{:S(2)}) collective-permute-start(bf16[48,2176]{1,0:T(8,128)(2,1)S(1)} %shard_map.85.a), channel_id=1, source_target_pairs={{128,0},{33,1},{130,2},{35,3},{132,4},{37,5},{134,6},{39,7},{136,8... | collective-permute-start | bytes 626696 | tf_op jit(solution)/shard_map/ppermute | solution.py:44
  28.5 2.4 %collective-permute-start = (bf16[48,2176]{1,0:T(8,128)(2,1)S(1)}, bf16[48,2176]{1,0:T(8,128)(2,1)S(1)}, u32[]{:S(2)}, u32[]{:S(2)}) collective-permute-start(bf16[48,2176]{1,0:T(8,128)(2,1)S(1)} %shard_map.85.a), channel_id=1, source_target_pairs={{64,0},{17,1},{66,2},{19,3},{68,4},{21,5},{70,6},{23,7},{72,8},{25... | collective-permute-start | bytes 626696 | tf_op jit(solution)/shard_map/ppermute | solution.py:44
  30.9 1.0 collective-permute-done.2.d
  31.9 2.5 %collective-permute-done.1.c = bf16[48,2176]{1,0:T(8,128)(2,1)S(1)} collective-permute-done((bf16[48,2176]{1,0:T(8,128)(2,1)S(1)}, bf16[48,2176]{1,0:T(8,128)(2,1)S(1)}, u32[]{:S(2)}, u32[]{:S(2)}) %collective-permute-start.1) | collective-permute-done | bytes 208928 | tf_op jit(solution)/shard_map/ppermute | solution.py:44
  34.4 1.0 collective-permute-start.3
  35.4 2.5 %copy-done = bf16[4096,640]{1,0:T(8,128)(2,1)S(1)} copy-done((bf16[4096,640]{1,0:T(8,128)(2,1)S(1)}, bf16[4096,640]{1,0:T(8,128)(2,1)}, u32[]{:S(2)}) %copy-start) | copy-done | bytes 5242904
  38.3 1.8 %collective-permute-start.6 = (bf16[4,48,2176]{2,1,0:T(8,128)(2,1)S(1)}, bf16[4,48,2176]{2,1,0:T(8,128)(2,1)S(1)}, u32[]{:S(2)}, u32[]{:S(2)}) collective-permute-start(bf16[4,48,2176]{2,1,0:T(8,128)(2,1)S(1)} %shard_map.88.a0), channel_id=1, source_target_pairs={{32,0},{129,1},{34,2},{131,3},{36,4},{133,5},{38,6},{135,7},{40,8}... | collective-permute-start | bytes 2506760 | tf_op jit(solution)/shard_map/ppermute | solution.py:44
  40.2 1.8 %collective-permute-start.5 = (bf16[4,48,2176]{2,1,0:T(8,128)(2,1)S(1)}, bf16[4,48,2176]{2,1,0:T(8,128)(2,1)S(1)}, u32[]{:S(2)}, u32[]{:S(2)}) collective-permute-start(bf16[4,48,2176]{2,1,0:T(8,128)(2,1)S(1)} %shard_map.88.a0), channel_id=1, source_target_pairs={{48,0},{193,1},{50,2},{195,3},{52,4},{197,5},{54,6},{199,7},{56,8}... | collective-permute-start | bytes 2506760 | tf_op jit(solution)/shard_map/ppermute | solution.py:44
  42.8 8.8 %collective-permute-done.6.a3 = bf16[4,48,2176]{2,1,0:T(8,128)(2,1)S(1)} collective-permute-done((bf16[4,48,2176]{2,1,0:T(8,128)(2,1)S(1)}, bf16[4,48,2176]{2,1,0:T(8,128)(2,1)S(1)}, u32[]{:S(2)}, u32[]{:S(2)}) %collective-permute-start.6) | collective-permute-done | bytes 835616 | tf_op jit(solution)/shard_map/ppermute | solution.py:44
  51.6 0.9 collective-permute-start.9
  52.6 8.0 %collective-permute-done.5.a2 = bf16[4,48,2176]{2,1,0:T(8,128)(2,1)S(1)} collective-permute-done((bf16[4,48,2176]{2,1,0:T(8,128)(2,1)S(1)}, bf16[4,48,2176]{2,1,0:T(8,128)(2,1)S(1)}, u32[]{:S(2)}, u32[]{:S(2)}) %collective-permute-start.5) | collective-permute-done | bytes 835616 | tf_op jit(solution)/shard_map/ppermute | solution.py:44
  61.5 1.8 %collective-permute-done.8.b2 = bf16[4,48,2176]{2,1,0:T(8,128)(2,1)S(1)} collective-permute-done((bf16[4,48,2176]{2,1,0:T(8,128)(2,1)S(1)}, bf16[4,48,2176]{2,1,0:T(8,128)(2,1)S(1)}, u32[]{:S(2)}, u32[]{:S(2)}) %collective-permute-start.8) | collective-permute-done | bytes 835616 | tf_op jit(solution)/shard_map/ppermute | solution.py:44
  63.4 1.2 collective-permute-done.7.b1
  64.6 7.1 %shard_map.89 = (bf16[768,4096]{1,0:T(8,128)(2,1)S(1)}, f32[768,640]{1,0:T(8,128)S(1)}, f32[3,8,128]{2,1,0:T(8,128)S(1)}, f32[8,128]{1,0:T(8,128)S(1)}) custom-call(s32[5]{0:T(128)S(1)} %stack.44.ids, bf16[4,48,2176]{2,1,0:T(8,128)(2,1)S(1)} %shard_map.88.a0, bf16[4,48,2176]{2,1,0:T(8,128)(2,1)S(1)} %collective-permute-done.4.a1, ...), custom_call_target="tpu_custom_call" | custom-call | flops 4026531840 | bytes 20971520 | tf_op jit(solution)/shard_map/pallas_call | solution.py:191
  71.7 13.8 %all_to_all.20.parts = f32[16,3,8,128]{3,2,1,0:T(8,128)S(1)} all-to-all(f32[16,3,8,128]{3,2,1,0:T(8,128)S(1)} %broadcast_in_dim.5), channel_id=1, replica_groups=mesh['y'=4,'x'=4,'z'=8,'c'=2] {'z','c'}, dimensions={0} | all-to-all | bytes 393216 | tf_op jit(solution)/shard_map/all_to_all | solution.py:211
  85.6 13.7 %all_to_all.21.parts = f32[16,3,8,128]{3,2,1,0:T(8,128)S(1)} all-to-all(f32[16,3,8,128]{3,2,1,0:T(8,128)S(1)} %shard_map.90), channel_id=1, replica_groups=mesh['y'=4,'x'=4,'z'=8,'c'=2] {'y','x'}, dimensions={0} | all-to-all | bytes 393216 | tf_op jit(solution)/shard_map/all_to_all | solution.py:451
  100.1 2.6 %shard_map.92 = (bf16[768,640]{1,0:T(8,128)(2,1)S(1)}, bf16[768,1024]{1,0:T(8,128)(2,1)S(1)}) custom-call(s32[5]{0:T(128)S(1)} %stack.44.ids, f32[768,640]{1,0:T(8,128)S(1)} %get-tuple-element.27.logits, f32[8,128]{1,0:T(8,128)S(1)} %get-tuple-element.29.norm, f32[8,128]{1,0:T(8,128)S(1)} %get-tuple-element.30.weight, ...), custom_call_target="tpu_custom_call" | custom-call | flops 1006632960 | bytes 6291456 | tf_op jit(solution)/shard_map/pallas_call | solution.py:302
  102.8 1.0 collective-permute-start.10
  103.8 2.0 %shard_map.93 = bf16[768,1024]{1,0:T(8,128)(2,1)S(1)} custom-call(s32[5]{0:T(128)S(1)} %stack.44.ids, bf16[768,640]{1,0:T(8,128)(2,1)S(1)} %get-tuple-element.32.grad, bf16[4096,640]{1,0:T(8,128)(2,1)S(1)} %get-tuple-element.26.head), custom_call_target="tpu_custom_call" | custom-call | flops 2013265920 | bytes 16777216 | tf_op jit(solution)/shard_map/pallas_call | solution.py:313
  106.8 2.6 %collective-permute-done.11.other1 = bf16[768,1024]{1,0:T(8,128)(2,1)S(1)} collective-permute-done((bf16[768,1024]{1,0:T(8,128)(2,1)S(1)}, bf16[768,1024]{1,0:T(8,128)(2,1)S(1)}, u32[]{:S(2)}, u32[]{:S(2)}) %collective-permute-start.11) | collective-permute-done | bytes 1572896 | tf_op jit(solution)/shard_map/ppermute | solution.py:44
  109.5 4.1 %shard_map.95 = (f32[4,48,2048]{2,1,0:T(8,128)S(1)}, bf16[4,48,2048]{2,1,0:T(8,128)(2,1)S(1)}, bf16[4,48,2048]{2,1,0:T(8,128)(2,1)S(1)}, bf16[4,48,2048]{2,1,0:T(8,128)(2,1)S(1)}, f32[8,128]{1,0:T(8,128)S(1)}) custom-call(s32[5]{0:T(128)S(1)} %stack.44.ids, bf16[768,640]{1,0:T(8,128)(2,1)S(1)} %get-tuple-element.32.grad, ...), custom_call_target="tpu_custom_call" | custom-call | tf_op jit(solution)/shard_map/pallas_call | solution.py:346
  113.6 2.7 %collective-permute-start.13 = (bf16[4,48,2048]{2,1,0:T(8,128)(2,1)S(1)}, bf16[4,48,2048]{2,1,0:T(8,128)(2,1)S(1)}, u32[]{:S(2)}, u32[]{:S(2)}) collective-permute-start(bf16[4,48,2048]{2,1,0:T(8,128)(2,1)S(1)} %get-tuple-element.36), channel_id=1, source_target_pairs={{16,0},{65,1},{18,2},{67,3},{20,4},{69,5},{22,6},{71,7},{24,8},{73... | collective-permute-start | bytes 2359304 | tf_op jit(solution)/shard_map/ppermute | solution.py:44
  116.3 8.0 %shard_map.96 = (bf16[4096,640]{1,0:T(8,128)(2,1)}, f32[8,128]{1,0:T(8,128)S(1)}) custom-call(bf16[768,4096]{1,0:T(8,128)(2,1)S(1)} %get-tuple-element.38.hidden, bf16[768,640]{1,0:T(8,128)(2,1)S(1)} %get-tuple-element.32.grad, f32[8,128]{1,0:T(8,128)S(1)} %get-tuple-element.39.after), custom_call_target="tpu_custom_call" | custom-call | flops 4026531840 | bytes 12582912 | tf_op jit(solution)/shard_map/pallas_call | solution.py:363
  124.3 10.1 %collective-permute-done.12.b = bf16[4,48,2048]{2,1,0:T(8,128)(2,1)S(1)} collective-permute-done((bf16[4,48,2048]{2,1,0:T(8,128)(2,1)S(1)}, bf16[4,48,2048]{2,1,0:T(8,128)(2,1)S(1)}, u32[]{:S(2)}, u32[]{:S(2)}) %collective-permute-start.12) | collective-permute-done | bytes 786464 | tf_op jit(solution)/shard_map/ppermute | solution.py:44
  135.0 2.5 %collective-permute-start.16 = (bf16[48,2048]{1,0:T(8,128)(2,1)S(1)}, bf16[48,2048]{1,0:T(8,128)(2,1)S(1)}, u32[]{:S(2)}, u32[]{:S(2)}) collective-permute-start(bf16[48,2048]{1,0:T(8,128)(2,1)S(1)} %get-tuple-element.43), channel_id=1, source_target_pairs={{64,0},{17,1},{66,2},{19,3},{68,4},{21,5},{70,6},{23,7},{72,8},{25... | collective-permute-start | bytes 589832 | tf_op jit(solution)/shard_map/ppermute | solution.py:44
  137.6 3.3 %collective-permute-done.15.b = bf16[48,2048]{1,0:T(8,128)(2,1)S(1)} collective-permute-done((bf16[48,2048]{1,0:T(8,128)(2,1)S(1)}, bf16[48,2048]{1,0:T(8,128)(2,1)S(1)}, u32[]{:S(2)}, u32[]{:S(2)}) %collective-permute-start.15) | collective-permute-done | bytes 196640 | tf_op jit(solution)/shard_map/ppermute | solution.py:44
  140.9 1.4 collective-permute-done.16.c
  142.3 1.6 collective-permute-done.17.d
  144.8 5.7 %all-to-all-start.3 = ((bf16[16,48,128]{2,1,0:T(8,128)(2,1)}), bf16[16,48,128]{2,1,0:T(8,128)(2,1)S(1)}, u32[]{:S(2)}, u32[]{:S(2)}) async-start(bf16[16,48,128]{2,1,0:T(8,128)(2,1)} %shard_map.98), calls=%async_computation.3 | async-start | bytes 393216 | tf_op jit(solution)/shard_map/all_to_all | solution.py:461
  151.0 9.9 %all-to-all-done.3.parts = bf16[16,48,128]{2,1,0:T(8,128)(2,1)S(1)} async-done(((bf16[16,48,128]{2,1,0:T(8,128)(2,1)}), bf16[16,48,128]{2,1,0:T(8,128)(2,1)S(1)}, u32[]{:S(2)}, u32[]{:S(2)}) %all-to-all-start.3) | async-done | bytes 196640 | tf_op jit(solution)/shard_map/all_to_all | solution.py:461
  (45 shorter events, 10.6 us)
Async XLA Ops:
  3.0 21.7 %all-to-all-start = ((bf16[16,64,128]{2,1,0:T(8,128)(2,1)}), bf16[16,64,128]{2,1,0:T(8,128)(2,1)S(1)}, u32[]{:S(2)}, u32[]{:S(2)}) async-start(bf16[16,64,128]{2,1,0:T(8,128)(2,1)} %bitcast.12), calls=%async_computation | async-start | bytes 524288 | tf_op jit(solution)/shard_map/all_to_all | solution.py:437
  25.4 6.5 %collective-permute-start.2 = (bf16[48,2176]{1,0:T(8,128)(2,1)S(1)}, bf16[48,2176]{1,0:T(8,128)(2,1)S(1)}, u32[]{:S(2)}, u32[]{:S(2)}) collective-permute-start(bf16[48,2176]{1,0:T(8,128)(2,1)S(1)} %shard_map.85.a), channel_id=1, source_target_pairs={{128,0},{33,1},{130,2},{35,3},{132,4},{37,5},{134,6},{39,7},{136,8... | collective-permute-start | bytes 626696 | tf_op jit(solution)/shard_map/ppermute | solution.py:44
  28.2 6.2 %collective-permute-start.1 = (bf16[48,2176]{1,0:T(8,128)(2,1)S(1)}, bf16[48,2176]{1,0:T(8,128)(2,1)S(1)}, u32[]{:S(2)}, u32[]{:S(2)}) collective-permute-start(bf16[48,2176]{1,0:T(8,128)(2,1)S(1)} %shard_map.85.a), channel_id=1, source_target_pairs={{192,0},{49,1},{194,2},{51,3},{196,4},{53,5},{198,6},{55,7},{200,8... | collective-permute-start | bytes 626696 | tf_op jit(solution)/shard_map/ppermute | solution.py:44
  28.5 5.8 %collective-permute-start = (bf16[48,2176]{1,0:T(8,128)(2,1)S(1)}, bf16[48,2176]{1,0:T(8,128)(2,1)S(1)}, u32[]{:S(2)}, u32[]{:S(2)}) collective-permute-start(bf16[48,2176]{1,0:T(8,128)(2,1)S(1)} %shard_map.85.a), channel_id=1, source_target_pairs={{64,0},{17,1},{66,2},{19,3},{68,4},{21,5},{70,6},{23,7},{72,8},{25... | collective-permute-start | bytes 626696 | tf_op jit(solution)/shard_map/ppermute | solution.py:44
  34.4 3.8 %collective-permute-start.3 = (bf16[4,48,2176]{2,1,0:T(8,128)(2,1)S(1)}, bf16[4,48,2176]{2,1,0:T(8,128)(2,1)S(1)}, u32[]{:S(2)}, u32[]{:S(2)}) collective-permute-start(bf16[4,48,2176]{2,1,0:T(8,128)(2,1)S(1)} %shard_map.86.value), channel_id=1, source_target_pairs={{1,0},{0,1},{3,2},{2,3},{5,4},{4,5},{7,6},{6,7},{9,8},{8,9},{11,10... | collective-permute-start | bytes 2506760 | tf_op jit(solution)/shard_map/ppermute | solution.py:44
  35.4 2.5 %copy-start = (bf16[4096,640]{1,0:T(8,128)(2,1)S(1)}, bf16[4096,640]{1,0:T(8,128)(2,1)}, u32[]{:S(2)}) copy-start(bf16[4096,640]{1,0:T(8,128)(2,1)} %head_hbm.1) | copy-start | bytes 15728644
  38.3 13.3 %collective-permute-start.6 = (bf16[4,48,2176]{2,1,0:T(8,128)(2,1)S(1)}, bf16[4,48,2176]{2,1,0:T(8,128)(2,1)S(1)}, u32[]{:S(2)}, u32[]{:S(2)}) collective-permute-start(bf16[4,48,2176]{2,1,0:T(8,128)(2,1)S(1)} %shard_map.88.a0), channel_id=1, source_target_pairs={{32,0},{129,1},{34,2},{131,3},{36,4},{133,5},{38,6},{135,7},{40,8}... | collective-permute-start | bytes 2506760 | tf_op jit(solution)/shard_map/ppermute | solution.py:44
  40.2 20.4 %collective-permute-start.5 = (bf16[4,48,2176]{2,1,0:T(8,128)(2,1)S(1)}, bf16[4,48,2176]{2,1,0:T(8,128)(2,1)S(1)}, u32[]{:S(2)}, u32[]{:S(2)}) collective-permute-start(bf16[4,48,2176]{2,1,0:T(8,128)(2,1)S(1)} %shard_map.88.a0), channel_id=1, source_target_pairs={{48,0},{193,1},{50,2},{195,3},{52,4},{197,5},{54,6},{199,7},{56,8}... | collective-permute-start | bytes 2506760 | tf_op jit(solution)/shard_map/ppermute | solution.py:44
  41.9 19.5 %collective-permute-start.4 = (bf16[4,48,2176]{2,1,0:T(8,128)(2,1)S(1)}, bf16[4,48,2176]{2,1,0:T(8,128)(2,1)S(1)}, u32[]{:S(2)}, u32[]{:S(2)}) collective-permute-start(bf16[4,48,2176]{2,1,0:T(8,128)(2,1)S(1)} %shard_map.88.a0), channel_id=1, source_target_pairs={{16,0},{65,1},{18,2},{67,3},{20,4},{69,5},{22,6},{71,7},{24,8},{73... | collective-permute-start | bytes 2506760 | tf_op jit(solution)/shard_map/ppermute | solution.py:44
  51.6 9.9 %collective-permute-start.9 = (bf16[4,48,2176]{2,1,0:T(8,128)(2,1)S(1)}, bf16[4,48,2176]{2,1,0:T(8,128)(2,1)S(1)}, u32[]{:S(2)}, u32[]{:S(2)}) collective-permute-start(bf16[4,48,2176]{2,1,0:T(8,128)(2,1)S(1)} %collective-permute-done.6.a3), channel_id=1, source_target_pairs={{1,0},{0,1},{3,2},{2,3},{5,4},{4,5},{7,6},{6,7},{9,8},{8,9},{11,10... | collective-permute-start | bytes 2506760 | tf_op jit(solution)/shard_map/ppermute | solution.py:44
  60.5 2.9 %collective-permute-start.8 = (bf16[4,48,2176]{2,1,0:T(8,128)(2,1)S(1)}, bf16[4,48,2176]{2,1,0:T(8,128)(2,1)S(1)}, u32[]{:S(2)}, u32[]{:S(2)}) collective-permute-start(bf16[4,48,2176]{2,1,0:T(8,128)(2,1)S(1)} %collective-permute-done.5.a2), channel_id=1, source_target_pairs={{1,0},{0,1},{3,2},{2,3},{5,4},{4,5},{7,6},{6,7},{9,8},{8,9},{11,10... | collective-permute-start | bytes 2506760 | tf_op jit(solution)/shard_map/ppermute | solution.py:44
  61.4 3.2 %collective-permute-start.7 = (bf16[4,48,2176]{2,1,0:T(8,128)(2,1)S(1)}, bf16[4,48,2176]{2,1,0:T(8,128)(2,1)S(1)}, u32[]{:S(2)}, u32[]{:S(2)}) collective-permute-start(bf16[4,48,2176]{2,1,0:T(8,128)(2,1)S(1)} %collective-permute-done.4.a1), channel_id=1, source_target_pairs={{1,0},{0,1},{3,2},{2,3},{5,4},{4,5},{7,6},{6,7},{9,8},{8,9},{11,10... | collective-permute-start | bytes 2506760 | tf_op jit(solution)/shard_map/ppermute | solution.py:44
  64.6 34.8 %copy-start.1 = (s32[16]{0:T(128)S(1)}, s32[16]{0:T(128)}, u32[]{:S(2)}) copy-start(s32[16]{0:T(128)} %lengths.1) | copy-start | bytes 196
  64.6 34.8 %copy-start.2 = (f32[16]{0:T(128)S(1)}, f32[16]{0:T(128)}, u32[]{:S(2)}) copy-start(f32[16]{0:T(128)} %ref_logps.1) | copy-start | bytes 196
  64.6 34.8 %copy-start.3 = (s32[16]{0:T(128)S(1)}, s32[16]{0:T(128)}, u32[]{:S(2)}) copy-start(s32[16]{0:T(128)} %pairing.1) | copy-start | bytes 196
  102.8 4.0 %collective-permute-start.10 = (bf16[768,1024]{1,0:T(8,128)(2,1)S(1)}, bf16[768,1024]{1,0:T(8,128)(2,1)S(1)}, u32[]{:S(2)}, u32[]{:S(2)}) collective-permute-start(bf16[768,1024]{1,0:T(8,128)(2,1)S(1)} %get-tuple-element.33), channel_id=1, source_target_pairs={{1,0},{0,1},{3,2},{2,3},{5,4},{4,5},{7,6},{6,7},{9,8},{8,9},{11,10... | collective-permute-start | bytes 4718600 | tf_op jit(solution)/shard_map/ppermute | solution.py:44
  105.7 3.7 %collective-permute-start.11 = (bf16[768,1024]{1,0:T(8,128)(2,1)S(1)}, bf16[768,1024]{1,0:T(8,128)(2,1)S(1)}, u32[]{:S(2)}, u32[]{:S(2)}) collective-permute-start(bf16[768,1024]{1,0:T(8,128)(2,1)S(1)} %shard_map.93), channel_id=1, source_target_pairs={{1,0},{0,1},{3,2},{2,3},{5,4},{4,5},{7,6},{6,7},{9,8},{8,9},{11,10... | collective-permute-start | bytes 4718600 | tf_op jit(solution)/shard_map/ppermute | solution.py:44
  113.5 20.8 %collective-permute-start.12 = (bf16[4,48,2048]{2,1,0:T(8,128)(2,1)S(1)}, bf16[4,48,2048]{2,1,0:T(8,128)(2,1)S(1)}, u32[]{:S(2)}, u32[]{:S(2)}) collective-permute-start(bf16[4,48,2048]{2,1,0:T(8,128)(2,1)S(1)} %get-tuple-element.35), channel_id=1, source_target_pairs={{48,0},{193,1},{50,2},{195,3},{52,4},{197,5},{54,6},{199,7},{56,8}... | collective-permute-start | bytes 2359304 | tf_op jit(solution)/shard_map/ppermute | solution.py:44
  113.6 20.8 %collective-permute-start.13 = (bf16[4,48,2048]{2,1,0:T(8,128)(2,1)S(1)}, bf16[4,48,2048]{2,1,0:T(8,128)(2,1)S(1)}, u32[]{:S(2)}, u32[]{:S(2)}) collective-permute-start(bf16[4,48,2048]{2,1,0:T(8,128)(2,1)S(1)} %get-tuple-element.36), channel_id=1, source_target_pairs={{16,0},{65,1},{18,2},{67,3},{20,4},{69,5},{22,6},{71,7},{24,8},{73... | collective-permute-start | bytes 2359304 | tf_op jit(solution)/shard_map/ppermute | solution.py:44
  116.3 18.1 %collective-permute-start.14 = (bf16[4,48,2048]{2,1,0:T(8,128)(2,1)S(1)}, bf16[4,48,2048]{2,1,0:T(8,128)(2,1)S(1)}, u32[]{:S(2)}, u32[]{:S(2)}) collective-permute-start(bf16[4,48,2048]{2,1,0:T(8,128)(2,1)S(1)} %get-tuple-element.37), channel_id=1, source_target_pairs={{32,0},{129,1},{34,2},{131,3},{36,4},{133,5},{38,6},{135,7},{40,8}... | collective-permute-start | bytes 2359304 | tf_op jit(solution)/shard_map/ppermute | solution.py:44
  134.8 6.1 %collective-permute-start.15 = (bf16[48,2048]{1,0:T(8,128)(2,1)S(1)}, bf16[48,2048]{1,0:T(8,128)(2,1)S(1)}, u32[]{:S(2)}, u32[]{:S(2)}) collective-permute-start(bf16[48,2048]{1,0:T(8,128)(2,1)S(1)} %get-tuple-element.42), channel_id=1, source_target_pairs={{192,0},{49,1},{194,2},{51,3},{196,4},{53,5},{198,6},{55,7},{200,8... | collective-permute-start | bytes 589832 | tf_op jit(solution)/shard_map/ppermute | solution.py:44
  135.0 7.3 %collective-permute-start.16 = (bf16[48,2048]{1,0:T(8,128)(2,1)S(1)}, bf16[48,2048]{1,0:T(8,128)(2,1)S(1)}, u32[]{:S(2)}, u32[]{:S(2)}) collective-permute-start(bf16[48,2048]{1,0:T(8,128)(2,1)S(1)} %get-tuple-element.43), channel_id=1, source_target_pairs={{64,0},{17,1},{66,2},{19,3},{68,4},{21,5},{70,6},{23,7},{72,8},{25... | collective-permute-start | bytes 589832 | tf_op jit(solution)/shard_map/ppermute | solution.py:44
  137.6 6.3 %collective-permute-start.17 = (bf16[48,2048]{1,0:T(8,128)(2,1)S(1)}, bf16[48,2048]{1,0:T(8,128)(2,1)S(1)}, u32[]{:S(2)}, u32[]{:S(2)}) collective-permute-start(bf16[48,2048]{1,0:T(8,128)(2,1)S(1)} %get-tuple-element.44), channel_id=1, source_target_pairs={{128,0},{33,1},{130,2},{35,3},{132,4},{37,5},{134,6},{39,7},{136,8... | collective-permute-start | bytes 589832 | tf_op jit(solution)/shard_map/ppermute | solution.py:44
  144.8 16.1 %all-to-all-start.3 = ((bf16[16,48,128]{2,1,0:T(8,128)(2,1)}), bf16[16,48,128]{2,1,0:T(8,128)(2,1)S(1)}, u32[]{:S(2)}, u32[]{:S(2)}) async-start(bf16[16,48,128]{2,1,0:T(8,128)(2,1)} %shard_map.98), calls=%async_computation.3 | async-start | bytes 393216 | tf_op jit(solution)/shard_map/all_to_all | solution.py:461
where the time goes:
time: 162 us
  waiting for transfers between devices  64.6 us (40%)
  starting transfers between devices  35.5 us (22%)
  blocking collectives  27.6 us (17%)
  Pallas kernels  27.1 us (17%)
  local copies, waits for them, and re-layouts  4.75 us (3%)
    ppermute x18, waiting for transfers between devices, fetch(): return lax.ppermute(value, AXES, pairs)  43.1 us
    ppermute x18, starting transfers between devices, fetch(): return lax.ppermute(value, AXES, pairs)  19.8 us
    all_to_all x1, blocking collectives, exchange(): lax.all_to_all(jnp.broadcast_to(value[None], (16,) + value.shape), axes,...  13.8 us
    all_to_all x1, blocking collectives, local(): stats = lax.all_to_all(stats, ('y', 'x'), 0, 0, tiled=True)  13.7 us
    all_to_all x1, waiting for transfers between devices, local(): lax.all_to_all(jnp.broadcast_to(jnp.stack([first, second])[None], (NZ, 2,...  11.6 us
    all_to_all x1, starting transfers between devices, local(): lax.all_to_all(jnp.broadcast_to(jnp.stack([first, second])[None], (NZ, 2,...  9.98 us
    all_to_all x1, waiting for transfers between devices, local(): grad_hidden = finish(lax.all_to_all(parts, ('z', 'c'), 0, 0, tiled=True))  9.87 us
    pallas_call x1, Pallas kernels, grad_head_of(): pl.pallas_call(head_kernel, grid=(D // BLOCK,), in_specs=[pl.BlockSpec((T...  8.02 us
  transfers between devices with their start and end apart: 20, of which 14 were waited for; matrix products, arithmetic and copies ran while one was open for 0% of the time, Pallas kernels for 6%

commit v1 on v0

--- a/solution.py
+++ b/solution.py
@@ -52,8 +52,8 @@
     return lambda y, x, z, c: (y, x + step, z, c) if c == 0 else (y + step, x, z, c)
 
 
-def near(q):
-    return lambda y, x, z, c: (y, x, z ^ (q >> 1), c ^ (q & 1))
+def near(y, x, z, c):
+    return y, x, z, 1 - c
 
 
 def window(ids, core, s, k):
@@ -101,27 +101,21 @@
     )(ids, parts)
 
 
-def join_blocks_kernel(a, b, c, d, out):
-    for k, v in enumerate((a, b, c, d)):
-        out[k] = v[...]
+def join_blocks_kernel(a, b, c, d, low, high):
+    low[0], low[1], high[0], high[1] = a[...], b[...], c[...], d[...]
 
 
 def join_blocks(*blocks):
-    return call(join_blocks_kernel, shape((4, WIN, WIDE), bf16), [VMEM] * 4)(*blocks)
-
-
-def gate_kernel(value, first, second, out):
-    out[...] = value[...]
-
-
-def gate(value, first, second):
-    return pl.pallas_call(
-        gate_kernel,
-        out_shape=shape(value.shape, value.dtype),
-        in_specs=[VMEM] * 3,
-        out_specs=VMEM,
-        compiler_params=pltpu.CompilerParams(vmem_limit_bytes=10 * MB),
-    )(value, first, second)
+    return call(join_blocks_kernel, [shape((2, WIN, WIDE), bf16)] * 2, [VMEM] * 4)(*blocks)
+
+
+def gate_kernel(low, high, first, second, third, out_low, out_high):
+    out_low[...] = low[...]
+    out_high[...] = high[...]
+
+
+def gate(low, high, *marks):
+    return call(gate_kernel, [shape(low.shape, low.dtype)] * 2, [VMEM] * 5)(low, high, *marks)
 
 
 def columns_of(rows):
@@ -148,19 +142,22 @@
 
 
 def logits_kernel(
-    ids, a0, a1, a2, a3, b0, b1, b2, b3, head, hidden, logits, stats, target, meta, cols
+    ids, *refs
 ):
+    own_blocks, other_blocks = refs[:8], refs[8:16]
+    head, hidden, logits, stats, target, meta, cols = refs[16:]
     rows = 256
     core = ids[3]
     own = pl.multiple_of(core * HALF, HALF)
     oth = pl.multiple_of((1 - core) * HALF, HALF)
-    for s, (a, b) in enumerate(((a0, b0), (a1, b1), (a2, b2), (a3, b3))):
-        for k in range(4):
+    for i, (a, b) in enumerate(zip(own_blocks, other_blocks)):
+        for inner in range(2):
+            s, k = i // 2, i % 2 * 2 + inner
             row = pl.multiple_of(window(ids, core, s, k) * WIN, 16)
-            hidden[pl.ds(row, WIN), pl.ds(own, HALF)] = a[k, :, 0:HALF]
-            meta[pl.ds(row, WIN), :] = a[k, :, HALF:WIDE].astype(f32)
+            hidden[pl.ds(row, WIN), pl.ds(own, HALF)] = a[inner, :, 0:HALF]
+            meta[pl.ds(row, WIN), :] = a[inner, :, HALF:WIDE].astype(f32)
             row = pl.multiple_of(window(ids, 1 - core, s, k) * WIN, 16)
-            hidden[pl.ds(row, WIN), pl.ds(oth, HALF)] = b[k, :, 0:HALF]
+            hidden[pl.ds(row, WIN), pl.ds(oth, HALF)] = b[inner, :, 0:HALF]
     first = ids[4] * COLS
     column = first + lax.broadcasted_iota(jnp.int32, (rows, COLS), 1)
     lane = lax.broadcasted_iota(jnp.int32, (rows, 128), 1)
@@ -175,16 +172,15 @@
         peak = jnp.max(masked, axis=1, keepdims=True)
         total = jnp.sum(jnp.where(in_range, jnp.exp(masked - peak), 0.0), axis=1, keepdims=True)
         hit = jnp.sum(jnp.where(column == goal, part, 0.0), axis=1, keepdims=True)
-        cols[at, :] = jnp.where(
-            lane == 0, peak, jnp.where(lane == 1, total, jnp.where(lane == 2, hit, goal.astype(f32)))
-        )
+        norm = peak + jnp.log(jnp.maximum(total, 1e-37))
+        cols[at, :] = jnp.where(lane == 0, norm, jnp.where(lane == 1, hit, goal.astype(f32)))
     stats[...] = jnp.zeros_like(stats)
     target[...] = jnp.zeros_like(target)
     for b in range(TOKENS // 128):
         turned = cols[b * 128:(b + 1) * 128, :].T
-        for i in range(3):
+        for i in range(2):
             stats[i, b:b + 1, :] = turned[i:i + 1, :]
-        target[b:b + 1, :] = turned[3:4, :]
+        target[b:b + 1, :] = turned[2:3, :]
 
 
 def local_logits(ids, own, other, head):
@@ -193,10 +189,10 @@
         out_shape=(
             shape((TOKENS, D), bf16),
             shape((TOKENS, COLS), f32),
-            shape((3, 8, 128), f32),
+            shape((2, 8, 128), f32),
             shape((8, 128), f32),
         ),
-        in_specs=[SMEM] + [VMEM] * 9,
+        in_specs=[SMEM] + [VMEM] * 17,
         out_specs=(VMEM, VMEM, VMEM, VMEM),
         scratch_shapes=[
             pltpu.VMEM((TOKENS, 128), f32),
@@ -218,23 +214,23 @@
     total = jnp.zeros_like(peak)
     hit = jnp.zeros_like(peak)
     for i in range(16):
-        total += parts[i, 1] * jnp.exp(parts[i, 0] - peak)
-        hit += parts[i, 2]
-    return peak, total, hit
+        total += jnp.exp(parts[i, 0] - peak)
+        hit += parts[i, 1]
+    return peak + jnp.log(total), hit
 
 
 def merge_kernel(parts, out):
+    norm, hit = merged(parts)
     for i in range(16):
-        out[i, 0], out[i, 1], out[i, 2] = merged(parts)
+        out[i, 0], out[i, 1] = norm, hit
 
 
 def merge(parts):
-    return call(merge_kernel, shape((16, 3, 8, 128), f32), [VMEM])(parts)
+    return call(merge_kernel, shape((16, 2, 8, 128), f32), [VMEM])(parts)
 
 
 def preference_kernel(parts, lengths, ref_logps, pairing, norm, weight, loss):
-    peak, total, hit = merged(parts)
-    log_norm = peak + jnp.log(jnp.maximum(total, 1e-37))
+    log_norm, hit = merged(parts)
     token_lp = hit - log_norm
     rows = lax.broadcasted_iota(jnp.int32, (8, 128), 0) * 128 + lax.broadcasted_iota(jnp.int32, (8, 128), 1)
     inner = rows % WIN
@@ -328,7 +324,8 @@
     return call(arrived_kernel, shape((8, 128), f32), [VMEM], vmem=4)(value)
 
 
-def grad_own_kernel(ids, grad, head, other0, other1, after, r0, r1, r2, r3, mark, total):
+def grad_own_kernel(ids, grad, head, other0, other1, after, *refs):
+    parts, mark, total = refs[:8], refs[8], refs[9]
     mark[...] = jnp.zeros_like(mark)
     for i in range(HALF // STEP):
         at = slice(i * STEP, (i + 1) * STEP)
@@ -336,16 +333,19 @@
         inner = i * STEP % PIECE
         total[...] = times_head(grad[...], head[head_rows(ids[3], i * STEP), :])
         total[...] += other[:, inner:inner + STEP].astype(f32)
-        for s, r in enumerate((r0, r1, r2, r3)):
-            for k in range(4):
-                row = pl.multiple_of(window(ids, ids[3], s, k) * WIN, 16)
-                r[k, :, at] = total[pl.ds(row, WIN), :].astype(r.dtype)
+        for n, r in enumerate(parts):
+            for inner in range(2):
+                row = pl.multiple_of(window(ids, ids[3], n // 2, n % 2 * 2 + inner) * WIN, 16)
+                r[inner, :, at] = total[pl.ds(row, WIN), :].astype(r.dtype)
+
+
+PART_TYPES = (f32, f32, f32, bf16, bf16, f32, bf16, bf16)
 
 
 def grad_own(ids, grad, head, other, after):
     return call(
         grad_own_kernel,
-        [shape((4, WIN, HALF), f32 if s == 0 else bf16) for s in range(4)] + [shape((8, 128), f32)],
+        [shape((2, WIN, HALF), t) for t in PART_TYPES] + [shape((8, 128), f32)],
         [SMEM] + [VMEM] * 5,
         [pltpu.VMEM((TOKENS, STEP), f32)],
         vmem=22,
@@ -379,18 +379,28 @@
     return (a.astype(f32) + d.astype(f32)) + (b.astype(f32) + c.astype(f32))
 
 
-def split_middle_kernel(a, b, c, d, after, *outs):
+def add_kernel(a, b, out):
+    out[...] = (a[...] + b[...].astype(f32)).astype(out.dtype)
+
+
+def add(a, b):
+    return call(add_kernel, shape(a.shape, bf16), [VMEM] * 2)(a, b)
+
+
+def split_middle_kernel(*refs):
+    ins, outs = refs[:6], refs[7:]
     for k, q in enumerate(outs):
-        q[...] = add_four(a[k], b[k], c[k], d[k]).astype(q.dtype)
-
-
-def split_middle(a, b, c, d, after):
+        own, back, ahead = (ins[3 * (k // 2) + i][k % 2].astype(f32) for i in range(3))
+        q[...] = (own + (back + ahead)).astype(q.dtype)
+
+
+def split_middle(low, high, after):
     return call(
         split_middle_kernel,
         [shape((WIN, HALF), f32 if k == 0 else bf16) for k in range(4)],
-        [VMEM] * 5,
+        [VMEM] * 7,
         bytes_accessed=6 * MB,
-    )(a, b, c, d, after)
+    )(*low, *high, after)
 
 
 def split_window_kernel(a, b, c, d, out, tok):
@@ -439,12 +449,15 @@
         ("z", "c"), 0, 0, tiled=True,
     )
     block = join_window(ids, parts)
-    blocks = join_blocks(block, *(fetch(block, middle(o)) for o in OFF[1:]))
-    other = [fetch(blocks, near(1))]
+    low, high = join_blocks(block, *(fetch(block, middle(o)) for o in OFF[1:]))
+    other = [fetch(low, near), fetch(high, near)]
     head, mark = load_head(head_weight)
-    blocks = gate(blocks, other[0], mark)
-    own = [blocks] + [fetch(blocks, final(o)) for o in OFF[1:]]
-    other = other + [fetch(v, near(1)) for v in own[1:]]
+    low, high = gate(low, high, *other, mark)
+    ahead_low, back_high = fetch(low, final(1)), fetch(high, final(-1))
+    ahead_high, back_low = fetch(high, final(1)), fetch(low, final(-1))
+    far_low, far_high = fetch(ahead_low, final(1)), fetch(back_high, final(-1))
+    own = [low, high, ahead_low, ahead_high, back_low, back_high, far_low, far_high]
+    other += [fetch(v, near) for v in own[2:]]
 
     rows, logits, stats, target = local_logits(ids, own, other, head)
     stats = merge(exchange(stats, ("z", "c")))
@@ -452,11 +465,18 @@
     log_norm, weight, loss = preference(stats, lengths, ref_logps, pairing)
 
     logit_grad, send = grad_other_first(ids, logits, log_norm, weight, target, head)
-    received = [fetch(send, near(1))]
-    received.append(fetch(grad_other_second(ids, logit_grad, head), near(1)))
+    received = [fetch(send, near)]
+    received.append(fetch(grad_other_second(ids, logit_grad, head), near))
     *parts, mark = grad_own(ids, logit_grad, head, received, arrived(received[0]))
     grad_head, mark = grad_head_of(rows, logit_grad, mark)
-    parts = split_middle(parts[0], *(fetch(parts[s], final(-OFF[s])) for s in (1, 2, 3)), mark)
+    keep_low, keep_high, ahead_low, ahead_high, back_low, back_high, far_low, far_high = parts
+    ahead_low = add(ahead_low, fetch(far_low, final(-1)))
+    back_high = add(back_high, fetch(far_high, final(1)))
+    parts = split_middle(
+        (keep_low, fetch(ahead_low, final(-1)), fetch(back_low, final(1))),
+        (keep_high, fetch(ahead_high, final(-1)), fetch(back_high, final(1))),
+        mark,
+    )
     parts = split_window(parts[0], *(fetch(parts[s], middle(-OFF[s])) for s in (1, 2, 3)))
     grad_hidden = finish(lax.all_to_all(parts, ("z", "c"), 0, 0, tiled=True))
     return grad_hidden.astype(bf16), grad_head, loss[0, 0]

time: 162 us -> 156 us (0.963)
  waiting for transfers between devices: 64.6 us -> 48.6 us
  starting transfers between devices: 35.5 us -> 48.8 us
  blocking collectives: 27.6 us -> 24.2 us
    ppermute x18 -> x28, waiting for transfers between devices: 43.1 us -> 27.1 us  [fetch(): return lax.ppermute(value, AXES, pairs)]
    ppermute x18 -> x28, starting transfers between devices: 19.8 us -> 32.2 us  [fetch(): return lax.ppermute(value, AXES, pairs)]
    all_to_all x1, blocking collectives: 13.7 us -> 11.6 us  [local(): stats = lax.all_to_all(stats, ('y', 'x'), 0, 0, tiled=True)]
    pallas_call x4 -> x6, Pallas kernels: 4.29 us -> 4.45 us  [the longest x1 4.11 us: grad_own(): call(grad_own_kernel, [shape((2, WIN, HALF), t) for t in PART_TYPES] + [s...]
  transfers between devices with their start and end apart: 20 -> 30, of which waited for: 14 -> 15; matrix products, arithmetic and copies ran while one was open for 0% -> 0% of each run, Pallas kernels for 6% -> 7%
where the time goes in v1:
time: 156 us
  starting transfers between devices  48.8 us (31%)
  waiting for transfers between devices  48.6 us (31%)
  Pallas kernels  27.2 us (17%)
  blocking collectives  24.2 us (16%)
  local copies, waits for them, and re-layouts  4.74 us (3%)
    ppermute x28, starting transfers between devices, fetch(): return lax.ppermute(value, AXES, pairs)  32.2 us
    ppermute x28, waiting for transfers between devices, fetch(): return lax.ppermute(value, AXES, pairs)  27.1 us
    all_to_all x1, blocking collectives, exchange(): lax.all_to_all(jnp.broadcast_to(value[None], (16,) + value.shape), axes,...  12.7 us
    all_to_all x1, waiting for transfers between devices, local(): lax.all_to_all(jnp.broadcast_to(jnp.stack([first, second])[None], (NZ, 2,...  11.6 us
    all_to_all x1, blocking collectives, local(): stats = lax.all_to_all(stats, ('y', 'x'), 0, 0, tiled=True)  11.6 us
    all_to_all x1, starting transfers between devices, local(): lax.all_to_all(jnp.broadcast_to(jnp.stack([first, second])[None], (NZ, 2,...  9.98 us
    all_to_all x1, waiting for transfers between devices, local(): grad_hidden = finish(lax.all_to_all(parts, ('z', 'c'), 0, 0, tiled=True))  9.87 us
    pallas_call x1, Pallas kernels, grad_head_of(): pl.pallas_call(head_kernel, grid=(D // BLOCK,), in_specs=[pl.BlockSpec((T...  8.02 us
  transfers between devices with their start and end apart: 30, of which 15 were waited for; matrix products, arithmetic and copies ran while one was open for 0% of the time, Pallas kernels for 7%

profile of v1, /device:TPU:1, one launch (start us, length us, event | category | flops | bytes accessed | tf_op | source)
XLA Modules:
  0.0 155.7 jit_solution(4160984869899375302)
XLA Ops:
  3.0 10.0 %all-to-all-start = ((bf16[16,64,128]{2,1,0:T(8,128)(2,1)}), bf16[16,64,128]{2,1,0:T(8,128)(2,1)S(1)}, u32[]{:S(2)}, u32[]{:S(2)}) async-start(bf16[16,64,128]{2,1,0:T(8,128)(2,1)} %bitcast.12), calls=%async_computation | async-start | bytes 524288 | tf_op jit(solution)/shard_map/all_to_all | solution.py:447
  13.0 11.6 %all-to-all-done.parts = bf16[16,64,128]{2,1,0:T(8,128)(2,1)S(1)} async-done(((bf16[16,64,128]{2,1,0:T(8,128)(2,1)}), bf16[16,64,128]{2,1,0:T(8,128)(2,1)S(1)}, u32[]{:S(2)}, u32[]{:S(2)}) %all-to-all-start) | async-done | bytes 262176 | tf_op jit(solution)/shard_map/all_to_all | solution.py:447
  25.4 2.8 %collective-permute-start.2 = (bf16[48,2176]{1,0:T(8,128)(2,1)S(1)}, bf16[48,2176]{1,0:T(8,128)(2,1)S(1)}, u32[]{:S(2)}, u32[]{:S(2)}) collective-permute-start(bf16[48,2176]{1,0:T(8,128)(2,1)S(1)} %shard_map.85.a), channel_id=1, source_target_pairs={{128,0},{33,1},{130,2},{35,3},{132,4},{37,5},{134,6},{39,7},{136,8... | collective-permute-start | bytes 626696 | tf_op jit(solution)/shard_map/ppermute | solution.py:44
  28.5 2.4 %collective-permute-start = (bf16[48,2176]{1,0:T(8,128)(2,1)S(1)}, bf16[48,2176]{1,0:T(8,128)(2,1)S(1)}, u32[]{:S(2)}, u32[]{:S(2)}) collective-permute-start(bf16[48,2176]{1,0:T(8,128)(2,1)S(1)} %shard_map.85.a), channel_id=1, source_target_pairs={{64,0},{17,1},{66,2},{19,3},{68,4},{21,5},{70,6},{23,7},{72,8},{25... | collective-permute-start | bytes 626696 | tf_op jit(solution)/shard_map/ppermute | solution.py:44
  31.9 2.5 %collective-permute-done.1.c = bf16[48,2176]{1,0:T(8,128)(2,1)S(1)} collective-permute-done((bf16[48,2176]{1,0:T(8,128)(2,1)S(1)}, bf16[48,2176]{1,0:T(8,128)(2,1)S(1)}, u32[]{:S(2)}, u32[]{:S(2)}) %collective-permute-start.1) | collective-permute-done | bytes 208928 | tf_op jit(solution)/shard_map/ppermute | solution.py:44
  35.5 2.5 %copy-done = bf16[4096,640]{1,0:T(8,128)(2,1)S(1)} copy-done((bf16[4096,640]{1,0:T(8,128)(2,1)S(1)}, bf16[4096,640]{1,0:T(8,128)(2,1)}, u32[]{:S(2)}) %copy-start) | copy-done | bytes 5242904
  39.3 2.2 %collective-permute-start.5 = (bf16[2,48,2176]{2,1,0:T(8,128)(2,1)S(1)}, bf16[2,48,2176]{2,1,0:T(8,128)(2,1)S(1)}, u32[]{:S(2)}, u32[]{:S(2)}) collective-permute-start(bf16[2,48,2176]{2,1,0:T(8,128)(2,1)S(1)} %get-tuple-element.36.refs_0_), channel_id=1, source_target_pairs={{16,0},{65,1},{18,2},{67,3},{20,4},{69,5},{22,6},{71,7},{24,8},{73... | collective-permute-start | bytes 1253384 | tf_op jit(solution)/shard_map/ppermute | solution.py:44
  41.6 2.7 %collective-permute-start.6 = (bf16[2,48,2176]{2,1,0:T(8,128)(2,1)S(1)}, bf16[2,48,2176]{2,1,0:T(8,128)(2,1)S(1)}, u32[]{:S(2)}, u32[]{:S(2)}) collective-permute-start(bf16[2,48,2176]{2,1,0:T(8,128)(2,1)S(1)} %get-tuple-element.37.refs_1_), channel_id=1, source_target_pairs={{16,0},{65,1},{18,2},{67,3},{20,4},{69,5},{22,6},{71,7},{24,8},{73... | collective-permute-start | bytes 1253384 | tf_op jit(solution)/shard_map/ppermute | solution.py:44
  44.2 3.0 %collective-permute-done.7.refs_4_ = bf16[2,48,2176]{2,1,0:T(8,128)(2,1)S(1)} collective-permute-done((bf16[2,48,2176]{2,1,0:T(8,128)(2,1)S(1)}, bf16[2,48,2176]{2,1,0:T(8,128)(2,1)S(1)}, u32[]{:S(2)}, u32[]{:S(2)}) %collective-permute-start.7) | collective-permute-done | bytes 417824 | tf_op jit(solution)/shard_map/ppermute | solution.py:44
  48.2 3.0 %collective-permute-start.9 = (bf16[2,48,2176]{2,1,0:T(8,128)(2,1)S(1)}, bf16[2,48,2176]{2,1,0:T(8,128)(2,1)S(1)}, u32[]{:S(2)}, u32[]{:S(2)}) collective-permute-start(bf16[2,48,2176]{2,1,0:T(8,128)(2,1)S(1)} %collective-permute-done.5.refs_2_), channel_id=1, source_target_pairs={{16,0},{65,1},{18,2},{67,3},{20,4},{69,5},{22,6},{71,7},{24,8},{73... | collective-permute-start | bytes 1253384 | tf_op jit(solution)/shard_map/ppermute | solution.py:44
  53.5 2.7 %collective-permute-done.9.refs_6_ = bf16[2,48,2176]{2,1,0:T(8,128)(2,1)S(1)} collective-permute-done((bf16[2,48,2176]{2,1,0:T(8,128)(2,1)S(1)}, bf16[2,48,2176]{2,1,0:T(8,128)(2,1)S(1)}, u32[]{:S(2)}, u32[]{:S(2)}) %collective-permute-start.9) | collective-permute-done | bytes 417824 | tf_op jit(solution)/shard_map/ppermute | solution.py:44
  57.4 2.7 %collective-permute-done.10.refs_7_ = bf16[2,48,2176]{2,1,0:T(8,128)(2,1)S(1)} collective-permute-done((bf16[2,48,2176]{2,1,0:T(8,128)(2,1)S(1)}, bf16[2,48,2176]{2,1,0:T(8,128)(2,1)S(1)}, u32[]{:S(2)}, u32[]{:S(2)}) %collective-permute-start.10) | collective-permute-done | bytes 417824 | tf_op jit(solution)/shard_map/ppermute | solution.py:44
  60.1 1.8 %collective-permute-start.16 = (bf16[2,48,2176]{2,1,0:T(8,128)(2,1)S(1)}, bf16[2,48,2176]{2,1,0:T(8,128)(2,1)S(1)}, u32[]{:S(2)}, u32[]{:S(2)}) collective-permute-start(bf16[2,48,2176]{2,1,0:T(8,128)(2,1)S(1)} %collective-permute-done.10.refs_7_), channel_id=1, source_target_pairs={{1,0},{0,1},{3,2},{2,3},{5,4},{4,5},{7,6},{6,7},{9,8},{8,9},{11,10... | collective-permute-start | bytes 1253384 | tf_op jit(solution)/shard_map/ppermute | solution.py:44
  61.9 1.4 collective-permute-done.16.refs_15_
  63.3 7.1 %shard_map.89 = (bf16[768,4096]{1,0:T(8,128)(2,1)S(1)}, f32[768,640]{1,0:T(8,128)S(1)}, f32[2,8,128]{2,1,0:T(8,128)S(1)}, f32[8,128]{1,0:T(8,128)S(1)}) custom-call(s32[5]{0:T(128)S(1)} %stack.44.ids, bf16[2,48,2176]{2,1,0:T(8,128)(2,1)S(1)} %get-tuple-element.36.refs_0_, bf16[2,48,2176]{2,1,0:T(8,128)(2,1)S(1)} %get-tuple-element.37.refs_1_, ...), custom_call_target="tpu_custom_call" | custom-call | flops 4026531840 | bytes 20971520 | tf_op jit(solution)/shard_map/pallas_call | solution.py:187
  70.4 12.7 %all_to_all.20.parts = f32[16,2,8,128]{3,2,1,0:T(8,128)S(1)} all-to-all(f32[16,2,8,128]{3,2,1,0:T(8,128)S(1)} %broadcast_in_dim.5), channel_id=1, replica_groups=mesh['y'=4,'x'=4,'z'=8,'c'=2] {'z','c'}, dimensions={0} | all-to-all | bytes 262144 | tf_op jit(solution)/shard_map/all_to_all | solution.py:207
  83.1 11.6 %all_to_all.21.parts = f32[16,2,8,128]{3,2,1,0:T(8,128)S(1)} all-to-all(f32[16,2,8,128]{3,2,1,0:T(8,128)S(1)} %shard_map.90), channel_id=1, replica_groups=mesh['y'=4,'x'=4,'z'=8,'c'=2] {'y','x'}, dimensions={0} | all-to-all | bytes 262144 | tf_op jit(solution)/shard_map/all_to_all | solution.py:464
  95.5 2.6 %shard_map.92 = (bf16[768,640]{1,0:T(8,128)(2,1)S(1)}, bf16[768,1024]{1,0:T(8,128)(2,1)S(1)}) custom-call(s32[5]{0:T(128)S(1)} %stack.44.ids, f32[768,640]{1,0:T(8,128)S(1)} %get-tuple-element.39.logits, f32[8,128]{1,0:T(8,128)S(1)} %get-tuple-element.41.norm, f32[8,128]{1,0:T(8,128)S(1)} %get-tuple-element.42.weight, ...), custom_call_target="tpu_custom_call" | custom-call | flops 1006632960 | bytes 6291456 | tf_op jit(solution)/shard_map/pallas_call | solution.py:298
  99.0 2.0 %shard_map.93 = bf16[768,1024]{1,0:T(8,128)(2,1)S(1)} custom-call(s32[5]{0:T(128)S(1)} %stack.44.ids, bf16[768,640]{1,0:T(8,128)(2,1)S(1)} %get-tuple-element.44.grad, bf16[4096,640]{1,0:T(8,128)(2,1)S(1)} %get-tuple-element.38.refs_16_.head), custom_call_target="tpu_custom_call" | custom-call | flops 2013265920 | bytes 16777216 | tf_op jit(solution)/shard_map/pallas_call | solution.py:309
  102.1 2.7 %collective-permute-done.18.other1 = bf16[768,1024]{1,0:T(8,128)(2,1)S(1)} collective-permute-done((bf16[768,1024]{1,0:T(8,128)(2,1)S(1)}, bf16[768,1024]{1,0:T(8,128)(2,1)S(1)}, u32[]{:S(2)}, u32[]{:S(2)}) %collective-permute-start.18) | collective-permute-done | bytes 1572896 | tf_op jit(solution)/shard_map/ppermute | solution.py:44
  104.7 4.1 %shard_map.95 = (f32[2,48,2048]{2,1,0:T(8,128)S(1)}, f32[2,48,2048]{2,1,0:T(8,128)S(1)}, f32[2,48,2048]{2,1,0:T(8,128)S(1)}, bf16[2,48,2048]{2,1,0:T(8,128)(2,1)...) custom-call(s32[5]{0:T(128)S(1)} %stack.44.ids, ...), custom_call_target="tpu_custom_call" | custom-call | tf_op jit(solution)/shard_map/pallas_call | solution.py:346
  108.9 2.7 %collective-permute-start.23 = (bf16[2,48,2048]{2,1,0:T(8,128)(2,1)S(1)}, bf16[2,48,2048]{2,1,0:T(8,128)(2,1)S(1)}, u32[]{:S(2)}, u32[]{:S(2)}) collective-permute-start(bf16[2,48,2048]{2,1,0:T(8,128)(2,1)S(1)} %get-tuple-element.53), channel_id=1, source_target_pairs={{16,0},{65,1},{18,2},{67,3},{20,4},{69,5},{22,6},{71,7},{24,8},{73... | collective-permute-start | bytes 1179656 | tf_op jit(solution)/shard_map/ppermute | solution.py:44
  111.6 1.4 collective-permute-start.22
  113.1 4.0 %collective-permute-done.19.b = bf16[2,48,2048]{2,1,0:T(8,128)(2,1)S(1)} collective-permute-done((bf16[2,48,2048]{2,1,0:T(8,128)(2,1)S(1)}, bf16[2,48,2048]{2,1,0:T(8,128)(2,1)S(1)}, u32[]{:S(2)}, u32[]{:S(2)}) %collective-permute-start.19) | collective-permute-done | bytes 393248 | tf_op jit(solution)/shard_map/ppermute | solution.py:44
  117.3 2.7 %collective-permute-start.24 = (bf16[2,48,2048]{2,1,0:T(8,128)(2,1)S(1)}, bf16[2,48,2048]{2,1,0:T(8,128)(2,1)S(1)}, u32[]{:S(2)}, u32[]{:S(2)}) collective-permute-start(bf16[2,48,2048]{2,1,0:T(8,128)(2,1)S(1)} %shard_map.97), channel_id=1, source_target_pairs={{16,0},{65,1},{18,2},{67,3},{20,4},{69,5},{22,6},{71,7},{24,8},{73... | collective-permute-start | bytes 1179656 | tf_op jit(solution)/shard_map/ppermute | solution.py:44
  120.1 8.0 %shard_map.98 = (bf16[4096,640]{1,0:T(8,128)(2,1)}, f32[8,128]{1,0:T(8,128)S(1)}) custom-call(bf16[768,4096]{1,0:T(8,128)(2,1)S(1)} %get-tuple-element.54.hidden, bf16[768,640]{1,0:T(8,128)(2,1)S(1)} %get-tuple-element.44.grad, f32[8,128]{1,0:T(8,128)S(1)} %get-tuple-element.55.after), custom_call_target="tpu_custom_call" | custom-call | flops 4026531840 | bytes 12582912 | tf_op jit(solution)/shard_map/pallas_call | solution.py:363
  128.4 2.7 %collective-permute-start.26 = (bf16[48,2048]{1,0:T(8,128)(2,1)S(1)}, bf16[48,2048]{1,0:T(8,128)(2,1)S(1)}, u32[]{:S(2)}, u32[]{:S(2)}) collective-permute-start(bf16[48,2048]{1,0:T(8,128)(2,1)S(1)} %get-tuple-element.59), channel_id=1, source_target_pairs={{64,0},{17,1},{66,2},{19,3},{68,4},{21,5},{70,6},{23,7},{72,8},{25... | collective-permute-start | bytes 589832 | tf_op jit(solution)/shard_map/ppermute | solution.py:44
  131.1 3.3 %collective-permute-done.25.b = bf16[48,2048]{1,0:T(8,128)(2,1)S(1)} collective-permute-done((bf16[48,2048]{1,0:T(8,128)(2,1)S(1)}, bf16[48,2048]{1,0:T(8,128)(2,1)S(1)}, u32[]{:S(2)}, u32[]{:S(2)}) %collective-permute-start.25) | collective-permute-done | bytes 196640 | tf_op jit(solution)/shard_map/ppermute | solution.py:44
  134.5 1.4 collective-permute-done.26.c
  135.8 1.3 collective-permute-done.27.d
  138.0 6.6 %all-to-all-start.3 = ((bf16[16,48,128]{2,1,0:T(8,128)(2,1)}), bf16[16,48,128]{2,1,0:T(8,128)(2,1)S(1)}, u32[]{:S(2)}, u32[]{:S(2)}) async-start(bf16[16,48,128]{2,1,0:T(8,128)(2,1)} %shard_map.100), calls=%async_computation.3 | async-start | bytes 393216 | tf_op jit(solution)/shard_map/all_to_all | solution.py:481
  145.1 9.9 %all-to-all-done.3.parts = bf16[16,48,128]{2,1,0:T(8,128)(2,1)S(1)} async-done(((bf16[16,48,128]{2,1,0:T(8,128)(2,1)}), bf16[16,48,128]{2,1,0:T(8,128)(2,1)S(1)}, u32[]{:S(2)}, u32[]{:S(2)}) %all-to-all-start.3) | async-done | bytes 196640 | tf_op jit(solution)/shard_map/all_to_all | solution.py:481
  (67 shorter events, 17.1 us)
Async XLA Ops:
  3.0 21.7 %all-to-all-start = ((bf16[16,64,128]{2,1,0:T(8,128)(2,1)}), bf16[16,64,128]{2,1,0:T(8,128)(2,1)S(1)}, u32[]{:S(2)}, u32[]{:S(2)}) async-start(bf16[16,64,128]{2,1,0:T(8,128)(2,1)} %bitcast.12), calls=%async_computation | async-start | bytes 524288 | tf_op jit(solution)/shard_map/all_to_all | solution.py:447
  25.4 6.5 %collective-permute-start.2 = (bf16[48,2176]{1,0:T(8,128)(2,1)S(1)}, bf16[48,2176]{1,0:T(8,128)(2,1)S(1)}, u32[]{:S(2)}, u32[]{:S(2)}) collective-permute-start(bf16[48,2176]{1,0:T(8,128)(2,1)S(1)} %shard_map.85.a), channel_id=1, source_target_pairs={{128,0},{33,1},{130,2},{35,3},{132,4},{37,5},{134,6},{39,7},{136,8... | collective-permute-start | bytes 626696 | tf_op jit(solution)/shard_map/ppermute | solution.py:44
  28.2 6.2 %collective-permute-start.1 = (bf16[48,2176]{1,0:T(8,128)(2,1)S(1)}, bf16[48,2176]{1,0:T(8,128)(2,1)S(1)}, u32[]{:S(2)}, u32[]{:S(2)}) collective-permute-start(bf16[48,2176]{1,0:T(8,128)(2,1)S(1)} %shard_map.85.a), channel_id=1, source_target_pairs={{192,0},{49,1},{194,2},{51,3},{196,4},{53,5},{198,6},{55,7},{200,8... | collective-permute-start | bytes 626696 | tf_op jit(solution)/shard_map/ppermute | solution.py:44
  28.5 5.8 %collective-permute-start = (bf16[48,2176]{1,0:T(8,128)(2,1)S(1)}, bf16[48,2176]{1,0:T(8,128)(2,1)S(1)}, u32[]{:S(2)}, u32[]{:S(2)}) collective-permute-start(bf16[48,2176]{1,0:T(8,128)(2,1)S(1)} %shard_map.85.a), channel_id=1, source_target_pairs={{64,0},{17,1},{66,2},{19,3},{68,4},{21,5},{70,6},{23,7},{72,8},{25... | collective-permute-start | bytes 626696 | tf_op jit(solution)/shard_map/ppermute | solution.py:44
  34.4 3.9 %collective-permute-start.3 = (bf16[2,48,2176]{2,1,0:T(8,128)(2,1)S(1)}, bf16[2,48,2176]{2,1,0:T(8,128)(2,1)S(1)}, u32[]{:S(2)}, u32[]{:S(2)}) collective-permute-start(bf16[2,48,2176]{2,1,0:T(8,128)(2,1)S(1)} %get-tuple-element.33.low), channel_id=1, source_target_pairs={{1,0},{0,1},{3,2},{2,3},{5,4},{4,5},{7,6},{6,7},{9,8},{8,9},{11,10... | collective-permute-start | bytes 1253384 | tf_op jit(solution)/shard_map/ppermute | solution.py:44
  35.4 3.0 %collective-permute-start.4 = (bf16[2,48,2176]{2,1,0:T(8,128)(2,1)S(1)}, bf16[2,48,2176]{2,1,0:T(8,128)(2,1)S(1)}, u32[]{:S(2)}, u32[]{:S(2)}) collective-permute-start(bf16[2,48,2176]{2,1,0:T(8,128)(2,1)S(1)} %get-tuple-element.34.high), channel_id=1, source_target_pairs={{1,0},{0,1},{3,2},{2,3},{5,4},{4,5},{7,6},{6,7},{9,8},{8,9},{11,10... | collective-permute-start | bytes 1253384 | tf_op jit(solution)/shard_map/ppermute | solution.py:44
  38.4 8.8 %collective-permute-start.7 = (bf16[2,48,2176]{2,1,0:T(8,128)(2,1)S(1)}, bf16[2,48,2176]{2,1,0:T(8,128)(2,1)S(1)}, u32[]{:S(2)}, u32[]{:S(2)}) collective-permute-start(bf16[2,48,2176]{2,1,0:T(8,128)(2,1)S(1)} %get-tuple-element.36.refs_0_), channel_id=1, source_target_pairs={{48,0},{193,1},{50,2},{195,3},{52,4},{197,5},{54,6},{199,7},{56,8}... | collective-permute-start | bytes 1253384 | tf_op jit(solution)/shard_map/ppermute | solution.py:44
  39.3 8.9 %collective-permute-start.5 = (bf16[2,48,2176]{2,1,0:T(8,128)(2,1)S(1)}, bf16[2,48,2176]{2,1,0:T(8,128)(2,1)S(1)}, u32[]{:S(2)}, u32[]{:S(2)}) collective-permute-start(bf16[2,48,2176]{2,1,0:T(8,128)(2,1)S(1)} %get-tuple-element.36.refs_0_), channel_id=1, source_target_pairs={{16,0},{65,1},{18,2},{67,3},{20,4},{69,5},{22,6},{71,7},{24,8},{73... | collective-permute-start | bytes 1253384 | tf_op jit(solution)/shard_map/ppermute | solution.py:44
  41.6 10.1 %collective-permute-start.8 = (bf16[2,48,2176]{2,1,0:T(8,128)(2,1)S(1)}, bf16[2,48,2176]{2,1,0:T(8,128)(2,1)S(1)}, u32[]{:S(2)}, u32[]{:S(2)}) collective-permute-start(bf16[2,48,2176]{2,1,0:T(8,128)(2,1)S(1)} %get-tuple-element.37.refs_1_), channel_id=1, source_target_pairs={{48,0},{193,1},{50,2},{195,3},{52,4},{197,5},{54,6},{199,7},{56,8}... | collective-permute-start | bytes 1253384 | tf_op jit(solution)/shard_map/ppermute | solution.py:44
  41.6 11.4 %collective-permute-start.6 = (bf16[2,48,2176]{2,1,0:T(8,128)(2,1)S(1)}, bf16[2,48,2176]{2,1,0:T(8,128)(2,1)S(1)}, u32[]{:S(2)}, u32[]{:S(2)}) collective-permute-start(bf16[2,48,2176]{2,1,0:T(8,128)(2,1)S(1)} %get-tuple-element.37.refs_1_), channel_id=1, source_target_pairs={{16,0},{65,1},{18,2},{67,3},{20,4},{69,5},{22,6},{71,7},{24,8},{73... | collective-permute-start | bytes 1253384 | tf_op jit(solution)/shard_map/ppermute | solution.py:44
  47.2 5.8 %collective-permute-start.13 = (bf16[2,48,2176]{2,1,0:T(8,128)(2,1)S(1)}, bf16[2,48,2176]{2,1,0:T(8,128)(2,1)S(1)}, u32[]{:S(2)}, u32[]{:S(2)}) collective-permute-start(bf16[2,48,2176]{2,1,0:T(8,128)(2,1)S(1)} %collective-permute-done.7.refs_4_), channel_id=1, source_target_pairs={{1,0},{0,1},{3,2},{2,3},{5,4},{4,5},{7,6},{6,7},{9,8},{8,9},{11,10... | collective-permute-start | bytes 1253384 | tf_op jit(solution)/shard_map/ppermute | solution.py:44
  48.2 7.9 %collective-permute-start.9 = (bf16[2,48,2176]{2,1,0:T(8,128)(2,1)S(1)}, bf16[2,48,2176]{2,1,0:T(8,128)(2,1)S(1)}, u32[]{:S(2)}, u32[]{:S(2)}) collective-permute-start(bf16[2,48,2176]{2,1,0:T(8,128)(2,1)S(1)} %collective-permute-done.5.refs_2_), channel_id=1, source_target_pairs={{16,0},{65,1},{18,2},{67,3},{20,4},{69,5},{22,6},{71,7},{24,8},{73... | collective-permute-start | bytes 1253384 | tf_op jit(solution)/shard_map/ppermute | solution.py:44
  51.7 8.4 %collective-permute-start.10 = (bf16[2,48,2176]{2,1,0:T(8,128)(2,1)S(1)}, bf16[2,48,2176]{2,1,0:T(8,128)(2,1)S(1)}, u32[]{:S(2)}, u32[]{:S(2)}) collective-permute-start(bf16[2,48,2176]{2,1,0:T(8,128)(2,1)S(1)} %collective-permute-done.8.refs_5_), channel_id=1, source_target_pairs={{48,0},{193,1},{50,2},{195,3},{52,4},{197,5},{54,6},{199,7},{56,8}... | collective-permute-start | bytes 1253384 | tf_op jit(solution)/shard_map/ppermute | solution.py:44
  51.7 10.2 %collective-permute-start.11 = (bf16[2,48,2176]{2,1,0:T(8,128)(2,1)S(1)}, bf16[2,48,2176]{2,1,0:T(8,128)(2,1)S(1)}, u32[]{:S(2)}, u32[]{:S(2)}) collective-permute-start(bf16[2,48,2176]{2,1,0:T(8,128)(2,1)S(1)} %collective-permute-done.5.refs_2_), channel_id=1, source_target_pairs={{1,0},{0,1},{3,2},{2,3},{5,4},{4,5},{7,6},{6,7},{9,8},{8,9},{11,10... | collective-permute-start | bytes 1253384 | tf_op jit(solution)/shard_map/ppermute | solution.py:44
  52.9 9.0 %collective-permute-start.14 = (bf16[2,48,2176]{2,1,0:T(8,128)(2,1)S(1)}, bf16[2,48,2176]{2,1,0:T(8,128)(2,1)S(1)}, u32[]{:S(2)}, u32[]{:S(2)}) collective-permute-start(bf16[2,48,2176]{2,1,0:T(8,128)(2,1)S(1)} %collective-permute-done.8.refs_5_), channel_id=1, source_target_pairs={{1,0},{0,1},{3,2},{2,3},{5,4},{4,5},{7,6},{6,7},{9,8},{8,9},{11,10... | collective-permute-start | bytes 1253384 | tf_op jit(solution)/shard_map/ppermute | solution.py:44
  52.9 9.0 %collective-permute-start.12 = (bf16[2,48,2176]{2,1,0:T(8,128)(2,1)S(1)}, bf16[2,48,2176]{2,1,0:T(8,128)(2,1)S(1)}, u32[]{:S(2)}, u32[]{:S(2)}) collective-permute-start(bf16[2,48,2176]{2,1,0:T(8,128)(2,1)S(1)} %collective-permute-done.6.refs_3_), channel_id=1, source_target_pairs={{1,0},{0,1},{3,2},{2,3},{5,4},{4,5},{7,6},{6,7},{9,8},{8,9},{11,10... | collective-permute-start | bytes 1253384 | tf_op jit(solution)/shard_map/ppermute | solution.py:44
  56.1 5.8 %collective-permute-start.15 = (bf16[2,48,2176]{2,1,0:T(8,128)(2,1)S(1)}, bf16[2,48,2176]{2,1,0:T(8,128)(2,1)S(1)}, u32[]{:S(2)}, u32[]{:S(2)}) collective-permute-start(bf16[2,48,2176]{2,1,0:T(8,128)(2,1)S(1)} %collective-permute-done.9.refs_6_), channel_id=1, source_target_pairs={{1,0},{0,1},{3,2},{2,3},{5,4},{4,5},{7,6},{6,7},{9,8},{8,9},{11,10... | collective-permute-start | bytes 1253384 | tf_op jit(solution)/shard_map/ppermute | solution.py:44
  60.1 3.2 %collective-permute-start.16 = (bf16[2,48,2176]{2,1,0:T(8,128)(2,1)S(1)}, bf16[2,48,2176]{2,1,0:T(8,128)(2,1)S(1)}, u32[]{:S(2)}, u32[]{:S(2)}) collective-permute-start(bf16[2,48,2176]{2,1,0:T(8,128)(2,1)S(1)} %collective-permute-done.10.refs_7_), channel_id=1, source_target_pairs={{1,0},{0,1},{3,2},{2,3},{5,4},{4,5},{7,6},{6,7},{9,8},{8,9},{11,10... | collective-permute-start | bytes 1253384 | tf_op jit(solution)/shard_map/ppermute | solution.py:44
  63.3 31.4 %copy-start.2 = (f32[16]{0:T(128)S(1)}, f32[16]{0:T(128)}, u32[]{:S(2)}) copy-start(f32[16]{0:T(128)} %ref_logps.1) | copy-start | bytes 196
  63.3 31.4 %copy-start.3 = (s32[16]{0:T(128)S(1)}, s32[16]{0:T(128)}, u32[]{:S(2)}) copy-start(s32[16]{0:T(128)} %pairing.1) | copy-start | bytes 196
  98.1 4.0 %collective-permute-start.17 = (bf16[768,1024]{1,0:T(8,128)(2,1)S(1)}, bf16[768,1024]{1,0:T(8,128)(2,1)S(1)}, u32[]{:S(2)}, u32[]{:S(2)}) collective-permute-start(bf16[768,1024]{1,0:T(8,128)(2,1)S(1)} %get-tuple-element.45), channel_id=1, source_target_pairs={{1,0},{0,1},{3,2},{2,3},{5,4},{4,5},{7,6},{6,7},{9,8},{8,9},{11,10... | collective-permute-start | bytes 4718600 | tf_op jit(solution)/shard_map/ppermute | solution.py:44
  101.0 3.7 %collective-permute-start.18 = (bf16[768,1024]{1,0:T(8,128)(2,1)S(1)}, bf16[768,1024]{1,0:T(8,128)(2,1)S(1)}, u32[]{:S(2)}, u32[]{:S(2)}) collective-permute-start(bf16[768,1024]{1,0:T(8,128)(2,1)S(1)} %shard_map.93), channel_id=1, source_target_pairs={{1,0},{0,1},{3,2},{2,3},{5,4},{4,5},{7,6},{6,7},{9,8},{8,9},{11,10... | collective-permute-start | bytes 4718600 | tf_op jit(solution)/shard_map/ppermute | solution.py:44
  108.8 8.2 %collective-permute-start.19 = (bf16[2,48,2048]{2,1,0:T(8,128)(2,1)S(1)}, bf16[2,48,2048]{2,1,0:T(8,128)(2,1)S(1)}, u32[]{:S(2)}, u32[]{:S(2)}) collective-permute-start(bf16[2,48,2048]{2,1,0:T(8,128)(2,1)S(1)} %get-tuple-element.48), channel_id=1, source_target_pairs={{48,0},{193,1},{50,2},{195,3},{52,4},{197,5},{54,6},{199,7},{56,8}... | collective-permute-start | bytes 1179656 | tf_op jit(solution)/shard_map/ppermute | solution.py:44
  108.9 8.3 %collective-permute-start.23 = (bf16[2,48,2048]{2,1,0:T(8,128)(2,1)S(1)}, bf16[2,48,2048]{2,1,0:T(8,128)(2,1)S(1)}, u32[]{:S(2)}, u32[]{:S(2)}) collective-permute-start(bf16[2,48,2048]{2,1,0:T(8,128)(2,1)S(1)} %get-tuple-element.53), channel_id=1, source_target_pairs={{16,0},{65,1},{18,2},{67,3},{20,4},{69,5},{22,6},{71,7},{24,8},{73... | collective-permute-start | bytes 1179656 | tf_op jit(solution)/shard_map/ppermute | solution.py:44
  111.6 16.5 %collective-permute-start.21 = (bf16[2,48,2048]{2,1,0:T(8,128)(2,1)S(1)}, bf16[2,48,2048]{2,1,0:T(8,128)(2,1)S(1)}, u32[]{:S(2)}, u32[]{:S(2)}) collective-permute-start(bf16[2,48,2048]{2,1,0:T(8,128)(2,1)S(1)} %get-tuple-element.49), channel_id=1, source_target_pairs={{16,0},{65,1},{18,2},{67,3},{20,4},{69,5},{22,6},{71,7},{24,8},{73... | collective-permute-start | bytes 1179656 | tf_op jit(solution)/shard_map/ppermute | solution.py:44
  111.6 16.5 %collective-permute-start.22 = (bf16[2,48,2048]{2,1,0:T(8,128)(2,1)S(1)}, bf16[2,48,2048]{2,1,0:T(8,128)(2,1)S(1)}, u32[]{:S(2)}, u32[]{:S(2)}) collective-permute-start(bf16[2,48,2048]{2,1,0:T(8,128)(2,1)S(1)} %get-tuple-element.51), channel_id=1, source_target_pairs={{48,0},{193,1},{50,2},{195,3},{52,4},{197,5},{54,6},{199,7},{56,8}... | collective-permute-start | bytes 1179656 | tf_op jit(solution)/shard_map/ppermute | solution.py:44
  117.1 11.0 %collective-permute-start.20 = (bf16[2,48,2048]{2,1,0:T(8,128)(2,1)S(1)}, bf16[2,48,2048]{2,1,0:T(8,128)(2,1)S(1)}, u32[]{:S(2)}, u32[]{:S(2)}) collective-permute-start(bf16[2,48,2048]{2,1,0:T(8,128)(2,1)S(1)} %shard_map.96), channel_id=1, source_target_pairs={{48,0},{193,1},{50,2},{195,3},{52,4},{197,5},{54,6},{199,7},{56,8}... | collective-permute-start | bytes 1179656 | tf_op jit(solution)/shard_map/ppermute | solution.py:44
  117.3 10.8 %collective-permute-start.24 = (bf16[2,48,2048]{2,1,0:T(8,128)(2,1)S(1)}, bf16[2,48,2048]{2,1,0:T(8,128)(2,1)S(1)}, u32[]{:S(2)}, u32[]{:S(2)}) collective-permute-start(bf16[2,48,2048]{2,1,0:T(8,128)(2,1)S(1)} %shard_map.97), channel_id=1, source_target_pairs={{16,0},{65,1},{18,2},{67,3},{20,4},{69,5},{22,6},{71,7},{24,8},{73... | collective-permute-start | bytes 1179656 | tf_op jit(solution)/shard_map/ppermute | solution.py:44
  128.4 6.1 %collective-permute-start.25 = (bf16[48,2048]{1,0:T(8,128)(2,1)S(1)}, bf16[48,2048]{1,0:T(8,128)(2,1)S(1)}, u32[]{:S(2)}, u32[]{:S(2)}) collective-permute-start(bf16[48,2048]{1,0:T(8,128)(2,1)S(1)} %get-tuple-element.58), channel_id=1, source_target_pairs={{192,0},{49,1},{194,2},{51,3},{196,4},{53,5},{198,6},{55,7},{200,8... | collective-permute-start | bytes 589832 | tf_op jit(solution)/shard_map/ppermute | solution.py:44
  128.4 7.4 %collective-permute-start.26 = (bf16[48,2048]{1,0:T(8,128)(2,1)S(1)}, bf16[48,2048]{1,0:T(8,128)(2,1)S(1)}, u32[]{:S(2)}, u32[]{:S(2)}) collective-permute-start(bf16[48,2048]{1,0:T(8,128)(2,1)S(1)} %get-tuple-element.59), channel_id=1, source_target_pairs={{64,0},{17,1},{66,2},{19,3},{68,4},{21,5},{70,6},{23,7},{72,8},{25... | collective-permute-start | bytes 589832 | tf_op jit(solution)/shard_map/ppermute | solution.py:44
  131.1 6.0 %collective-permute-start.27 = (bf16[48,2048]{1,0:T(8,128)(2,1)S(1)}, bf16[48,2048]{1,0:T(8,128)(2,1)S(1)}, u32[]{:S(2)}, u32[]{:S(2)}) collective-permute-start(bf16[48,2048]{1,0:T(8,128)(2,1)S(1)} %get-tuple-element.60), channel_id=1, source_target_pairs={{128,0},{33,1},{130,2},{35,3},{132,4},{37,5},{134,6},{39,7},{136,8... | collective-permute-start | bytes 589832 | tf_op jit(solution)/shard_map/ppermute | solution.py:44
  138.0 16.9 %all-to-all-start.3 = ((bf16[16,48,128]{2,1,0:T(8,128)(2,1)}), bf16[16,48,128]{2,1,0:T(8,128)(2,1)S(1)}, u32[]{:S(2)}, u32[]{:S(2)}) async-start(bf16[16,48,128]{2,1,0:T(8,128)(2,1)} %shard_map.100), calls=%async_computation.3 | async-start | bytes 393216 | tf_op jit(solution)/shard_map/all_to_all | solution.py:481
  (2 other events, 33.9 us)

commit v2 on v1

--- a/solution.py
+++ b/solution.py
@@ -82,6 +82,32 @@
     return jax.ShapeDtypeStruct(dims, dtype)
 
 
+def first_message_kernel(targets, hidden, out, tok):
+    rows = hidden[...].astype(f32)
+    row = lax.broadcasted_iota(jnp.int32, (16, 128), 0)
+    lane = lax.broadcasted_iota(jnp.int32, (16, 128), 1)
+    meta = jnp.zeros((16, 128), f32)
+    for j in range(3):
+        goal = targets[j]
+        for n, digit in enumerate((goal & 255, (goal >> 8) & 255, goal >> 16)):
+            meta = jnp.where((row == j) & (lane == n), digit.astype(f32), meta)
+    meta = meta.astype(bf16)
+    for half in range(2):
+        for r in range(16):
+            at = half * HALF + r * 128
+            tok[pl.ds(r, 3, stride=16), :] = rows[:, at:at + 128]
+        part = tok[...].astype(bf16)
+        for z in range(NZ):
+            out[2 * z + half, 0:48, :] = part
+            out[2 * z + half, 48:64, :] = meta
+
+
+def first_message(targets, hidden):
+    return call(
+        first_message_kernel, shape((16, 64, 128), bf16), [SMEM, VMEM], [pltpu.VMEM((48, 128), f32)]
+    )(targets, hidden)
+
+
 def join_window_kernel(ids, parts, out, tok, meta):
     for dev in range(16):
         tok[dev * 48:(dev + 1) * 48, :] = parts[dev, 0:48, :].astype(f32)
@@ -101,21 +127,21 @@
     )(ids, parts)
 
 
-def join_blocks_kernel(a, b, c, d, low, high):
+def join_blocks_kernel(a, b, c, d, after, low, high):
     low[0], low[1], high[0], high[1] = a[...], b[...], c[...], d[...]
 
 
 def join_blocks(*blocks):
-    return call(join_blocks_kernel, [shape((2, WIN, WIDE), bf16)] * 2, [VMEM] * 4)(*blocks)
-
-
-def gate_kernel(low, high, first, second, third, out_low, out_high):
+    return call(join_blocks_kernel, [shape((2, WIN, WIDE), bf16)] * 2, [VMEM] * 5)(*blocks)
+
+
+def gate_kernel(low, high, first, second, out_low, out_high):
     out_low[...] = low[...]
     out_high[...] = high[...]
 
 
 def gate(low, high, *marks):
-    return call(gate_kernel, [shape(low.shape, low.dtype)] * 2, [VMEM] * 5)(low, high, *marks)
+    return call(gate_kernel, [shape(low.shape, low.dtype)] * 2, [VMEM] * 4)(low, high, *marks)
 
 
 def columns_of(rows):
@@ -352,39 +378,44 @@
     )(ids, grad, head, *other, after)
 
 
-def head_kernel(hidden, grad, after, out, mark):
+def head_kernel(hidden, grad, *refs):
+    out, mark = refs[-2:]
     mark[...] = jnp.zeros_like(mark)
     out[...] = lax.dot_general(
         hidden[...], grad[...], (((0,), (0,)), ((), ())), preferred_element_type=f32
     ).astype(out.dtype)
 
 
-def grad_head_of(hidden, grad, after):
+def grad_head_half(hidden, grad, after, first=None):
+    steps = D // BLOCK // 2
+    base = 0 if first is None else steps
     return pl.pallas_call(
         head_kernel,
-        grid=(D // BLOCK,),
+        grid=(steps,),
         in_specs=[
-            pl.BlockSpec((TOKENS, BLOCK), lambda i: (0, i)),
+            pl.BlockSpec((TOKENS, BLOCK), lambda i: (0, i + base)),
             pl.BlockSpec((TOKENS, COLS), lambda i: (0, 0)),
             pl.BlockSpec((8, 128), lambda i: (0, 0)),
-        ],
-        out_specs=(pl.BlockSpec((BLOCK, COLS), lambda i: (i, 0)), pl.BlockSpec((8, 128), lambda i: (0, 0))),
+        ] + ([] if first is None else [pl.BlockSpec(memory_space=pl.ANY)]),
+        out_specs=(pl.BlockSpec((BLOCK, COLS), lambda i: (i + base, 0)), pl.BlockSpec((8, 128), lambda i: (0, 0))),
         out_shape=(shape((D, COLS), bf16), shape((8, 128), f32)),
+        input_output_aliases={} if first is None else {3: 0},
         compiler_params=pltpu.CompilerParams(vmem_limit_bytes=20 * MB),
-        cost_estimate=pl.CostEstimate(flops=2 * TOKENS * D * COLS, bytes_accessed=12 * MB, transcendentals=0),
-    )(hidden, grad, after)
+        cost_estimate=pl.CostEstimate(flops=TOKENS * D * COLS, bytes_accessed=6 * MB, transcendentals=0),
+    )(hidden, grad, after, *([] if first is None else [first]))
 
 
 def add_four(a, b, c, d):
     return (a.astype(f32) + d.astype(f32)) + (b.astype(f32) + c.astype(f32))
 
 
-def add_kernel(a, b, out):
+def add_kernel(a, b, after, out, mark):
+    mark[...] = jnp.zeros_like(mark)
     out[...] = (a[...] + b[...].astype(f32)).astype(out.dtype)
 
 
-def add(a, b):
-    return call(add_kernel, shape(a.shape, bf16), [VMEM] * 2)(a, b)
+def add(a, b, after):
+    return call(add_kernel, (shape(a.shape, bf16), shape((8, 128), f32)), [VMEM] * 3)(a, b, after)
 
 
 def split_middle_kernel(*refs):
@@ -429,30 +460,23 @@
         tok[...] = total
         for r in range(16):
             at = half * HALF + r * 128
-            out[:, at:at + 128] = tok[pl.ds(r, 3, stride=16), :]
+            out[:, at:at + 128] = tok[pl.ds(r, 3, stride=16), :].astype(bf16)
 
 
 def finish(parts):
-    return call(finish_kernel, shape((3, D), f32), [VMEM], [pltpu.VMEM((48, 128), f32)])(parts)
+    return call(finish_kernel, shape((3, D), bf16), [VMEM], [pltpu.VMEM((48, 128), f32)])(parts)
 
 
 def local(hidden, head_weight, targets, image_mask, lengths, ref_logps, pairing):
     y, x, z, c = (lax.axis_index(a) for a in AXES)
     ids = jnp.stack([y, x, z, c, flat(y, x, z, c)]).astype(jnp.int32)
 
-    digits = jnp.stack([targets % 256, targets // 256 % 256, targets // 65536], axis=1)
-    meta = jnp.pad(digits.astype(f32).astype(bf16), ((0, 13), (0, 125)))
-    halves = hidden.reshape(3, 2, 16, 128)
-    first, second = (jnp.concatenate([halves[:, i].reshape(48, 128), meta], axis=0) for i in range(2))
-    parts = lax.all_to_all(
-        jnp.broadcast_to(jnp.stack([first, second])[None], (NZ, 2, 64, 128)).reshape(16, 64, 128),
-        ("z", "c"), 0, 0, tiled=True,
-    )
+    parts = lax.all_to_all(first_message(targets, hidden), ("z", "c"), 0, 0, tiled=True)
     block = join_window(ids, parts)
-    low, high = join_blocks(block, *(fetch(block, middle(o)) for o in OFF[1:]))
+    head, mark = load_head(head_weight)
+    low, high = join_blocks(block, *(fetch(block, middle(o)) for o in OFF[1:]), mark)
     other = [fetch(low, near), fetch(high, near)]
-    head, mark = load_head(head_weight)
-    low, high = gate(low, high, *other, mark)
+    low, high = gate(low, high, *other)
     ahead_low, back_high = fetch(low, final(1)), fetch(high, final(-1))
     ahead_high, back_low = fetch(high, final(1)), fetch(low, final(-1))
     far_low, far_high = fetch(ahead_low, final(1)), fetch(back_high, final(-1))
@@ -468,10 +492,11 @@
     received = [fetch(send, near)]
     received.append(fetch(grad_other_second(ids, logit_grad, head), near))
     *parts, mark = grad_own(ids, logit_grad, head, received, arrived(received[0]))
-    grad_head, mark = grad_head_of(rows, logit_grad, mark)
+    half, mark = grad_head_half(rows, logit_grad, mark)
     keep_low, keep_high, ahead_low, ahead_high, back_low, back_high, far_low, far_high = parts
-    ahead_low = add(ahead_low, fetch(far_low, final(-1)))
-    back_high = add(back_high, fetch(far_high, final(1)))
+    ahead_low, _ = add(ahead_low, fetch(far_low, final(-1)), mark)
+    back_high, mark = add(back_high, fetch(far_high, final(1)), mark)
+    grad_head, mark = grad_head_half(rows, logit_grad, mark, half)
     parts = split_middle(
         (keep_low, fetch(ahead_low, final(-1)), fetch(back_low, final(1))),
         (keep_high, fetch(ahead_high, final(-1)), fetch(back_high, final(1))),
@@ -479,7 +504,7 @@
     )
     parts = split_window(parts[0], *(fetch(parts[s], middle(-OFF[s])) for s in (1, 2, 3)))
     grad_hidden = finish(lax.all_to_all(parts, ("z", "c"), 0, 0, tiled=True))
-    return grad_hidden.astype(bf16), grad_head, loss[0, 0]
+    return grad_hidden, grad_head, loss[0, 0]
 
 
 def solution(mesh):

time: 156 us -> 156 us (level)
  Pallas kernels: 27.2 us -> 30.3 us
    pallas_call x6 -> x8, Pallas kernels: 8.36 us -> 11.7 us  [the longest x2 8.87 us: grad_head_half(): pl.pallas_call(head_kernel, grid=(steps,), in_specs=[pl.BlockSpec((TOKENS...]
    unnamed x10 -> x12, local copies, waits for them, and re-layouts: 3.37 us -> 3.9 us
  transfers between devices with their start and end apart: 30 -> 30, of which waited for: 15 -> 16; matrix products, arithmetic and copies ran while one was open for 0% -> 0% of each run, Pallas kernels for 7% -> 8%
where the time goes in v2:
time: 156 us
  starting transfers between devices  48.5 us (31%)
  waiting for transfers between devices  47.4 us (30%)
  Pallas kernels  30.3 us (19%)
  blocking collectives  24.2 us (16%)
  local copies, waits for them, and re-layouts  4.52 us (3%)
    ppermute x28, starting transfers between devices, fetch(): return lax.ppermute(value, AXES, pairs)  31.2 us
    ppermute x28, waiting for transfers between devices, fetch(): return lax.ppermute(value, AXES, pairs)  25.9 us
    all_to_all x1, blocking collectives, exchange(): lax.all_to_all(jnp.broadcast_to(value[None], (16,) + value.shape), axes,...  12.7 us
    all_to_all x1, waiting for transfers between devices, local(): lax.all_to_all(first_message(targets, hidden), ('z', 'c'), 0, 0, tiled=True)  11.6 us
    all_to_all x1, blocking collectives, local(): stats = lax.all_to_all(stats, ('y', 'x'), 0, 0, tiled=True)  11.6 us
    all_to_all x1, starting transfers between devices, local(): lax.all_to_all(first_message(targets, hidden), ('z', 'c'), 0, 0, tiled=True)  9.98 us
    all_to_all x1, waiting for transfers between devices, local(): grad_hidden = finish(lax.all_to_all(parts, ('z', 'c'), 0, 0, tiled=True))  9.87 us
    pallas_call x2, Pallas kernels, grad_head_half(): pl.pallas_call(head_kernel, grid=(steps,), in_specs=[pl.BlockSpec((TOKENS...  8.87 us
  transfers between devices with their start and end apart: 30, of which 16 were waited for; matrix products, arithmetic and copies ran while one was open for 0% of the time, Pallas kernels for 8%

profile of v2, /device:TPU:1, one launch (start us, length us, event | category | flops | bytes accessed | tf_op | source)
XLA Modules:
  0.0 155.7 jit_solution(12011205020026635783)
XLA Ops:
  3.3 10.0 %all-to-all-start = ((bf16[16,64,128]{2,1,0:T(8,128)(2,1)}), bf16[16,64,128]{2,1,0:T(8,128)(2,1)S(1)}, u32[]{:S(2)}, u32[]{:S(2)}) async-start(bf16[16,64,128]{2,1,0:T(8,128)(2,1)} %shard_map.85), calls=%async_computation | async-start | bytes 524288 | tf_op jit(solution)/shard_map/all_to_all | solution.py:474
  13.4 11.6 %all-to-all-done.parts = bf16[16,64,128]{2,1,0:T(8,128)(2,1)S(1)} async-done(((bf16[16,64,128]{2,1,0:T(8,128)(2,1)}), bf16[16,64,128]{2,1,0:T(8,128)(2,1)S(1)}, u32[]{:S(2)}, u32[]{:S(2)}) %all-to-all-start) | async-done | bytes 262176 | tf_op jit(solution)/shard_map/all_to_all | solution.py:474
  25.7 2.8 %collective-permute-start.2 = (bf16[48,2176]{1,0:T(8,128)(2,1)S(1)}, bf16[48,2176]{1,0:T(8,128)(2,1)S(1)}, u32[]{:S(2)}, u32[]{:S(2)}) collective-permute-start(bf16[48,2176]{1,0:T(8,128)(2,1)S(1)} %shard_map.86.a), channel_id=1, source_target_pairs={{128,0},{33,1},{130,2},{35,3},{132,4},{37,5},{134,6},{39,7},{136,8... | collective-permute-start | bytes 626696 | tf_op jit(solution)/shard_map/ppermute | solution.py:44
  28.9 2.4 %collective-permute-start = (bf16[48,2176]{1,0:T(8,128)(2,1)S(1)}, bf16[48,2176]{1,0:T(8,128)(2,1)S(1)}, u32[]{:S(2)}, u32[]{:S(2)}) collective-permute-start(bf16[48,2176]{1,0:T(8,128)(2,1)S(1)} %shard_map.86.a), channel_id=1, source_target_pairs={{64,0},{17,1},{66,2},{19,3},{68,4},{21,5},{70,6},{23,7},{72,8},{25... | collective-permute-start | bytes 626696 | tf_op jit(solution)/shard_map/ppermute | solution.py:44
  31.2 2.5 %copy-done = bf16[4096,640]{1,0:T(8,128)(2,1)S(1)} copy-done((bf16[4096,640]{1,0:T(8,128)(2,1)S(1)}, bf16[4096,640]{1,0:T(8,128)(2,1)}, u32[]{:S(2)}) %copy-start) | copy-done | bytes 5242904
  38.7 2.2 %collective-permute-start.5 = (bf16[2,48,2176]{2,1,0:T(8,128)(2,1)S(1)}, bf16[2,48,2176]{2,1,0:T(8,128)(2,1)S(1)}, u32[]{:S(2)}, u32[]{:S(2)}) collective-permute-start(bf16[2,48,2176]{2,1,0:T(8,128)(2,1)S(1)} %get-tuple-element.41.refs_0_), channel_id=1, source_target_pairs={{16,0},{65,1},{18,2},{67,3},{20,4},{69,5},{22,6},{71,7},{24,8},{73... | collective-permute-start | bytes 1253384 | tf_op jit(solution)/shard_map/ppermute | solution.py:44
  40.9 2.7 %collective-permute-start.6 = (bf16[2,48,2176]{2,1,0:T(8,128)(2,1)S(1)}, bf16[2,48,2176]{2,1,0:T(8,128)(2,1)S(1)}, u32[]{:S(2)}, u32[]{:S(2)}) collective-permute-start(bf16[2,48,2176]{2,1,0:T(8,128)(2,1)S(1)} %get-tuple-element.42.refs_1_), channel_id=1, source_target_pairs={{16,0},{65,1},{18,2},{67,3},{20,4},{69,5},{22,6},{71,7},{24,8},{73... | collective-permute-start | bytes 1253384 | tf_op jit(solution)/shard_map/ppermute | solution.py:44
  43.6 3.0 %collective-permute-done.7.refs_4_ = bf16[2,48,2176]{2,1,0:T(8,128)(2,1)S(1)} collective-permute-done((bf16[2,48,2176]{2,1,0:T(8,128)(2,1)S(1)}, bf16[2,48,2176]{2,1,0:T(8,128)(2,1)S(1)}, u32[]{:S(2)}, u32[]{:S(2)}) %collective-permute-start.7) | collective-permute-done | bytes 417824 | tf_op jit(solution)/shard_map/ppermute | solution.py:44
  47.5 3.0 %collective-permute-start.9 = (bf16[2,48,2176]{2,1,0:T(8,128)(2,1)S(1)}, bf16[2,48,2176]{2,1,0:T(8,128)(2,1)S(1)}, u32[]{:S(2)}, u32[]{:S(2)}) collective-permute-start(bf16[2,48,2176]{2,1,0:T(8,128)(2,1)S(1)} %collective-permute-done.5.refs_2_), channel_id=1, source_target_pairs={{16,0},{65,1},{18,2},{67,3},{20,4},{69,5},{22,6},{71,7},{24,8},{73... | collective-permute-start | bytes 1253384 | tf_op jit(solution)/shard_map/ppermute | solution.py:44
  52.8 2.7 %collective-permute-done.9.refs_6_ = bf16[2,48,2176]{2,1,0:T(8,128)(2,1)S(1)} collective-permute-done((bf16[2,48,2176]{2,1,0:T(8,128)(2,1)S(1)}, bf16[2,48,2176]{2,1,0:T(8,128)(2,1)S(1)}, u32[]{:S(2)}, u32[]{:S(2)}) %collective-permute-start.9) | collective-permute-done | bytes 417824 | tf_op jit(solution)/shard_map/ppermute | solution.py:44
  55.4 1.3 collective-permute-start.15
  56.7 2.7 %collective-permute-done.10.refs_7_ = bf16[2,48,2176]{2,1,0:T(8,128)(2,1)S(1)} collective-permute-done((bf16[2,48,2176]{2,1,0:T(8,128)(2,1)S(1)}, bf16[2,48,2176]{2,1,0:T(8,128)(2,1)S(1)}, u32[]{:S(2)}, u32[]{:S(2)}) %collective-permute-start.10) | collective-permute-done | bytes 417824 | tf_op jit(solution)/shard_map/ppermute | solution.py:44
  59.4 1.8 %collective-permute-start.16 = (bf16[2,48,2176]{2,1,0:T(8,128)(2,1)S(1)}, bf16[2,48,2176]{2,1,0:T(8,128)(2,1)S(1)}, u32[]{:S(2)}, u32[]{:S(2)}) collective-permute-start(bf16[2,48,2176]{2,1,0:T(8,128)(2,1)S(1)} %collective-permute-done.10.refs_7_), channel_id=1, source_target_pairs={{1,0},{0,1},{3,2},{2,3},{5,4},{4,5},{7,6},{6,7},{9,8},{8,9},{11,10... | collective-permute-start | bytes 1253384 | tf_op jit(solution)/shard_map/ppermute | solution.py:44
  61.2 1.4 collective-permute-done.16.refs_15_
  62.6 7.0 %shard_map.90 = (bf16[768,4096]{1,0:T(8,128)(2,1)S(1)}, f32[768,640]{1,0:T(8,128)S(1)}, f32[2,8,128]{2,1,0:T(8,128)S(1)}, f32[8,128]{1,0:T(8,128)S(1)}) custom-call(s32[5]{0:T(128)S(1)} %stack.23.ids, bf16[2,48,2176]{2,1,0:T(8,128)(2,1)S(1)} %get-tuple-element.41.refs_0_, bf16[2,48,2176]{2,1,0:T(8,128)(2,1)S(1)} %get-tuple-element.42.refs_1_, ...), custom_call_target="tpu_custom_call" | custom-call | flops 4026531840 | bytes 20971520 | tf_op jit(solution)/shard_map/pallas_call | solution.py:213
  69.6 12.7 %all_to_all.20.parts = f32[16,2,8,128]{3,2,1,0:T(8,128)S(1)} all-to-all(f32[16,2,8,128]{3,2,1,0:T(8,128)S(1)} %broadcast_in_dim.2), channel_id=1, replica_groups=mesh['y'=4,'x'=4,'z'=8,'c'=2] {'z','c'}, dimensions={0} | all-to-all | bytes 262144 | tf_op jit(solution)/shard_map/all_to_all | solution.py:233
  82.3 11.6 %all_to_all.21.parts = f32[16,2,8,128]{3,2,1,0:T(8,128)S(1)} all-to-all(f32[16,2,8,128]{3,2,1,0:T(8,128)S(1)} %shard_map.91), channel_id=1, replica_groups=mesh['y'=4,'x'=4,'z'=8,'c'=2] {'y','x'}, dimensions={0} | all-to-all | bytes 262144 | tf_op jit(solution)/shard_map/all_to_all | solution.py:488
  94.7 2.6 %shard_map.93 = (bf16[768,640]{1,0:T(8,128)(2,1)S(1)}, bf16[768,1024]{1,0:T(8,128)(2,1)S(1)}) custom-call(s32[5]{0:T(128)S(1)} %stack.23.ids, f32[768,640]{1,0:T(8,128)S(1)} %get-tuple-element.44.logits, f32[8,128]{1,0:T(8,128)S(1)} %get-tuple-element.46.norm, f32[8,128]{1,0:T(8,128)S(1)} %get-tuple-element.47.weight, ...), custom_call_target="tpu_custom_call" | custom-call | flops 1006632960 | bytes 6291456 | tf_op jit(solution)/shard_map/pallas_call | solution.py:324
  98.2 2.0 %shard_map.94 = bf16[768,1024]{1,0:T(8,128)(2,1)S(1)} custom-call(s32[5]{0:T(128)S(1)} %stack.23.ids, bf16[768,640]{1,0:T(8,128)(2,1)S(1)} %get-tuple-element.49.grad, bf16[4096,640]{1,0:T(8,128)(2,1)S(1)} %get-tuple-element.43.refs_16_.head), custom_call_target="tpu_custom_call" | custom-call | flops 2013265920 | bytes 16777216 | tf_op jit(solution)/shard_map/pallas_call | solution.py:335
  101.2 2.6 %collective-permute-done.18.other1 = bf16[768,1024]{1,0:T(8,128)(2,1)S(1)} collective-permute-done((bf16[768,1024]{1,0:T(8,128)(2,1)S(1)}, bf16[768,1024]{1,0:T(8,128)(2,1)S(1)}, u32[]{:S(2)}, u32[]{:S(2)}) %collective-permute-start.18) | collective-permute-done | bytes 1572896 | tf_op jit(solution)/shard_map/ppermute | solution.py:44
  103.9 4.1 %shard_map.96 = (f32[2,48,2048]{2,1,0:T(8,128)S(1)}, f32[2,48,2048]{2,1,0:T(8,128)S(1)}, f32[2,48,2048]{2,1,0:T(8,128)S(1)}, bf16[2,48,2048]{2,1,0:T(8,128)(2,1)...) custom-call(s32[5]{0:T(128)S(1)} %stack.23.ids, ...), custom_call_target="tpu_custom_call" | custom-call | tf_op jit(solution)/shard_map/pallas_call | solution.py:372
  109.5 1.8 %collective-permute-start.21 = (bf16[2,48,2048]{2,1,0:T(8,128)(2,1)S(1)}, bf16[2,48,2048]{2,1,0:T(8,128)(2,1)S(1)}, u32[]{:S(2)}, u32[]{:S(2)}) collective-permute-start(bf16[2,48,2048]{2,1,0:T(8,128)(2,1)S(1)} %get-tuple-element.58), channel_id=1, source_target_pairs={{16,0},{65,1},{18,2},{67,3},{20,4},{69,5},{22,6},{71,7},{24,8},{73... | collective-permute-start | bytes 1179656 | tf_op jit(solution)/shard_map/ppermute | solution.py:44
  111.3 4.4 %shard_map.97 = (bf16[4096,640]{1,0:T(8,128)(2,1)}, f32[8,128]{1,0:T(8,128)S(1)}) custom-call(bf16[768,4096]{1,0:T(8,128)(2,1)S(1)} %get-tuple-element.54.hidden, bf16[768,640]{1,0:T(8,128)(2,1)S(1)} %get-tuple-element.49.grad, f32[8,128]{1,0:T(8,128)S(1)} %get-tuple-element.55.refs_0_), custom_call_target="tpu_custom_call" | custom-call | flops 2013265920 | bytes 6291456 | tf_op jit(solution)/shard_map/pallas_call | solution.py:392
  115.8 2.8 %collective-permute-start.24 = (bf16[2,48,2048]{2,1,0:T(8,128)(2,1)S(1)}, bf16[2,48,2048]{2,1,0:T(8,128)(2,1)S(1)}, u32[]{:S(2)}, u32[]{:S(2)}) collective-permute-start(bf16[2,48,2048]{2,1,0:T(8,128)(2,1)S(1)} %get-tuple-element.63), channel_id=1, source_target_pairs={{16,0},{65,1},{18,2},{67,3},{20,4},{69,5},{22,6},{71,7},{24,8},{73... | collective-permute-start | bytes 1179656 | tf_op jit(solution)/shard_map/ppermute | solution.py:44
  119.2 4.4 %shard_map.100 = (bf16[4096,640]{1,0:T(8,128)(2,1)}, f32[8,128]{1,0:T(8,128)S(1)}) custom-call(bf16[768,4096]{1,0:T(8,128)(2,1)S(1)} %get-tuple-element.54.hidden, bf16[768,640]{1,0:T(8,128)(2,1)S(1)} %get-tuple-element.49.grad, f32[8,128]{1,0:T(8,128)S(1)} %get-tuple-element.64.refs_0_, ...), custom_call_target="tpu_custom_call", output_to_operand_aliasing={{0}: (3, {})} | custom-call | flops 2013265920 | bytes 6291456 | tf_op jit(solution)/shard_map/pallas_call | solution.py:392
  123.7 3.7 %collective-permute-done.20.refs_1_ = bf16[2,48,2048]{2,1,0:T(8,128)(2,1)S(1)} collective-permute-done((bf16[2,48,2048]{2,1,0:T(8,128)(2,1)S(1)}, bf16[2,48,2048]{2,1,0:T(8,128)(2,1)S(1)}, u32[]{:S(2)}, u32[]{:S(2)}) %collective-permute-start.20) | collective-permute-done | bytes 393248 | tf_op jit(solution)/shard_map/ppermute | solution.py:44
  127.7 2.7 %collective-permute-start.26 = (bf16[48,2048]{1,0:T(8,128)(2,1)S(1)}, bf16[48,2048]{1,0:T(8,128)(2,1)S(1)}, u32[]{:S(2)}, u32[]{:S(2)}) collective-permute-start(bf16[48,2048]{1,0:T(8,128)(2,1)S(1)} %get-tuple-element.69), channel_id=1, source_target_pairs={{64,0},{17,1},{66,2},{19,3},{68,4},{21,5},{70,6},{23,7},{72,8},{25... | collective-permute-start | bytes 589832 | tf_op jit(solution)/shard_map/ppermute | solution.py:44
  130.4 3.1 %collective-permute-done.25.b = bf16[48,2048]{1,0:T(8,128)(2,1)S(1)} collective-permute-done((bf16[48,2048]{1,0:T(8,128)(2,1)S(1)}, bf16[48,2048]{1,0:T(8,128)(2,1)S(1)}, u32[]{:S(2)}, u32[]{:S(2)}) %collective-permute-start.25) | collective-permute-done | bytes 196640 | tf_op jit(solution)/shard_map/ppermute | solution.py:44
  133.4 1.7 %collective-permute-done.26.c = bf16[48,2048]{1,0:T(8,128)(2,1)S(1)} collective-permute-done((bf16[48,2048]{1,0:T(8,128)(2,1)S(1)}, bf16[48,2048]{1,0:T(8,128)(2,1)S(1)}, u32[]{:S(2)}, u32[]{:S(2)}) %collective-permute-start.26) | collective-permute-done | bytes 196640 | tf_op jit(solution)/shard_map/ppermute | solution.py:44
  135.1 1.3 collective-permute-done.27.d
  137.3 7.4 %all-to-all-start.3 = ((bf16[16,48,128]{2,1,0:T(8,128)(2,1)}), bf16[16,48,128]{2,1,0:T(8,128)(2,1)S(1)}, u32[]{:S(2)}, u32[]{:S(2)}) async-start(bf16[16,48,128]{2,1,0:T(8,128)(2,1)} %shard_map.102), calls=%async_computation.3 | async-start | bytes 393216 | tf_op jit(solution)/shard_map/all_to_all | solution.py:506
  145.2 9.9 %all-to-all-done.3.parts = bf16[16,48,128]{2,1,0:T(8,128)(2,1)S(1)} async-done(((bf16[16,48,128]{2,1,0:T(8,128)(2,1)}), bf16[16,48,128]{2,1,0:T(8,128)(2,1)S(1)}, u32[]{:S(2)}, u32[]{:S(2)}) %all-to-all-start.3) | async-done | bytes 196640 | tf_op jit(solution)/shard_map/all_to_all | solution.py:506
  (64 shorter events, 19.5 us)
Async XLA Ops:
  3.3 21.7 %all-to-all-start = ((bf16[16,64,128]{2,1,0:T(8,128)(2,1)}), bf16[16,64,128]{2,1,0:T(8,128)(2,1)S(1)}, u32[]{:S(2)}, u32[]{:S(2)}) async-start(bf16[16,64,128]{2,1,0:T(8,128)(2,1)} %shard_map.85), calls=%async_computation | async-start | bytes 524288 | tf_op jit(solution)/shard_map/all_to_all | solution.py:474
  25.7 8.4 %collective-permute-start.2 = (bf16[48,2176]{1,0:T(8,128)(2,1)S(1)}, bf16[48,2176]{1,0:T(8,128)(2,1)S(1)}, u32[]{:S(2)}, u32[]{:S(2)}) collective-permute-start(bf16[48,2176]{1,0:T(8,128)(2,1)S(1)} %shard_map.86.a), channel_id=1, source_target_pairs={{128,0},{33,1},{130,2},{35,3},{132,4},{37,5},{134,6},{39,7},{136,8... | collective-permute-start | bytes 626696 | tf_op jit(solution)/shard_map/ppermute | solution.py:44
  28.6 6.2 %collective-permute-start.1 = (bf16[48,2176]{1,0:T(8,128)(2,1)S(1)}, bf16[48,2176]{1,0:T(8,128)(2,1)S(1)}, u32[]{:S(2)}, u32[]{:S(2)}) collective-permute-start(bf16[48,2176]{1,0:T(8,128)(2,1)S(1)} %shard_map.86.a), channel_id=1, source_target_pairs={{192,0},{49,1},{194,2},{51,3},{196,4},{53,5},{198,6},{55,7},{200,8... | collective-permute-start | bytes 626696 | tf_op jit(solution)/shard_map/ppermute | solution.py:44
  28.9 5.8 %collective-permute-start = (bf16[48,2176]{1,0:T(8,128)(2,1)S(1)}, bf16[48,2176]{1,0:T(8,128)(2,1)S(1)}, u32[]{:S(2)}, u32[]{:S(2)}) collective-permute-start(bf16[48,2176]{1,0:T(8,128)(2,1)S(1)} %shard_map.86.a), channel_id=1, source_target_pairs={{64,0},{17,1},{66,2},{19,3},{68,4},{21,5},{70,6},{23,7},{72,8},{25... | collective-permute-start | bytes 626696 | tf_op jit(solution)/shard_map/ppermute | solution.py:44
  34.8 2.3 %collective-permute-start.3 = (bf16[2,48,2176]{2,1,0:T(8,128)(2,1)S(1)}, bf16[2,48,2176]{2,1,0:T(8,128)(2,1)S(1)}, u32[]{:S(2)}, u32[]{:S(2)}) collective-permute-start(bf16[2,48,2176]{2,1,0:T(8,128)(2,1)S(1)} %get-tuple-element.39.low), channel_id=1, source_target_pairs={{1,0},{0,1},{3,2},{2,3},{5,4},{4,5},{7,6},{6,7},{9,8},{8,9},{11,10... | collective-permute-start | bytes 1253384 | tf_op jit(solution)/shard_map/ppermute | solution.py:44
  35.7 2.0 %collective-permute-start.4 = (bf16[2,48,2176]{2,1,0:T(8,128)(2,1)S(1)}, bf16[2,48,2176]{2,1,0:T(8,128)(2,1)S(1)}, u32[]{:S(2)}, u32[]{:S(2)}) collective-permute-start(bf16[2,48,2176]{2,1,0:T(8,128)(2,1)S(1)} %get-tuple-element.40.high), channel_id=1, source_target_pairs={{1,0},{0,1},{3,2},{2,3},{5,4},{4,5},{7,6},{6,7},{9,8},{8,9},{11,10... | collective-permute-start | bytes 1253384 | tf_op jit(solution)/shard_map/ppermute | solution.py:44
  37.8 8.8 %collective-permute-start.7 = (bf16[2,48,2176]{2,1,0:T(8,128)(2,1)S(1)}, bf16[2,48,2176]{2,1,0:T(8,128)(2,1)S(1)}, u32[]{:S(2)}, u32[]{:S(2)}) collective-permute-start(bf16[2,48,2176]{2,1,0:T(8,128)(2,1)S(1)} %get-tuple-element.41.refs_0_), channel_id=1, source_target_pairs={{48,0},{193,1},{50,2},{195,3},{52,4},{197,5},{54,6},{199,7},{56,8}... | collective-permute-start | bytes 1253384 | tf_op jit(solution)/shard_map/ppermute | solution.py:44
  38.7 8.8 %collective-permute-start.5 = (bf16[2,48,2176]{2,1,0:T(8,128)(2,1)S(1)}, bf16[2,48,2176]{2,1,0:T(8,128)(2,1)S(1)}, u32[]{:S(2)}, u32[]{:S(2)}) collective-permute-start(bf16[2,48,2176]{2,1,0:T(8,128)(2,1)S(1)} %get-tuple-element.41.refs_0_), channel_id=1, source_target_pairs={{16,0},{65,1},{18,2},{67,3},{20,4},{69,5},{22,6},{71,7},{24,8},{73... | collective-permute-start | bytes 1253384 | tf_op jit(solution)/shard_map/ppermute | solution.py:44
  40.9 10.1 %collective-permute-start.8 = (bf16[2,48,2176]{2,1,0:T(8,128)(2,1)S(1)}, bf16[2,48,2176]{2,1,0:T(8,128)(2,1)S(1)}, u32[]{:S(2)}, u32[]{:S(2)}) collective-permute-start(bf16[2,48,2176]{2,1,0:T(8,128)(2,1)S(1)} %get-tuple-element.42.refs_1_), channel_id=1, source_target_pairs={{48,0},{193,1},{50,2},{195,3},{52,4},{197,5},{54,6},{199,7},{56,8}... | collective-permute-start | bytes 1253384 | tf_op jit(solution)/shard_map/ppermute | solution.py:44
  40.9 11.3 %collective-permute-start.6 = (bf16[2,48,2176]{2,1,0:T(8,128)(2,1)S(1)}, bf16[2,48,2176]{2,1,0:T(8,128)(2,1)S(1)}, u32[]{:S(2)}, u32[]{:S(2)}) collective-permute-start(bf16[2,48,2176]{2,1,0:T(8,128)(2,1)S(1)} %get-tuple-element.42.refs_1_), channel_id=1, source_target_pairs={{16,0},{65,1},{18,2},{67,3},{20,4},{69,5},{22,6},{71,7},{24,8},{73... | collective-permute-start | bytes 1253384 | tf_op jit(solution)/shard_map/ppermute | solution.py:44
  46.5 5.7 %collective-permute-start.13 = (bf16[2,48,2176]{2,1,0:T(8,128)(2,1)S(1)}, bf16[2,48,2176]{2,1,0:T(8,128)(2,1)S(1)}, u32[]{:S(2)}, u32[]{:S(2)}) collective-permute-start(bf16[2,48,2176]{2,1,0:T(8,128)(2,1)S(1)} %collective-permute-done.7.refs_4_), channel_id=1, source_target_pairs={{1,0},{0,1},{3,2},{2,3},{5,4},{4,5},{7,6},{6,7},{9,8},{8,9},{11,10... | collective-permute-start | bytes 1253384 | tf_op jit(solution)/shard_map/ppermute | solution.py:44
  47.5 7.9 %collective-permute-start.9 = (bf16[2,48,2176]{2,1,0:T(8,128)(2,1)S(1)}, bf16[2,48,2176]{2,1,0:T(8,128)(2,1)S(1)}, u32[]{:S(2)}, u32[]{:S(2)}) collective-permute-start(bf16[2,48,2176]{2,1,0:T(8,128)(2,1)S(1)} %collective-permute-done.5.refs_2_), channel_id=1, source_target_pairs={{16,0},{65,1},{18,2},{67,3},{20,4},{69,5},{22,6},{71,7},{24,8},{73... | collective-permute-start | bytes 1253384 | tf_op jit(solution)/shard_map/ppermute | solution.py:44
  51.0 8.4 %collective-permute-start.10 = (bf16[2,48,2176]{2,1,0:T(8,128)(2,1)S(1)}, bf16[2,48,2176]{2,1,0:T(8,128)(2,1)S(1)}, u32[]{:S(2)}, u32[]{:S(2)}) collective-permute-start(bf16[2,48,2176]{2,1,0:T(8,128)(2,1)S(1)} %collective-permute-done.8.refs_5_), channel_id=1, source_target_pairs={{48,0},{193,1},{50,2},{195,3},{52,4},{197,5},{54,6},{199,7},{56,8}... | collective-permute-start | bytes 1253384 | tf_op jit(solution)/shard_map/ppermute | solution.py:44
  51.0 10.2 %collective-permute-start.11 = (bf16[2,48,2176]{2,1,0:T(8,128)(2,1)S(1)}, bf16[2,48,2176]{2,1,0:T(8,128)(2,1)S(1)}, u32[]{:S(2)}, u32[]{:S(2)}) collective-permute-start(bf16[2,48,2176]{2,1,0:T(8,128)(2,1)S(1)} %collective-permute-done.5.refs_2_), channel_id=1, source_target_pairs={{1,0},{0,1},{3,2},{2,3},{5,4},{4,5},{7,6},{6,7},{9,8},{8,9},{11,10... | collective-permute-start | bytes 1253384 | tf_op jit(solution)/shard_map/ppermute | solution.py:44
  52.3 9.0 %collective-permute-start.14 = (bf16[2,48,2176]{2,1,0:T(8,128)(2,1)S(1)}, bf16[2,48,2176]{2,1,0:T(8,128)(2,1)S(1)}, u32[]{:S(2)}, u32[]{:S(2)}) collective-permute-start(bf16[2,48,2176]{2,1,0:T(8,128)(2,1)S(1)} %collective-permute-done.8.refs_5_), channel_id=1, source_target_pairs={{1,0},{0,1},{3,2},{2,3},{5,4},{4,5},{7,6},{6,7},{9,8},{8,9},{11,10... | collective-permute-start | bytes 1253384 | tf_op jit(solution)/shard_map/ppermute | solution.py:44
  52.3 9.0 %collective-permute-start.12 = (bf16[2,48,2176]{2,1,0:T(8,128)(2,1)S(1)}, bf16[2,48,2176]{2,1,0:T(8,128)(2,1)S(1)}, u32[]{:S(2)}, u32[]{:S(2)}) collective-permute-start(bf16[2,48,2176]{2,1,0:T(8,128)(2,1)S(1)} %collective-permute-done.6.refs_3_), channel_id=1, source_target_pairs={{1,0},{0,1},{3,2},{2,3},{5,4},{4,5},{7,6},{6,7},{9,8},{8,9},{11,10... | collective-permute-start | bytes 1253384 | tf_op jit(solution)/shard_map/ppermute | solution.py:44
  55.4 5.8 %collective-permute-start.15 = (bf16[2,48,2176]{2,1,0:T(8,128)(2,1)S(1)}, bf16[2,48,2176]{2,1,0:T(8,128)(2,1)S(1)}, u32[]{:S(2)}, u32[]{:S(2)}) collective-permute-start(bf16[2,48,2176]{2,1,0:T(8,128)(2,1)S(1)} %collective-permute-done.9.refs_6_), channel_id=1, source_target_pairs={{1,0},{0,1},{3,2},{2,3},{5,4},{4,5},{7,6},{6,7},{9,8},{8,9},{11,10... | collective-permute-start | bytes 1253384 | tf_op jit(solution)/shard_map/ppermute | solution.py:44
  59.4 3.2 %collective-permute-start.16 = (bf16[2,48,2176]{2,1,0:T(8,128)(2,1)S(1)}, bf16[2,48,2176]{2,1,0:T(8,128)(2,1)S(1)}, u32[]{:S(2)}, u32[]{:S(2)}) collective-permute-start(bf16[2,48,2176]{2,1,0:T(8,128)(2,1)S(1)} %collective-permute-done.10.refs_7_), channel_id=1, source_target_pairs={{1,0},{0,1},{3,2},{2,3},{5,4},{4,5},{7,6},{6,7},{9,8},{8,9},{11,10... | collective-permute-start | bytes 1253384 | tf_op jit(solution)/shard_map/ppermute | solution.py:44
  62.6 31.3 %copy-start.4 = (f32[16]{0:T(128)S(1)}, f32[16]{0:T(128)}, u32[]{:S(2)}) copy-start(f32[16]{0:T(128)} %ref_logps.1) | copy-start | bytes 196
  62.6 31.3 %copy-start.5 = (s32[16]{0:T(128)S(1)}, s32[16]{0:T(128)}, u32[]{:S(2)}) copy-start(s32[16]{0:T(128)} %pairing.1) | copy-start | bytes 196
  97.3 4.0 %collective-permute-start.17 = (bf16[768,1024]{1,0:T(8,128)(2,1)S(1)}, bf16[768,1024]{1,0:T(8,128)(2,1)S(1)}, u32[]{:S(2)}, u32[]{:S(2)}) collective-permute-start(bf16[768,1024]{1,0:T(8,128)(2,1)S(1)} %get-tuple-element.50), channel_id=1, source_target_pairs={{1,0},{0,1},{3,2},{2,3},{5,4},{4,5},{7,6},{6,7},{9,8},{8,9},{11,10... | collective-permute-start | bytes 4718600 | tf_op jit(solution)/shard_map/ppermute | solution.py:44
  100.2 3.7 %collective-permute-start.18 = (bf16[768,1024]{1,0:T(8,128)(2,1)S(1)}, bf16[768,1024]{1,0:T(8,128)(2,1)S(1)}, u32[]{:S(2)}, u32[]{:S(2)}) collective-permute-start(bf16[768,1024]{1,0:T(8,128)(2,1)S(1)} %shard_map.94), channel_id=1, source_target_pairs={{1,0},{0,1},{3,2},{2,3},{5,4},{4,5},{7,6},{6,7},{9,8},{8,9},{11,10... | collective-permute-start | bytes 4718600 | tf_op jit(solution)/shard_map/ppermute | solution.py:44
  108.0 7.8 %collective-permute-start.23 = (bf16[2,48,2048]{2,1,0:T(8,128)(2,1)S(1)}, bf16[2,48,2048]{2,1,0:T(8,128)(2,1)S(1)}, u32[]{:S(2)}, u32[]{:S(2)}) collective-permute-start(bf16[2,48,2048]{2,1,0:T(8,128)(2,1)S(1)} %get-tuple-element.62), channel_id=1, source_target_pairs={{16,0},{65,1},{18,2},{67,3},{20,4},{69,5},{22,6},{71,7},{24,8},{73... | collective-permute-start | bytes 1179656 | tf_op jit(solution)/shard_map/ppermute | solution.py:44
  108.6 9.9 %collective-permute-start.19 = (bf16[2,48,2048]{2,1,0:T(8,128)(2,1)S(1)}, bf16[2,48,2048]{2,1,0:T(8,128)(2,1)S(1)}, u32[]{:S(2)}, u32[]{:S(2)}) collective-permute-start(bf16[2,48,2048]{2,1,0:T(8,128)(2,1)S(1)} %get-tuple-element.53), channel_id=1, source_target_pairs={{48,0},{193,1},{50,2},{195,3},{52,4},{197,5},{54,6},{199,7},{56,8}... | collective-permute-start | bytes 1179656 | tf_op jit(solution)/shard_map/ppermute | solution.py:44
  109.5 14.1 %collective-permute-start.21 = (bf16[2,48,2048]{2,1,0:T(8,128)(2,1)S(1)}, bf16[2,48,2048]{2,1,0:T(8,128)(2,1)S(1)}, u32[]{:S(2)}, u32[]{:S(2)}) collective-permute-start(bf16[2,48,2048]{2,1,0:T(8,128)(2,1)S(1)} %get-tuple-element.58), channel_id=1, source_target_pairs={{16,0},{65,1},{18,2},{67,3},{20,4},{69,5},{22,6},{71,7},{24,8},{73... | collective-permute-start | bytes 1179656 | tf_op jit(solution)/shard_map/ppermute | solution.py:44
  111.3 12.4 %collective-permute-start.22 = (bf16[2,48,2048]{2,1,0:T(8,128)(2,1)S(1)}, bf16[2,48,2048]{2,1,0:T(8,128)(2,1)S(1)}, u32[]{:S(2)}, u32[]{:S(2)}) collective-permute-start(bf16[2,48,2048]{2,1,0:T(8,128)(2,1)S(1)} %get-tuple-element.60), channel_id=1, source_target_pairs={{48,0},{193,1},{50,2},{195,3},{52,4},{197,5},{54,6},{199,7},{56,8}... | collective-permute-start | bytes 1179656 | tf_op jit(solution)/shard_map/ppermute | solution.py:44
  115.8 7.9 %collective-permute-start.24 = (bf16[2,48,2048]{2,1,0:T(8,128)(2,1)S(1)}, bf16[2,48,2048]{2,1,0:T(8,128)(2,1)S(1)}, u32[]{:S(2)}, u32[]{:S(2)}) collective-permute-start(bf16[2,48,2048]{2,1,0:T(8,128)(2,1)S(1)} %get-tuple-element.63), channel_id=1, source_target_pairs={{16,0},{65,1},{18,2},{67,3},{20,4},{69,5},{22,6},{71,7},{24,8},{73... | collective-permute-start | bytes 1179656 | tf_op jit(solution)/shard_map/ppermute | solution.py:44
  119.2 8.1 %collective-permute-start.20 = (bf16[2,48,2048]{2,1,0:T(8,128)(2,1)S(1)}, bf16[2,48,2048]{2,1,0:T(8,128)(2,1)S(1)}, u32[]{:S(2)}, u32[]{:S(2)}) collective-permute-start(bf16[2,48,2048]{2,1,0:T(8,128)(2,1)S(1)} %get-tuple-element.57), channel_id=1, source_target_pairs={{48,0},{193,1},{50,2},{195,3},{52,4},{197,5},{54,6},{199,7},{56,8}... | collective-permute-start | bytes 1179656 | tf_op jit(solution)/shard_map/ppermute | solution.py:44
  127.6 5.8 %collective-permute-start.25 = (bf16[48,2048]{1,0:T(8,128)(2,1)S(1)}, bf16[48,2048]{1,0:T(8,128)(2,1)S(1)}, u32[]{:S(2)}, u32[]{:S(2)}) collective-permute-start(bf16[48,2048]{1,0:T(8,128)(2,1)S(1)} %get-tuple-element.68), channel_id=1, source_target_pairs={{192,0},{49,1},{194,2},{51,3},{196,4},{53,5},{198,6},{55,7},{200,8... | collective-permute-start | bytes 589832 | tf_op jit(solution)/shard_map/ppermute | solution.py:44
  127.7 7.4 %collective-permute-start.26 = (bf16[48,2048]{1,0:T(8,128)(2,1)S(1)}, bf16[48,2048]{1,0:T(8,128)(2,1)S(1)}, u32[]{:S(2)}, u32[]{:S(2)}) collective-permute-start(bf16[48,2048]{1,0:T(8,128)(2,1)S(1)} %get-tuple-element.69), channel_id=1, source_target_pairs={{64,0},{17,1},{66,2},{19,3},{68,4},{21,5},{70,6},{23,7},{72,8},{25... | collective-permute-start | bytes 589832 | tf_op jit(solution)/shard_map/ppermute | solution.py:44
  130.4 6.0 %collective-permute-start.27 = (bf16[48,2048]{1,0:T(8,128)(2,1)S(1)}, bf16[48,2048]{1,0:T(8,128)(2,1)S(1)}, u32[]{:S(2)}, u32[]{:S(2)}) collective-permute-start(bf16[48,2048]{1,0:T(8,128)(2,1)S(1)} %get-tuple-element.70), channel_id=1, source_target_pairs={{128,0},{33,1},{130,2},{35,3},{132,4},{37,5},{134,6},{39,7},{136,8... | collective-permute-start | bytes 589832 | tf_op jit(solution)/shard_map/ppermute | solution.py:44
  137.3 17.8 %all-to-all-start.3 = ((bf16[16,48,128]{2,1,0:T(8,128)(2,1)}), bf16[16,48,128]{2,1,0:T(8,128)(2,1)S(1)}, u32[]{:S(2)}, u32[]{:S(2)}) async-start(bf16[16,48,128]{2,1,0:T(8,128)(2,1)} %shard_map.102), calls=%async_computation.3 | async-start | bytes 393216 | tf_op jit(solution)/shard_map/all_to_all | solution.py:506
  (4 other events, 35.2 us)

commit v3 on v2

--- a/solution.py
+++ b/solution.py
@@ -350,32 +350,44 @@
     return call(arrived_kernel, shape((8, 128), f32), [VMEM], vmem=4)(value)
 
 
-def grad_own_kernel(ids, grad, head, other0, other1, after, *refs):
-    parts, mark, total = refs[:8], refs[8], refs[9]
+def grad_own_kernel(ids, grad, head, out):
+    for i in range(HALF // STEP):
+        out[:, i * STEP:(i + 1) * STEP] = times_head(grad[...], head[head_rows(ids[3], i * STEP), :])
+
+
+def grad_own(ids, grad, head):
+    return call(
+        grad_own_kernel,
+        shape((TOKENS, HALF), f32),
+        [SMEM, VMEM, VMEM],
+        vmem=16,
+        flops=TOKENS * HALF * COLS * 2,
+        bytes_accessed=10 * MB,
+    )(ids, grad, head)
+
+
+PART_TYPES = (f32, f32, f32, bf16, bf16, f32, bf16, bf16)
+
+
+def split_final_kernel(first, ids, own, other0, other1, after, *refs):
+    parts, mark = refs[:-1], refs[-1]
     mark[...] = jnp.zeros_like(mark)
-    for i in range(HALF // STEP):
-        at = slice(i * STEP, (i + 1) * STEP)
-        other = (other0, other1)[i * STEP // PIECE]
-        inner = i * STEP % PIECE
-        total[...] = times_head(grad[...], head[head_rows(ids[3], i * STEP), :])
-        total[...] += other[:, inner:inner + STEP].astype(f32)
-        for n, r in enumerate(parts):
-            for inner in range(2):
-                row = pl.multiple_of(window(ids, ids[3], n // 2, n % 2 * 2 + inner) * WIN, 16)
-                r[inner, :, at] = total[pl.ds(row, WIN), :].astype(r.dtype)
-
-
-PART_TYPES = (f32, f32, f32, bf16, bf16, f32, bf16, bf16)
-
-
-def grad_own(ids, grad, head, other, after):
-    return call(
-        grad_own_kernel,
-        [shape((2, WIN, HALF), t) for t in PART_TYPES] + [shape((8, 128), f32)],
-        [SMEM] + [VMEM] * 5,
-        [pltpu.VMEM((TOKENS, STEP), f32)],
-        vmem=22,
-    )(ids, grad, head, *other, after)
+    for n, r in enumerate(parts, first):
+        for inner in range(2):
+            row = pl.multiple_of(window(ids, ids[3], n // 2, n % 2 * 2 + inner) * WIN, 16)
+            for h, other in enumerate((other0, other1)):
+                at = slice(h * PIECE, (h + 1) * PIECE)
+                total = own[pl.ds(row, WIN), at] + other[pl.ds(row, WIN), :].astype(f32)
+                r[inner, :, at] = total.astype(r.dtype)
+
+
+def split_final(ids, own, other, after, first, last):
+    return call(
+        functools.partial(split_final_kernel, first),
+        [shape((2, WIN, HALF), t) for t in PART_TYPES[first:last]] + [shape((8, 128), f32)],
+        [SMEM] + [VMEM] * 4,
+        vmem=18,
+    )(ids, own, *other, after)
 
 
 def head_kernel(hidden, grad, *refs):
@@ -478,7 +490,8 @@
     other = [fetch(low, near), fetch(high, near)]
     low, high = gate(low, high, *other)
     ahead_low, back_high = fetch(low, final(1)), fetch(high, final(-1))
-    ahead_high, back_low = fetch(high, final(1)), fetch(low, final(-1))
+    late_low, late_high = gate(low, high, ahead_low, back_high)
+    ahead_high, back_low = fetch(late_high, final(1)), fetch(late_low, final(-1))
     far_low, far_high = fetch(ahead_low, final(1)), fetch(back_high, final(-1))
     own = [low, high, ahead_low, ahead_high, back_low, back_high, far_low, far_high]
     other += [fetch(v, near) for v in own[2:]]
@@ -491,9 +504,11 @@
     logit_grad, send = grad_other_first(ids, logits, log_norm, weight, target, head)
     received = [fetch(send, near)]
     received.append(fetch(grad_other_second(ids, logit_grad, head), near))
-    *parts, mark = grad_own(ids, logit_grad, head, received, arrived(received[0]))
+    own = grad_own(ids, logit_grad, head)
+    far_low, far_high, mark = split_final(ids, own, received, arrived(received[0]), 6, 8)
     half, mark = grad_head_half(rows, logit_grad, mark)
-    keep_low, keep_high, ahead_low, ahead_high, back_low, back_high, far_low, far_high = parts
+    *parts, mark = split_final(ids, own, received, mark, 0, 6)
+    keep_low, keep_high, ahead_low, ahead_high, back_low, back_high = parts
     ahead_low, _ = add(ahead_low, fetch(far_low, final(-1)), mark)
     back_high, mark = add(back_high, fetch(far_high, final(1)), mark)
     grad_head, mark = grad_head_half(rows, logit_grad, mark, half)

time: 156 us -> 157 us (level)
    ppermute x28, starting transfers between devices: 31.2 us -> 32.8 us  [fetch(): return lax.ppermute(value, AXES, pairs)]
    pallas_call x1 -> x3, Pallas kernels: 4.11 us -> 4.8 us  [the longest x1 3.18 us: grad_own(): call(grad_own_kernel, shape((TOKENS, HALF), f32), [SMEM, VMEM, VMEM], vme...]
  transfers between devices with their start and end apart: 30 -> 30, of which waited for: 16 -> 17; matrix products, arithmetic and copies ran while one was open for 0% -> 0% of each run, Pallas kernels for 8% -> 10%
where the time goes in v3:
time: 157 us; the launch traced here: 156 us
  starting transfers between devices  49.8 us (32%)
  waiting for transfers between devices  46 us (29%)
  Pallas kernels  31.1 us (20%)
  blocking collectives  24.2 us (15%)
  local copies, waits for them, and re-layouts  4.52 us (3%)
    ppermute x28, starting transfers between devices, fetch(): return lax.ppermute(value, AXES, pairs)  32.8 us
    ppermute x28, waiting for transfers between devices, fetch(): return lax.ppermute(value, AXES, pairs)  24.5 us
    all_to_all x1, blocking collectives, exchange(): lax.all_to_all(jnp.broadcast_to(value[None], (16,) + value.shape), axes,...  12.7 us
    all_to_all x1, waiting for transfers between devices, local(): lax.all_to_all(first_message(targets, hidden), ('z', 'c'), 0, 0, tiled=True)  11.6 us
    all_to_all x1, blocking collectives, local(): stats = lax.all_to_all(stats, ('y', 'x'), 0, 0, tiled=True)  11.5 us
    all_to_all x1, starting transfers between devices, local(): lax.all_to_all(first_message(targets, hidden), ('z', 'c'), 0, 0, tiled=True)  9.98 us
    all_to_all x1, waiting for transfers between devices, local(): grad_hidden = finish(lax.all_to_all(parts, ('z', 'c'), 0, 0, tiled=True))  9.87 us
    pallas_call x2, Pallas kernels, grad_head_half(): pl.pallas_call(head_kernel, grid=(steps,), in_specs=[pl.BlockSpec((TOKENS...  8.87 us
  transfers between devices with their start and end apart: 30, of which 17 were waited for; matrix products, arithmetic and copies ran while one was open for 0% of the time, Pallas kernels for 10%

profile of v3, /device:TPU:1, one launch (start us, length us, event | category | flops | bytes accessed | tf_op | source)
XLA Modules:
  0.0 156.5 jit_solution(16717213707988787513)
XLA Ops:
  3.3 10.0 %all-to-all-start = ((bf16[16,64,128]{2,1,0:T(8,128)(2,1)}), bf16[16,64,128]{2,1,0:T(8,128)(2,1)S(1)}, u32[]{:S(2)}, u32[]{:S(2)}) async-start(bf16[16,64,128]{2,1,0:T(8,128)(2,1)} %shard_map.85), calls=%async_computation | async-start | bytes 524288 | tf_op jit(solution)/shard_map/all_to_all | solution.py:486
  13.4 11.6 %all-to-all-done.parts = bf16[16,64,128]{2,1,0:T(8,128)(2,1)S(1)} async-done(((bf16[16,64,128]{2,1,0:T(8,128)(2,1)}), bf16[16,64,128]{2,1,0:T(8,128)(2,1)S(1)}, u32[]{:S(2)}, u32[]{:S(2)}) %all-to-all-start) | async-done | bytes 262176 | tf_op jit(solution)/shard_map/all_to_all | solution.py:486
  25.7 2.8 %collective-permute-start.2 = (bf16[48,2176]{1,0:T(8,128)(2,1)S(1)}, bf16[48,2176]{1,0:T(8,128)(2,1)S(1)}, u32[]{:S(2)}, u32[]{:S(2)}) collective-permute-start(bf16[48,2176]{1,0:T(8,128)(2,1)S(1)} %shard_map.86.a), channel_id=1, source_target_pairs={{128,0},{33,1},{130,2},{35,3},{132,4},{37,5},{134,6},{39,7},{136,8... | collective-permute-start | bytes 626696 | tf_op jit(solution)/shard_map/ppermute | solution.py:44
  28.9 2.4 %collective-permute-start = (bf16[48,2176]{1,0:T(8,128)(2,1)S(1)}, bf16[48,2176]{1,0:T(8,128)(2,1)S(1)}, u32[]{:S(2)}, u32[]{:S(2)}) collective-permute-start(bf16[48,2176]{1,0:T(8,128)(2,1)S(1)} %shard_map.86.a), channel_id=1, source_target_pairs={{64,0},{17,1},{66,2},{19,3},{68,4},{21,5},{70,6},{23,7},{72,8},{25... | collective-permute-start | bytes 626696 | tf_op jit(solution)/shard_map/ppermute | solution.py:44
  31.2 2.5 %copy-done = bf16[4096,640]{1,0:T(8,128)(2,1)S(1)} copy-done((bf16[4096,640]{1,0:T(8,128)(2,1)S(1)}, bf16[4096,640]{1,0:T(8,128)(2,1)}, u32[]{:S(2)}) %copy-start) | copy-done | bytes 5242904
  37.8 3.0 %collective-permute-start.5 = (bf16[2,48,2176]{2,1,0:T(8,128)(2,1)S(1)}, bf16[2,48,2176]{2,1,0:T(8,128)(2,1)S(1)}, u32[]{:S(2)}, u32[]{:S(2)}) collective-permute-start(bf16[2,48,2176]{2,1,0:T(8,128)(2,1)S(1)} %get-tuple-element.44.low.refs_0_), channel_id=1, source_target_pairs={{16,0},{65,1},{18,2},{67,3},{20,4},{69,5},{22,6},{71,7},{24,8},{73... | collective-permute-start | bytes 1253384 | tf_op jit(solution)/shard_map/ppermute | solution.py:44
  40.8 5.0 %collective-permute-done.5.first.refs_2_ = bf16[2,48,2176]{2,1,0:T(8,128)(2,1)S(1)} collective-permute-done((bf16[2,48,2176]{2,1,0:T(8,128)(2,1)S(1)}, bf16[2,48,2176]{2,1,0:T(8,128)(2,1)S(1)}, u32[]{:S(2)}, u32[]{:S(2)}) %collective-permute-start.5) | collective-permute-done | bytes 417824 | tf_op jit(solution)/shard_map/ppermute | solution.py:44
  46.6 3.0 %collective-permute-start.9 = (bf16[2,48,2176]{2,1,0:T(8,128)(2,1)S(1)}, bf16[2,48,2176]{2,1,0:T(8,128)(2,1)S(1)}, u32[]{:S(2)}, u32[]{:S(2)}) collective-permute-start(bf16[2,48,2176]{2,1,0:T(8,128)(2,1)S(1)} %collective-permute-done.5.first.refs_2_), channel_id=1, source_target_pairs={{16,0},{65,1},{18,2},{67,3},{20,4},{69,5},{22,6},{71,7},{24,8},{73... | collective-permute-start | bytes 1253384 | tf_op jit(solution)/shard_map/ppermute | solution.py:44
  49.6 2.8 %collective-permute-start.7 = (bf16[2,48,2176]{2,1,0:T(8,128)(2,1)S(1)}, bf16[2,48,2176]{2,1,0:T(8,128)(2,1)S(1)}, u32[]{:S(2)}, u32[]{:S(2)}) collective-permute-start(bf16[2,48,2176]{2,1,0:T(8,128)(2,1)S(1)} %get-tuple-element.46), channel_id=1, source_target_pairs={{16,0},{65,1},{18,2},{67,3},{20,4},{69,5},{22,6},{71,7},{24,8},{73... | collective-permute-start | bytes 1253384 | tf_op jit(solution)/shard_map/ppermute | solution.py:44
  52.3 1.3 collective-permute-start.14
  54.5 1.3 collective-permute-start.15
  55.8 2.1 %collective-permute-done.10.refs_7_ = bf16[2,48,2176]{2,1,0:T(8,128)(2,1)S(1)} collective-permute-done((bf16[2,48,2176]{2,1,0:T(8,128)(2,1)S(1)}, bf16[2,48,2176]{2,1,0:T(8,128)(2,1)S(1)}, u32[]{:S(2)}, u32[]{:S(2)}) %collective-permute-start.10) | collective-permute-done | bytes 417824 | tf_op jit(solution)/shard_map/ppermute | solution.py:44
  57.9 1.6 %collective-permute-start.16 = (bf16[2,48,2176]{2,1,0:T(8,128)(2,1)S(1)}, bf16[2,48,2176]{2,1,0:T(8,128)(2,1)S(1)}, u32[]{:S(2)}, u32[]{:S(2)}) collective-permute-start(bf16[2,48,2176]{2,1,0:T(8,128)(2,1)S(1)} %collective-permute-done.10.refs_7_), channel_id=1, source_target_pairs={{1,0},{0,1},{3,2},{2,3},{5,4},{4,5},{7,6},{6,7},{9,8},{8,9},{11,10... | collective-permute-start | bytes 1253384 | tf_op jit(solution)/shard_map/ppermute | solution.py:44
  60.3 2.1 %collective-permute-done.8.refs_4_ = bf16[2,48,2176]{2,1,0:T(8,128)(2,1)S(1)} collective-permute-done((bf16[2,48,2176]{2,1,0:T(8,128)(2,1)S(1)}, bf16[2,48,2176]{2,1,0:T(8,128)(2,1)S(1)}, u32[]{:S(2)}, u32[]{:S(2)}) %collective-permute-start.8) | collective-permute-done | bytes 417824 | tf_op jit(solution)/shard_map/ppermute | solution.py:44
  62.4 1.6 %collective-permute-start.13 = (bf16[2,48,2176]{2,1,0:T(8,128)(2,1)S(1)}, bf16[2,48,2176]{2,1,0:T(8,128)(2,1)S(1)}, u32[]{:S(2)}, u32[]{:S(2)}) collective-permute-start(bf16[2,48,2176]{2,1,0:T(8,128)(2,1)S(1)} %collective-permute-done.8.refs_4_), channel_id=1, source_target_pairs={{1,0},{0,1},{3,2},{2,3},{5,4},{4,5},{7,6},{6,7},{9,8},{8,9},{11,10... | collective-permute-start | bytes 1253384 | tf_op jit(solution)/shard_map/ppermute | solution.py:44
  64.0 1.4 collective-permute-done.13.refs_12_
  65.4 7.0 %shard_map.91 = (bf16[768,4096]{1,0:T(8,128)(2,1)S(1)}, f32[768,640]{1,0:T(8,128)S(1)}, f32[2,8,128]{2,1,0:T(8,128)S(1)}, f32[8,128]{1,0:T(8,128)S(1)}) custom-call(s32[5]{0:T(128)S(1)} %stack.23.ids, bf16[2,48,2176]{2,1,0:T(8,128)(2,1)S(1)} %get-tuple-element.44.low.refs_0_, bf16[2,48,2176]{2,1,0:T(8,128)(2,1)S(1)} %get-tuple-element.45.high.refs_1_, ...), custom_call_target="tpu_custom_call" | custom-call | flops 4026531840 | bytes 20971520 | tf_op jit(solution)/shard_map/pallas_call | solution.py:213
  72.4 12.7 %all_to_all.20.parts = f32[16,2,8,128]{3,2,1,0:T(8,128)S(1)} all-to-all(f32[16,2,8,128]{3,2,1,0:T(8,128)S(1)} %broadcast_in_dim.2), channel_id=1, replica_groups=mesh['y'=4,'x'=4,'z'=8,'c'=2] {'z','c'}, dimensions={0} | all-to-all | bytes 262144 | tf_op jit(solution)/shard_map/all_to_all | solution.py:233
  85.1 11.5 %all_to_all.21.parts = f32[16,2,8,128]{3,2,1,0:T(8,128)S(1)} all-to-all(f32[16,2,8,128]{3,2,1,0:T(8,128)S(1)} %shard_map.92), channel_id=1, replica_groups=mesh['y'=4,'x'=4,'z'=8,'c'=2] {'y','x'}, dimensions={0} | all-to-all | bytes 262144 | tf_op jit(solution)/shard_map/all_to_all | solution.py:501
  97.4 2.6 %shard_map.94 = (bf16[768,640]{1,0:T(8,128)(2,1)S(1)}, bf16[768,1024]{1,0:T(8,128)(2,1)S(1)}) custom-call(s32[5]{0:T(128)S(1)} %stack.23.ids, f32[768,640]{1,0:T(8,128)S(1)} %get-tuple-element.49.logits, f32[8,128]{1,0:T(8,128)S(1)} %get-tuple-element.51.norm, f32[8,128]{1,0:T(8,128)S(1)} %get-tuple-element.52.weight, ...), custom_call_target="tpu_custom_call" | custom-call | flops 1006632960 | bytes 6291456 | tf_op jit(solution)/shard_map/pallas_call | solution.py:324
  101.0 2.0 %shard_map.96 = bf16[768,1024]{1,0:T(8,128)(2,1)S(1)} custom-call(s32[5]{0:T(128)S(1)} %stack.23.ids, bf16[768,640]{1,0:T(8,128)(2,1)S(1)} %get-tuple-element.54.grad, bf16[4096,640]{1,0:T(8,128)(2,1)S(1)} %get-tuple-element.48.refs_16_.head), custom_call_target="tpu_custom_call" | custom-call | flops 2013265920 | bytes 16777216 | tf_op jit(solution)/shard_map/pallas_call | solution.py:335
  103.3 3.2 %shard_map.95.own = f32[768,2048]{1,0:T(8,128)S(1)} custom-call(s32[5]{0:T(128)S(1)} %stack.23.ids, bf16[768,640]{1,0:T(8,128)(2,1)S(1)} %get-tuple-element.54.grad, bf16[4096,640]{1,0:T(8,128)(2,1)S(1)} %get-tuple-element.48.refs_16_.head), custom_call_target="tpu_custom_call" | custom-call | flops 2013265920 | bytes 10485760 | tf_op jit(solution)/shard_map/pallas_call | solution.py:359
  108.9 4.4 %shard_map.99 = (bf16[4096,640]{1,0:T(8,128)(2,1)}, f32[8,128]{1,0:T(8,128)S(1)}) custom-call(bf16[768,4096]{1,0:T(8,128)(2,1)S(1)} %get-tuple-element.56.hidden, bf16[768,640]{1,0:T(8,128)(2,1)S(1)} %get-tuple-element.54.grad, f32[8,128]{1,0:T(8,128)S(1)} %get-tuple-element.57.refs_0_), custom_call_target="tpu_custom_call" | custom-call | flops 2013265920 | bytes 6291456 | tf_op jit(solution)/shard_map/pallas_call | solution.py:404
  114.3 1.9 %collective-permute-start.21 = (bf16[2,48,2048]{2,1,0:T(8,128)(2,1)S(1)}, bf16[2,48,2048]{2,1,0:T(8,128)(2,1)S(1)}, u32[]{:S(2)}, u32[]{:S(2)}) collective-permute-start(bf16[2,48,2048]{2,1,0:T(8,128)(2,1)S(1)} %get-tuple-element.64), channel_id=1, source_target_pairs={{16,0},{65,1},{18,2},{67,3},{20,4},{69,5},{22,6},{71,7},{24,8},{73... | collective-permute-start | bytes 1179656 | tf_op jit(solution)/shard_map/ppermute | solution.py:44
  116.3 2.8 %collective-permute-start.24 = (bf16[2,48,2048]{2,1,0:T(8,128)(2,1)S(1)}, bf16[2,48,2048]{2,1,0:T(8,128)(2,1)S(1)}, u32[]{:S(2)}, u32[]{:S(2)}) collective-permute-start(bf16[2,48,2048]{2,1,0:T(8,128)(2,1)S(1)} %get-tuple-element.69), channel_id=1, source_target_pairs={{16,0},{65,1},{18,2},{67,3},{20,4},{69,5},{22,6},{71,7},{24,8},{73... | collective-permute-start | bytes 1179656 | tf_op jit(solution)/shard_map/ppermute | solution.py:44
  119.7 4.4 %shard_map.103 = (bf16[4096,640]{1,0:T(8,128)(2,1)}, f32[8,128]{1,0:T(8,128)S(1)}) custom-call(bf16[768,4096]{1,0:T(8,128)(2,1)S(1)} %get-tuple-element.56.hidden, bf16[768,640]{1,0:T(8,128)(2,1)S(1)} %get-tuple-element.54.grad, f32[8,128]{1,0:T(8,128)S(1)} %get-tuple-element.70.refs_0_, ...), custom_call_target="tpu_custom_call", output_to_operand_aliasing={{0}: (3, {})} | custom-call | flops 2013265920 | bytes 6291456 | tf_op jit(solution)/shard_map/pallas_call | solution.py:404
  125.5 3.0 %collective-permute-done.20.refs_1_ = bf16[2,48,2048]{2,1,0:T(8,128)(2,1)S(1)} collective-permute-done((bf16[2,48,2048]{2,1,0:T(8,128)(2,1)S(1)}, bf16[2,48,2048]{2,1,0:T(8,128)(2,1)S(1)}, u32[]{:S(2)}, u32[]{:S(2)}) %collective-permute-start.20) | collective-permute-done | bytes 393248 | tf_op jit(solution)/shard_map/ppermute | solution.py:44
  128.8 2.7 %collective-permute-start.26 = (bf16[48,2048]{1,0:T(8,128)(2,1)S(1)}, bf16[48,2048]{1,0:T(8,128)(2,1)S(1)}, u32[]{:S(2)}, u32[]{:S(2)}) collective-permute-start(bf16[48,2048]{1,0:T(8,128)(2,1)S(1)} %get-tuple-element.75), channel_id=1, source_target_pairs={{64,0},{17,1},{66,2},{19,3},{68,4},{21,5},{70,6},{23,7},{72,8},{25... | collective-permute-start | bytes 589832 | tf_op jit(solution)/shard_map/ppermute | solution.py:44
  131.5 3.1 %collective-permute-done.25.b = bf16[48,2048]{1,0:T(8,128)(2,1)S(1)} collective-permute-done((bf16[48,2048]{1,0:T(8,128)(2,1)S(1)}, bf16[48,2048]{1,0:T(8,128)(2,1)S(1)}, u32[]{:S(2)}, u32[]{:S(2)}) %collective-permute-start.25) | collective-permute-done | bytes 196640 | tf_op jit(solution)/shard_map/ppermute | solution.py:44
  134.5 1.7 %collective-permute-done.26.c = bf16[48,2048]{1,0:T(8,128)(2,1)S(1)} collective-permute-done((bf16[48,2048]{1,0:T(8,128)(2,1)S(1)}, bf16[48,2048]{1,0:T(8,128)(2,1)S(1)}, u32[]{:S(2)}, u32[]{:S(2)}) %collective-permute-start.26) | collective-permute-done | bytes 196640 | tf_op jit(solution)/shard_map/ppermute | solution.py:44
  138.4 7.0 %all-to-all-start.3 = ((bf16[16,48,128]{2,1,0:T(8,128)(2,1)}), bf16[16,48,128]{2,1,0:T(8,128)(2,1)S(1)}, u32[]{:S(2)}, u32[]{:S(2)}) async-start(bf16[16,48,128]{2,1,0:T(8,128)(2,1)} %shard_map.105), calls=%async_computation.3 | async-start | bytes 393216 | tf_op jit(solution)/shard_map/all_to_all | solution.py:521
  146.0 9.9 %all-to-all-done.3.parts = bf16[16,48,128]{2,1,0:T(8,128)(2,1)S(1)} async-done(((bf16[16,48,128]{2,1,0:T(8,128)(2,1)}), bf16[16,48,128]{2,1,0:T(8,128)(2,1)S(1)}, u32[]{:S(2)}, u32[]{:S(2)}) %all-to-all-start.3) | async-done | bytes 196640 | tf_op jit(solution)/shard_map/all_to_all | solution.py:521
  (67 shorter events, 21.6 us)
Async XLA Ops:
  3.3 21.7 %all-to-all-start = ((bf16[16,64,128]{2,1,0:T(8,128)(2,1)}), bf16[16,64,128]{2,1,0:T(8,128)(2,1)S(1)}, u32[]{:S(2)}, u32[]{:S(2)}) async-start(bf16[16,64,128]{2,1,0:T(8,128)(2,1)} %shard_map.85), calls=%async_computation | async-start | bytes 524288 | tf_op jit(solution)/shard_map/all_to_all | solution.py:486
  25.7 8.4 %collective-permute-start.2 = (bf16[48,2176]{1,0:T(8,128)(2,1)S(1)}, bf16[48,2176]{1,0:T(8,128)(2,1)S(1)}, u32[]{:S(2)}, u32[]{:S(2)}) collective-permute-start(bf16[48,2176]{1,0:T(8,128)(2,1)S(1)} %shard_map.86.a), channel_id=1, source_target_pairs={{128,0},{33,1},{130,2},{35,3},{132,4},{37,5},{134,6},{39,7},{136,8... | collective-permute-start | bytes 626696 | tf_op jit(solution)/shard_map/ppermute | solution.py:44
  28.6 6.2 %collective-permute-start.1 = (bf16[48,2176]{1,0:T(8,128)(2,1)S(1)}, bf16[48,2176]{1,0:T(8,128)(2,1)S(1)}, u32[]{:S(2)}, u32[]{:S(2)}) collective-permute-start(bf16[48,2176]{1,0:T(8,128)(2,1)S(1)} %shard_map.86.a), channel_id=1, source_target_pairs={{192,0},{49,1},{194,2},{51,3},{196,4},{53,5},{198,6},{55,7},{200,8... | collective-permute-start | bytes 626696 | tf_op jit(solution)/shard_map/ppermute | solution.py:44
  28.9 5.8 %collective-permute-start = (bf16[48,2176]{1,0:T(8,128)(2,1)S(1)}, bf16[48,2176]{1,0:T(8,128)(2,1)S(1)}, u32[]{:S(2)}, u32[]{:S(2)}) collective-permute-start(bf16[48,2176]{1,0:T(8,128)(2,1)S(1)} %shard_map.86.a), channel_id=1, source_target_pairs={{64,0},{17,1},{66,2},{19,3},{68,4},{21,5},{70,6},{23,7},{72,8},{25... | collective-permute-start | bytes 626696 | tf_op jit(solution)/shard_map/ppermute | solution.py:44
  34.8 2.3 %collective-permute-start.3 = (bf16[2,48,2176]{2,1,0:T(8,128)(2,1)S(1)}, bf16[2,48,2176]{2,1,0:T(8,128)(2,1)S(1)}, u32[]{:S(2)}, u32[]{:S(2)}) collective-permute-start(bf16[2,48,2176]{2,1,0:T(8,128)(2,1)S(1)} %get-tuple-element.42.low), channel_id=1, source_target_pairs={{1,0},{0,1},{3,2},{2,3},{5,4},{4,5},{7,6},{6,7},{9,8},{8,9},{11,10... | collective-permute-start | bytes 1253384 | tf_op jit(solution)/shard_map/ppermute | solution.py:44
  35.7 2.0 %collective-permute-start.4 = (bf16[2,48,2176]{2,1,0:T(8,128)(2,1)S(1)}, bf16[2,48,2176]{2,1,0:T(8,128)(2,1)S(1)}, u32[]{:S(2)}, u32[]{:S(2)}) collective-permute-start(bf16[2,48,2176]{2,1,0:T(8,128)(2,1)S(1)} %get-tuple-element.43.high), channel_id=1, source_target_pairs={{1,0},{0,1},{3,2},{2,3},{5,4},{4,5},{7,6},{6,7},{9,8},{8,9},{11,10... | collective-permute-start | bytes 1253384 | tf_op jit(solution)/shard_map/ppermute | solution.py:44
  37.8 8.0 %collective-permute-start.5 = (bf16[2,48,2176]{2,1,0:T(8,128)(2,1)S(1)}, bf16[2,48,2176]{2,1,0:T(8,128)(2,1)S(1)}, u32[]{:S(2)}, u32[]{:S(2)}) collective-permute-start(bf16[2,48,2176]{2,1,0:T(8,128)(2,1)S(1)} %get-tuple-element.44.low.refs_0_), channel_id=1, source_target_pairs={{16,0},{65,1},{18,2},{67,3},{20,4},{69,5},{22,6},{71,7},{24,8},{73... | collective-permute-start | bytes 1253384 | tf_op jit(solution)/shard_map/ppermute | solution.py:44
  40.8 8.7 %collective-permute-start.6 = (bf16[2,48,2176]{2,1,0:T(8,128)(2,1)S(1)}, bf16[2,48,2176]{2,1,0:T(8,128)(2,1)S(1)}, u32[]{:S(2)}, u32[]{:S(2)}) collective-permute-start(bf16[2,48,2176]{2,1,0:T(8,128)(2,1)S(1)} %get-tuple-element.45.high.refs_1_), channel_id=1, source_target_pairs={{48,0},{193,1},{50,2},{195,3},{52,4},{197,5},{54,6},{199,7},{56,8}... | collective-permute-start | bytes 1253384 | tf_op jit(solution)/shard_map/ppermute | solution.py:44
  45.8 6.5 %collective-permute-start.11 = (bf16[2,48,2176]{2,1,0:T(8,128)(2,1)S(1)}, bf16[2,48,2176]{2,1,0:T(8,128)(2,1)S(1)}, u32[]{:S(2)}, u32[]{:S(2)}) collective-permute-start(bf16[2,48,2176]{2,1,0:T(8,128)(2,1)S(1)} %collective-permute-done.5.first.refs_2_), channel_id=1, source_target_pairs={{1,0},{0,1},{3,2},{2,3},{5,4},{4,5},{7,6},{6,7},{9,8},{8,9},{11,10... | collective-permute-start | bytes 1253384 | tf_op jit(solution)/shard_map/ppermute | solution.py:44
  46.6 7.9 %collective-permute-start.9 = (bf16[2,48,2176]{2,1,0:T(8,128)(2,1)S(1)}, bf16[2,48,2176]{2,1,0:T(8,128)(2,1)S(1)}, u32[]{:S(2)}, u32[]{:S(2)}) collective-permute-start(bf16[2,48,2176]{2,1,0:T(8,128)(2,1)S(1)} %collective-permute-done.5.first.refs_2_), channel_id=1, source_target_pairs={{16,0},{65,1},{18,2},{67,3},{20,4},{69,5},{22,6},{71,7},{24,8},{73... | collective-permute-start | bytes 1253384 | tf_op jit(solution)/shard_map/ppermute | solution.py:44
  49.5 8.4 %collective-permute-start.10 = (bf16[2,48,2176]{2,1,0:T(8,128)(2,1)S(1)}, bf16[2,48,2176]{2,1,0:T(8,128)(2,1)S(1)}, u32[]{:S(2)}, u32[]{:S(2)}) collective-permute-start(bf16[2,48,2176]{2,1,0:T(8,128)(2,1)S(1)} %collective-permute-done.6.second.refs_5_), channel_id=1, source_target_pairs={{48,0},{193,1},{50,2},{195,3},{52,4},{197,5},{54,6},{199,7},{56,8}... | collective-permute-start | bytes 1253384 | tf_op jit(solution)/shard_map/ppermute | solution.py:44
  49.6 9.9 %collective-permute-start.7 = (bf16[2,48,2176]{2,1,0:T(8,128)(2,1)S(1)}, bf16[2,48,2176]{2,1,0:T(8,128)(2,1)S(1)}, u32[]{:S(2)}, u32[]{:S(2)}) collective-permute-start(bf16[2,48,2176]{2,1,0:T(8,128)(2,1)S(1)} %get-tuple-element.46), channel_id=1, source_target_pairs={{16,0},{65,1},{18,2},{67,3},{20,4},{69,5},{22,6},{71,7},{24,8},{73... | collective-permute-start | bytes 1253384 | tf_op jit(solution)/shard_map/ppermute | solution.py:44
  52.3 10.1 %collective-permute-start.8 = (bf16[2,48,2176]{2,1,0:T(8,128)(2,1)S(1)}, bf16[2,48,2176]{2,1,0:T(8,128)(2,1)S(1)}, u32[]{:S(2)}, u32[]{:S(2)}) collective-permute-start(bf16[2,48,2176]{2,1,0:T(8,128)(2,1)S(1)} %get-tuple-element.47), channel_id=1, source_target_pairs={{48,0},{193,1},{50,2},{195,3},{52,4},{197,5},{54,6},{199,7},{56,8}... | collective-permute-start | bytes 1253384 | tf_op jit(solution)/shard_map/ppermute | solution.py:44
  52.3 11.7 %collective-permute-start.14 = (bf16[2,48,2176]{2,1,0:T(8,128)(2,1)S(1)}, bf16[2,48,2176]{2,1,0:T(8,128)(2,1)S(1)}, u32[]{:S(2)}, u32[]{:S(2)}) collective-permute-start(bf16[2,48,2176]{2,1,0:T(8,128)(2,1)S(1)} %collective-permute-done.6.second.refs_5_), channel_id=1, source_target_pairs={{1,0},{0,1},{3,2},{2,3},{5,4},{4,5},{7,6},{6,7},{9,8},{8,9},{11,10... | collective-permute-start | bytes 1253384 | tf_op jit(solution)/shard_map/ppermute | solution.py:44
  54.5 9.5 %collective-permute-start.15 = (bf16[2,48,2176]{2,1,0:T(8,128)(2,1)S(1)}, bf16[2,48,2176]{2,1,0:T(8,128)(2,1)S(1)}, u32[]{:S(2)}, u32[]{:S(2)}) collective-permute-start(bf16[2,48,2176]{2,1,0:T(8,128)(2,1)S(1)} %collective-permute-done.9.refs_6_), channel_id=1, source_target_pairs={{1,0},{0,1},{3,2},{2,3},{5,4},{4,5},{7,6},{6,7},{9,8},{8,9},{11,10... | collective-permute-start | bytes 1253384 | tf_op jit(solution)/shard_map/ppermute | solution.py:44
  57.9 6.1 %collective-permute-start.16 = (bf16[2,48,2176]{2,1,0:T(8,128)(2,1)S(1)}, bf16[2,48,2176]{2,1,0:T(8,128)(2,1)S(1)}, u32[]{:S(2)}, u32[]{:S(2)}) collective-permute-start(bf16[2,48,2176]{2,1,0:T(8,128)(2,1)S(1)} %collective-permute-done.10.refs_7_), channel_id=1, source_target_pairs={{1,0},{0,1},{3,2},{2,3},{5,4},{4,5},{7,6},{6,7},{9,8},{8,9},{11,10... | collective-permute-start | bytes 1253384 | tf_op jit(solution)/shard_map/ppermute | solution.py:44
  59.5 4.5 %collective-permute-start.12 = (bf16[2,48,2176]{2,1,0:T(8,128)(2,1)S(1)}, bf16[2,48,2176]{2,1,0:T(8,128)(2,1)S(1)}, u32[]{:S(2)}, u32[]{:S(2)}) collective-permute-start(bf16[2,48,2176]{2,1,0:T(8,128)(2,1)S(1)} %collective-permute-done.7.refs_3_), channel_id=1, source_target_pairs={{1,0},{0,1},{3,2},{2,3},{5,4},{4,5},{7,6},{6,7},{9,8},{8,9},{11,10... | collective-permute-start | bytes 1253384 | tf_op jit(solution)/shard_map/ppermute | solution.py:44
  62.4 3.0 %collective-permute-start.13 = (bf16[2,48,2176]{2,1,0:T(8,128)(2,1)S(1)}, bf16[2,48,2176]{2,1,0:T(8,128)(2,1)S(1)}, u32[]{:S(2)}, u32[]{:S(2)}) collective-permute-start(bf16[2,48,2176]{2,1,0:T(8,128)(2,1)S(1)} %collective-permute-done.8.refs_4_), channel_id=1, source_target_pairs={{1,0},{0,1},{3,2},{2,3},{5,4},{4,5},{7,6},{6,7},{9,8},{8,9},{11,10... | collective-permute-start | bytes 1253384 | tf_op jit(solution)/shard_map/ppermute | solution.py:44
  65.4 31.3 %copy-start.4 = (f32[16]{0:T(128)S(1)}, f32[16]{0:T(128)}, u32[]{:S(2)}) copy-start(f32[16]{0:T(128)} %ref_logps.1) | copy-start | bytes 196
  65.4 31.3 %copy-start.5 = (s32[16]{0:T(128)S(1)}, s32[16]{0:T(128)}, u32[]{:S(2)}) copy-start(s32[16]{0:T(128)} %pairing.1) | copy-start | bytes 196
  100.1 6.4 %collective-permute-start.17 = (bf16[768,1024]{1,0:T(8,128)(2,1)S(1)}, bf16[768,1024]{1,0:T(8,128)(2,1)S(1)}, u32[]{:S(2)}, u32[]{:S(2)}) collective-permute-start(bf16[768,1024]{1,0:T(8,128)(2,1)S(1)} %get-tuple-element.55), channel_id=1, source_target_pairs={{1,0},{0,1},{3,2},{2,3},{5,4},{4,5},{7,6},{6,7},{9,8},{8,9},{11,10... | collective-permute-start | bytes 4718600 | tf_op jit(solution)/shard_map/ppermute | solution.py:44
  103.0 3.7 %collective-permute-start.18 = (bf16[768,1024]{1,0:T(8,128)(2,1)S(1)}, bf16[768,1024]{1,0:T(8,128)(2,1)S(1)}, u32[]{:S(2)}, u32[]{:S(2)}) collective-permute-start(bf16[768,1024]{1,0:T(8,128)(2,1)S(1)} %shard_map.96), channel_id=1, source_target_pairs={{1,0},{0,1},{3,2},{2,3},{5,4},{4,5},{7,6},{6,7},{9,8},{8,9},{11,10... | collective-permute-start | bytes 4718600 | tf_op jit(solution)/shard_map/ppermute | solution.py:44
  107.4 8.8 %collective-permute-start.23 = (bf16[2,48,2048]{2,1,0:T(8,128)(2,1)S(1)}, bf16[2,48,2048]{2,1,0:T(8,128)(2,1)S(1)}, u32[]{:S(2)}, u32[]{:S(2)}) collective-permute-start(bf16[2,48,2048]{2,1,0:T(8,128)(2,1)S(1)} %get-tuple-element.68), channel_id=1, source_target_pairs={{16,0},{65,1},{18,2},{67,3},{20,4},{69,5},{22,6},{71,7},{24,8},{73... | collective-permute-start | bytes 1179656 | tf_op jit(solution)/shard_map/ppermute | solution.py:44
  108.0 11.0 %collective-permute-start.19 = (bf16[2,48,2048]{2,1,0:T(8,128)(2,1)S(1)}, bf16[2,48,2048]{2,1,0:T(8,128)(2,1)S(1)}, u32[]{:S(2)}, u32[]{:S(2)}) collective-permute-start(bf16[2,48,2048]{2,1,0:T(8,128)(2,1)S(1)} %get-tuple-element.61), channel_id=1, source_target_pairs={{48,0},{193,1},{50,2},{195,3},{52,4},{197,5},{54,6},{199,7},{56,8}... | collective-permute-start | bytes 1179656 | tf_op jit(solution)/shard_map/ppermute | solution.py:44
  114.3 9.8 %collective-permute-start.21 = (bf16[2,48,2048]{2,1,0:T(8,128)(2,1)S(1)}, bf16[2,48,2048]{2,1,0:T(8,128)(2,1)S(1)}, u32[]{:S(2)}, u32[]{:S(2)}) collective-permute-start(bf16[2,48,2048]{2,1,0:T(8,128)(2,1)S(1)} %get-tuple-element.64), channel_id=1, source_target_pairs={{16,0},{65,1},{18,2},{67,3},{20,4},{69,5},{22,6},{71,7},{24,8},{73... | collective-permute-start | bytes 1179656 | tf_op jit(solution)/shard_map/ppermute | solution.py:44
  116.2 8.1 %collective-permute-start.22 = (bf16[2,48,2048]{2,1,0:T(8,128)(2,1)S(1)}, bf16[2,48,2048]{2,1,0:T(8,128)(2,1)S(1)}, u32[]{:S(2)}, u32[]{:S(2)}) collective-permute-start(bf16[2,48,2048]{2,1,0:T(8,128)(2,1)S(1)} %get-tuple-element.66), channel_id=1, source_target_pairs={{48,0},{193,1},{50,2},{195,3},{52,4},{197,5},{54,6},{199,7},{56,8}... | collective-permute-start | bytes 1179656 | tf_op jit(solution)/shard_map/ppermute | solution.py:44
  116.3 9.3 %collective-permute-start.24 = (bf16[2,48,2048]{2,1,0:T(8,128)(2,1)S(1)}, bf16[2,48,2048]{2,1,0:T(8,128)(2,1)S(1)}, u32[]{:S(2)}, u32[]{:S(2)}) collective-permute-start(bf16[2,48,2048]{2,1,0:T(8,128)(2,1)S(1)} %get-tuple-element.69), channel_id=1, source_target_pairs={{16,0},{65,1},{18,2},{67,3},{20,4},{69,5},{22,6},{71,7},{24,8},{73... | collective-permute-start | bytes 1179656 | tf_op jit(solution)/shard_map/ppermute | solution.py:44
  119.7 8.8 %collective-permute-start.20 = (bf16[2,48,2048]{2,1,0:T(8,128)(2,1)S(1)}, bf16[2,48,2048]{2,1,0:T(8,128)(2,1)S(1)}, u32[]{:S(2)}, u32[]{:S(2)}) collective-permute-start(bf16[2,48,2048]{2,1,0:T(8,128)(2,1)S(1)} %get-tuple-element.63), channel_id=1, source_target_pairs={{48,0},{193,1},{50,2},{195,3},{52,4},{197,5},{54,6},{199,7},{56,8}... | collective-permute-start | bytes 1179656 | tf_op jit(solution)/shard_map/ppermute | solution.py:44
  128.7 5.8 %collective-permute-start.25 = (bf16[48,2048]{1,0:T(8,128)(2,1)S(1)}, bf16[48,2048]{1,0:T(8,128)(2,1)S(1)}, u32[]{:S(2)}, u32[]{:S(2)}) collective-permute-start(bf16[48,2048]{1,0:T(8,128)(2,1)S(1)} %get-tuple-element.74), channel_id=1, source_target_pairs={{192,0},{49,1},{194,2},{51,3},{196,4},{53,5},{198,6},{55,7},{200,8... | collective-permute-start | bytes 589832 | tf_op jit(solution)/shard_map/ppermute | solution.py:44
  128.8 7.4 %collective-permute-start.26 = (bf16[48,2048]{1,0:T(8,128)(2,1)S(1)}, bf16[48,2048]{1,0:T(8,128)(2,1)S(1)}, u32[]{:S(2)}, u32[]{:S(2)}) collective-permute-start(bf16[48,2048]{1,0:T(8,128)(2,1)S(1)} %get-tuple-element.75), channel_id=1, source_target_pairs={{64,0},{17,1},{66,2},{19,3},{68,4},{21,5},{70,6},{23,7},{72,8},{25... | collective-permute-start | bytes 589832 | tf_op jit(solution)/shard_map/ppermute | solution.py:44
  131.5 6.0 %collective-permute-start.27 = (bf16[48,2048]{1,0:T(8,128)(2,1)S(1)}, bf16[48,2048]{1,0:T(8,128)(2,1)S(1)}, u32[]{:S(2)}, u32[]{:S(2)}) collective-permute-start(bf16[48,2048]{1,0:T(8,128)(2,1)S(1)} %get-tuple-element.76), channel_id=1, source_target_pairs={{128,0},{33,1},{130,2},{35,3},{132,4},{37,5},{134,6},{39,7},{136,8... | collective-permute-start | bytes 589832 | tf_op jit(solution)/shard_map/ppermute | solution.py:44
  138.4 17.4 %all-to-all-start.3 = ((bf16[16,48,128]{2,1,0:T(8,128)(2,1)}), bf16[16,48,128]{2,1,0:T(8,128)(2,1)S(1)}, u32[]{:S(2)}, u32[]{:S(2)}) async-start(bf16[16,48,128]{2,1,0:T(8,128)(2,1)} %shard_map.105), calls=%async_computation.3 | async-start | bytes 393216 | tf_op jit(solution)/shard_map/all_to_all | solution.py:521
  (4 other events, 35.2 us)

commit v4 on v3

--- a/solution.py
+++ b/solution.py
@@ -490,8 +490,7 @@
     other = [fetch(low, near), fetch(high, near)]
     low, high = gate(low, high, *other)
     ahead_low, back_high = fetch(low, final(1)), fetch(high, final(-1))
-    late_low, late_high = gate(low, high, ahead_low, back_high)
-    ahead_high, back_low = fetch(late_high, final(1)), fetch(late_low, final(-1))
+    ahead_high, back_low = fetch(high, final(1)), fetch(low, final(-1))
     far_low, far_high = fetch(ahead_low, final(1)), fetch(back_high, final(-1))
     own = [low, high, ahead_low, ahead_high, back_low, back_high, far_low, far_high]
     other += [fetch(v, near) for v in own[2:]]
@@ -505,10 +504,9 @@
     received = [fetch(send, near)]
     received.append(fetch(grad_other_second(ids, logit_grad, head), near))
     own = grad_own(ids, logit_grad, head)
-    far_low, far_high, mark = split_final(ids, own, received, arrived(received[0]), 6, 8)
+    *parts, mark = split_final(ids, own, received, arrived(received[0]), 0, 8)
+    keep_low, keep_high, ahead_low, ahead_high, back_low, back_high, far_low, far_high = parts
     half, mark = grad_head_half(rows, logit_grad, mark)
-    *parts, mark = split_final(ids, own, received, mark, 0, 6)
-    keep_low, keep_high, ahead_low, ahead_high, back_low, back_high = parts
     ahead_low, _ = add(ahead_low, fetch(far_low, final(-1)), mark)
     back_high, mark = add(back_high, fetch(far_high, final(1)), mark)
     grad_head, mark = grad_head_half(rows, logit_grad, mark, half)

time: 157 us -> 153 us (0.975)
  waiting for transfers between devices: 46 us -> 44.2 us
    ppermute x28, waiting for transfers between devices: 24.5 us -> 22.7 us  [fetch(): return lax.ppermute(value, AXES, pairs)]
    ppermute x28, starting transfers between devices: 32.8 us -> 31.2 us  [fetch(): return lax.ppermute(value, AXES, pairs)]
  transfers between devices with their start and end apart: 30 -> 30, of which waited for: 17 -> 15; matrix products, arithmetic and copies ran while one was open for 0% -> 0% of each run, Pallas kernels for 10% -> 10%
where the time goes in v4:
time: 153 us
  starting transfers between devices  48.7 us (32%)
  waiting for transfers between devices  44.2 us (29%)
  Pallas kernels  30.6 us (20%)
  blocking collectives  24.2 us (16%)
  local copies, waits for them, and re-layouts  4.52 us (3%)
    ppermute x28, starting transfers between devices, fetch(): return lax.ppermute(value, AXES, pairs)  31.2 us
    ppermute x28, waiting for transfers between devices, fetch(): return lax.ppermute(value, AXES, pairs)  22.7 us
    all_to_all x1, blocking collectives, exchange(): lax.all_to_all(jnp.broadcast_to(value[None], (16,) + value.shape), axes,...  12.7 us
    all_to_all x1, waiting for transfers between devices, local(): lax.all_to_all(first_message(targets, hidden), ('z', 'c'), 0, 0, tiled=True)  11.6 us
    all_to_all x1, blocking collectives, local(): stats = lax.all_to_all(stats, ('y', 'x'), 0, 0, tiled=True)  11.6 us
    all_to_all x1, starting transfers between devices, local(): lax.all_to_all(first_message(targets, hidden), ('z', 'c'), 0, 0, tiled=True)  9.98 us
    all_to_all x1, waiting for transfers between devices, local(): grad_hidden = finish(lax.all_to_all(parts, ('z', 'c'), 0, 0, tiled=True))  9.87 us
    pallas_call x2, Pallas kernels, grad_head_half(): pl.pallas_call(head_kernel, grid=(steps,), in_specs=[pl.BlockSpec((TOKENS...  8.87 us
  transfers between devices with their start and end apart: 30, of which 15 were waited for; matrix products, arithmetic and copies ran while one was open for 0% of the time, Pallas kernels for 10%

profile of v4, /device:TPU:1, one launch (start us, length us, event | category | flops | bytes accessed | tf_op | source)
XLA Modules:
  0.0 153.0 jit_solution(9188099734059784210)
XLA Ops:
  2.0 1.3 shard_map.85
  3.3 10.0 %all-to-all-start = ((bf16[16,64,128]{2,1,0:T(8,128)(2,1)}), bf16[16,64,128]{2,1,0:T(8,128)(2,1)S(1)}, u32[]{:S(2)}, u32[]{:S(2)}) async-start(bf16[16,64,128]{2,1,0:T(8,128)(2,1)} %shard_map.85), calls=%async_computation | async-start | bytes 524288 | tf_op jit(solution)/shard_map/all_to_all | solution.py:486
  13.4 11.6 %all-to-all-done.parts = bf16[16,64,128]{2,1,0:T(8,128)(2,1)S(1)} async-done(((bf16[16,64,128]{2,1,0:T(8,128)(2,1)}), bf16[16,64,128]{2,1,0:T(8,128)(2,1)S(1)}, u32[]{:S(2)}, u32[]{:S(2)}) %all-to-all-start) | async-done | bytes 262176 | tf_op jit(solution)/shard_map/all_to_all | solution.py:486
  25.7 2.8 %collective-permute-start.2 = (bf16[48,2176]{1,0:T(8,128)(2,1)S(1)}, bf16[48,2176]{1,0:T(8,128)(2,1)S(1)}, u32[]{:S(2)}, u32[]{:S(2)}) collective-permute-start(bf16[48,2176]{1,0:T(8,128)(2,1)S(1)} %shard_map.86.a), channel_id=1, source_target_pairs={{128,0},{33,1},{130,2},{35,3},{132,4},{37,5},{134,6},{39,7},{136,8... | collective-permute-start | bytes 626696 | tf_op jit(solution)/shard_map/ppermute | solution.py:44
  28.9 2.4 %collective-permute-start = (bf16[48,2176]{1,0:T(8,128)(2,1)S(1)}, bf16[48,2176]{1,0:T(8,128)(2,1)S(1)}, u32[]{:S(2)}, u32[]{:S(2)}) collective-permute-start(bf16[48,2176]{1,0:T(8,128)(2,1)S(1)} %shard_map.86.a), channel_id=1, source_target_pairs={{64,0},{17,1},{66,2},{19,3},{68,4},{21,5},{70,6},{23,7},{72,8},{25... | collective-permute-start | bytes 626696 | tf_op jit(solution)/shard_map/ppermute | solution.py:44
  31.2 2.5 %copy-done = bf16[4096,640]{1,0:T(8,128)(2,1)S(1)} copy-done((bf16[4096,640]{1,0:T(8,128)(2,1)S(1)}, bf16[4096,640]{1,0:T(8,128)(2,1)}, u32[]{:S(2)}) %copy-start) | copy-done | bytes 5242904
  38.7 2.2 %collective-permute-start.5 = (bf16[2,48,2176]{2,1,0:T(8,128)(2,1)S(1)}, bf16[2,48,2176]{2,1,0:T(8,128)(2,1)S(1)}, u32[]{:S(2)}, u32[]{:S(2)}) collective-permute-start(bf16[2,48,2176]{2,1,0:T(8,128)(2,1)S(1)} %get-tuple-element.41.refs_0_), channel_id=1, source_target_pairs={{16,0},{65,1},{18,2},{67,3},{20,4},{69,5},{22,6},{71,7},{24,8},{73... | collective-permute-start | bytes 1253384 | tf_op jit(solution)/shard_map/ppermute | solution.py:44
  40.9 2.7 %collective-permute-start.6 = (bf16[2,48,2176]{2,1,0:T(8,128)(2,1)S(1)}, bf16[2,48,2176]{2,1,0:T(8,128)(2,1)S(1)}, u32[]{:S(2)}, u32[]{:S(2)}) collective-permute-start(bf16[2,48,2176]{2,1,0:T(8,128)(2,1)S(1)} %get-tuple-element.42.refs_1_), channel_id=1, source_target_pairs={{16,0},{65,1},{18,2},{67,3},{20,4},{69,5},{22,6},{71,7},{24,8},{73... | collective-permute-start | bytes 1253384 | tf_op jit(solution)/shard_map/ppermute | solution.py:44
  43.6 3.0 %collective-permute-done.7.refs_4_ = bf16[2,48,2176]{2,1,0:T(8,128)(2,1)S(1)} collective-permute-done((bf16[2,48,2176]{2,1,0:T(8,128)(2,1)S(1)}, bf16[2,48,2176]{2,1,0:T(8,128)(2,1)S(1)}, u32[]{:S(2)}, u32[]{:S(2)}) %collective-permute-start.7) | collective-permute-done | bytes 417824 | tf_op jit(solution)/shard_map/ppermute | solution.py:44
  47.5 3.0 %collective-permute-start.9 = (bf16[2,48,2176]{2,1,0:T(8,128)(2,1)S(1)}, bf16[2,48,2176]{2,1,0:T(8,128)(2,1)S(1)}, u32[]{:S(2)}, u32[]{:S(2)}) collective-permute-start(bf16[2,48,2176]{2,1,0:T(8,128)(2,1)S(1)} %collective-permute-done.5.refs_2_), channel_id=1, source_target_pairs={{16,0},{65,1},{18,2},{67,3},{20,4},{69,5},{22,6},{71,7},{24,8},{73... | collective-permute-start | bytes 1253384 | tf_op jit(solution)/shard_map/ppermute | solution.py:44
  52.8 2.7 %collective-permute-done.9.refs_6_ = bf16[2,48,2176]{2,1,0:T(8,128)(2,1)S(1)} collective-permute-done((bf16[2,48,2176]{2,1,0:T(8,128)(2,1)S(1)}, bf16[2,48,2176]{2,1,0:T(8,128)(2,1)S(1)}, u32[]{:S(2)}, u32[]{:S(2)}) %collective-permute-start.9) | collective-permute-done | bytes 417824 | tf_op jit(solution)/shard_map/ppermute | solution.py:44
  55.4 1.3 collective-permute-start.15
  56.7 2.7 %collective-permute-done.10.refs_7_ = bf16[2,48,2176]{2,1,0:T(8,128)(2,1)S(1)} collective-permute-done((bf16[2,48,2176]{2,1,0:T(8,128)(2,1)S(1)}, bf16[2,48,2176]{2,1,0:T(8,128)(2,1)S(1)}, u32[]{:S(2)}, u32[]{:S(2)}) %collective-permute-start.10) | collective-permute-done | bytes 417824 | tf_op jit(solution)/shard_map/ppermute | solution.py:44
  59.4 1.8 %collective-permute-start.16 = (bf16[2,48,2176]{2,1,0:T(8,128)(2,1)S(1)}, bf16[2,48,2176]{2,1,0:T(8,128)(2,1)S(1)}, u32[]{:S(2)}, u32[]{:S(2)}) collective-permute-start(bf16[2,48,2176]{2,1,0:T(8,128)(2,1)S(1)} %collective-permute-done.10.refs_7_), channel_id=1, source_target_pairs={{1,0},{0,1},{3,2},{2,3},{5,4},{4,5},{7,6},{6,7},{9,8},{8,9},{11,10... | collective-permute-start | bytes 1253384 | tf_op jit(solution)/shard_map/ppermute | solution.py:44
  61.2 1.4 collective-permute-done.16.refs_15_
  62.6 7.0 %shard_map.90 = (bf16[768,4096]{1,0:T(8,128)(2,1)S(1)}, f32[768,640]{1,0:T(8,128)S(1)}, f32[2,8,128]{2,1,0:T(8,128)S(1)}, f32[8,128]{1,0:T(8,128)S(1)}) custom-call(s32[5]{0:T(128)S(1)} %stack.23.ids, bf16[2,48,2176]{2,1,0:T(8,128)(2,1)S(1)} %get-tuple-element.41.refs_0_, bf16[2,48,2176]{2,1,0:T(8,128)(2,1)S(1)} %get-tuple-element.42.refs_1_, ...), custom_call_target="tpu_custom_call" | custom-call | flops 4026531840 | bytes 20971520 | tf_op jit(solution)/shard_map/pallas_call | solution.py:213
  69.6 12.7 %all_to_all.20.parts = f32[16,2,8,128]{3,2,1,0:T(8,128)S(1)} all-to-all(f32[16,2,8,128]{3,2,1,0:T(8,128)S(1)} %broadcast_in_dim.2), channel_id=1, replica_groups=mesh['y'=4,'x'=4,'z'=8,'c'=2] {'z','c'}, dimensions={0} | all-to-all | bytes 262144 | tf_op jit(solution)/shard_map/all_to_all | solution.py:233
  82.3 11.6 %all_to_all.21.parts = f32[16,2,8,128]{3,2,1,0:T(8,128)S(1)} all-to-all(f32[16,2,8,128]{3,2,1,0:T(8,128)S(1)} %shard_map.91), channel_id=1, replica_groups=mesh['y'=4,'x'=4,'z'=8,'c'=2] {'y','x'}, dimensions={0} | all-to-all | bytes 262144 | tf_op jit(solution)/shard_map/all_to_all | solution.py:500
  94.7 2.6 %shard_map.93 = (bf16[768,640]{1,0:T(8,128)(2,1)S(1)}, bf16[768,1024]{1,0:T(8,128)(2,1)S(1)}) custom-call(s32[5]{0:T(128)S(1)} %stack.23.ids, f32[768,640]{1,0:T(8,128)S(1)} %get-tuple-element.44.logits, f32[8,128]{1,0:T(8,128)S(1)} %get-tuple-element.46.norm, f32[8,128]{1,0:T(8,128)S(1)} %get-tuple-element.47.weight, ...), custom_call_target="tpu_custom_call" | custom-call | flops 1006632960 | bytes 6291456 | tf_op jit(solution)/shard_map/pallas_call | solution.py:324
  98.2 2.0 %shard_map.95 = bf16[768,1024]{1,0:T(8,128)(2,1)S(1)} custom-call(s32[5]{0:T(128)S(1)} %stack.23.ids, bf16[768,640]{1,0:T(8,128)(2,1)S(1)} %get-tuple-element.49.grad, bf16[4096,640]{1,0:T(8,128)(2,1)S(1)} %get-tuple-element.43.refs_16_.head), custom_call_target="tpu_custom_call" | custom-call | flops 2013265920 | bytes 16777216 | tf_op jit(solution)/shard_map/pallas_call | solution.py:335
  100.5 3.2 %shard_map.94.own = f32[768,2048]{1,0:T(8,128)S(1)} custom-call(s32[5]{0:T(128)S(1)} %stack.23.ids, bf16[768,640]{1,0:T(8,128)(2,1)S(1)} %get-tuple-element.49.grad, bf16[4096,640]{1,0:T(8,128)(2,1)S(1)} %get-tuple-element.43.refs_16_.head), custom_call_target="tpu_custom_call" | custom-call | flops 2013265920 | bytes 10485760 | tf_op jit(solution)/shard_map/pallas_call | solution.py:359
  106.6 1.8 %collective-permute-start.21 = (bf16[2,48,2048]{2,1,0:T(8,128)(2,1)S(1)}, bf16[2,48,2048]{2,1,0:T(8,128)(2,1)S(1)}, u32[]{:S(2)}, u32[]{:S(2)}) collective-permute-start(bf16[2,48,2048]{2,1,0:T(8,128)(2,1)S(1)} %get-tuple-element.58), channel_id=1, source_target_pairs={{16,0},{65,1},{18,2},{67,3},{20,4},{69,5},{22,6},{71,7},{24,8},{73... | collective-permute-start | bytes 1179656 | tf_op jit(solution)/shard_map/ppermute | solution.py:44
  108.4 4.4 %shard_map.98 = (bf16[4096,640]{1,0:T(8,128)(2,1)}, f32[8,128]{1,0:T(8,128)S(1)}) custom-call(bf16[768,4096]{1,0:T(8,128)(2,1)S(1)} %get-tuple-element.54.hidden, bf16[768,640]{1,0:T(8,128)(2,1)S(1)} %get-tuple-element.49.grad, f32[8,128]{1,0:T(8,128)S(1)} %get-tuple-element.55.refs_0_), custom_call_target="tpu_custom_call" | custom-call | flops 2013265920 | bytes 6291456 | tf_op jit(solution)/shard_map/pallas_call | solution.py:404
  112.9 2.8 %collective-permute-start.24 = (bf16[2,48,2048]{2,1,0:T(8,128)(2,1)S(1)}, bf16[2,48,2048]{2,1,0:T(8,128)(2,1)S(1)}, u32[]{:S(2)}, u32[]{:S(2)}) collective-permute-start(bf16[2,48,2048]{2,1,0:T(8,128)(2,1)S(1)} %get-tuple-element.63), channel_id=1, source_target_pairs={{16,0},{65,1},{18,2},{67,3},{20,4},{69,5},{22,6},{71,7},{24,8},{73... | collective-permute-start | bytes 1179656 | tf_op jit(solution)/shard_map/ppermute | solution.py:44
  116.3 4.4 %shard_map.101 = (bf16[4096,640]{1,0:T(8,128)(2,1)}, f32[8,128]{1,0:T(8,128)S(1)}) custom-call(bf16[768,4096]{1,0:T(8,128)(2,1)S(1)} %get-tuple-element.54.hidden, bf16[768,640]{1,0:T(8,128)(2,1)S(1)} %get-tuple-element.49.grad, f32[8,128]{1,0:T(8,128)S(1)} %get-tuple-element.64.refs_0_, ...), custom_call_target="tpu_custom_call", output_to_operand_aliasing={{0}: (3, {})} | custom-call | flops 2013265920 | bytes 6291456 | tf_op jit(solution)/shard_map/pallas_call | solution.py:404
  120.8 3.7 %collective-permute-done.20.refs_1_ = bf16[2,48,2048]{2,1,0:T(8,128)(2,1)S(1)} collective-permute-done((bf16[2,48,2048]{2,1,0:T(8,128)(2,1)S(1)}, bf16[2,48,2048]{2,1,0:T(8,128)(2,1)S(1)}, u32[]{:S(2)}, u32[]{:S(2)}) %collective-permute-start.20) | collective-permute-done | bytes 393248 | tf_op jit(solution)/shard_map/ppermute | solution.py:44
  124.8 2.7 %collective-permute-start.26 = (bf16[48,2048]{1,0:T(8,128)(2,1)S(1)}, bf16[48,2048]{1,0:T(8,128)(2,1)S(1)}, u32[]{:S(2)}, u32[]{:S(2)}) collective-permute-start(bf16[48,2048]{1,0:T(8,128)(2,1)S(1)} %get-tuple-element.69), channel_id=1, source_target_pairs={{64,0},{17,1},{66,2},{19,3},{68,4},{21,5},{70,6},{23,7},{72,8},{25... | collective-permute-start | bytes 589832 | tf_op jit(solution)/shard_map/ppermute | solution.py:44
  127.5 3.1 %collective-permute-done.25.b = bf16[48,2048]{1,0:T(8,128)(2,1)S(1)} collective-permute-done((bf16[48,2048]{1,0:T(8,128)(2,1)S(1)}, bf16[48,2048]{1,0:T(8,128)(2,1)S(1)}, u32[]{:S(2)}, u32[]{:S(2)}) %collective-permute-start.25) | collective-permute-done | bytes 196640 | tf_op jit(solution)/shard_map/ppermute | solution.py:44
  130.5 1.7 %collective-permute-done.26.c = bf16[48,2048]{1,0:T(8,128)(2,1)S(1)} collective-permute-done((bf16[48,2048]{1,0:T(8,128)(2,1)S(1)}, bf16[48,2048]{1,0:T(8,128)(2,1)S(1)}, u32[]{:S(2)}, u32[]{:S(2)}) %collective-permute-start.26) | collective-permute-done | bytes 196640 | tf_op jit(solution)/shard_map/ppermute | solution.py:44
  132.2 1.3 collective-permute-done.27.d
  134.4 7.6 %all-to-all-start.3 = ((bf16[16,48,128]{2,1,0:T(8,128)(2,1)}), bf16[16,48,128]{2,1,0:T(8,128)(2,1)S(1)}, u32[]{:S(2)}, u32[]{:S(2)}) async-start(bf16[16,48,128]{2,1,0:T(8,128)(2,1)} %shard_map.103), calls=%async_computation.3 | async-start | bytes 393216 | tf_op jit(solution)/shard_map/all_to_all | solution.py:519
  142.5 9.9 %all-to-all-done.3.parts = bf16[16,48,128]{2,1,0:T(8,128)(2,1)S(1)} async-done(((bf16[16,48,128]{2,1,0:T(8,128)(2,1)}), bf16[16,48,128]{2,1,0:T(8,128)(2,1)S(1)}, u32[]{:S(2)}, u32[]{:S(2)}) %all-to-all-start.3) | async-done | bytes 196640 | tf_op jit(solution)/shard_map/all_to_all | solution.py:519
  (65 shorter events, 18.9 us)
Async XLA Ops:
  3.3 21.7 %all-to-all-start = ((bf16[16,64,128]{2,1,0:T(8,128)(2,1)}), bf16[16,64,128]{2,1,0:T(8,128)(2,1)S(1)}, u32[]{:S(2)}, u32[]{:S(2)}) async-start(bf16[16,64,128]{2,1,0:T(8,128)(2,1)} %shard_map.85), calls=%async_computation | async-start | bytes 524288 | tf_op jit(solution)/shard_map/all_to_all | solution.py:486
  25.7 8.4 %collective-permute-start.2 = (bf16[48,2176]{1,0:T(8,128)(2,1)S(1)}, bf16[48,2176]{1,0:T(8,128)(2,1)S(1)}, u32[]{:S(2)}, u32[]{:S(2)}) collective-permute-start(bf16[48,2176]{1,0:T(8,128)(2,1)S(1)} %shard_map.86.a), channel_id=1, source_target_pairs={{128,0},{33,1},{130,2},{35,3},{132,4},{37,5},{134,6},{39,7},{136,8... | collective-permute-start | bytes 626696 | tf_op jit(solution)/shard_map/ppermute | solution.py:44
  28.6 6.2 %collective-permute-start.1 = (bf16[48,2176]{1,0:T(8,128)(2,1)S(1)}, bf16[48,2176]{1,0:T(8,128)(2,1)S(1)}, u32[]{:S(2)}, u32[]{:S(2)}) collective-permute-start(bf16[48,2176]{1,0:T(8,128)(2,1)S(1)} %shard_map.86.a), channel_id=1, source_target_pairs={{192,0},{49,1},{194,2},{51,3},{196,4},{53,5},{198,6},{55,7},{200,8... | collective-permute-start | bytes 626696 | tf_op jit(solution)/shard_map/ppermute | solution.py:44
  28.9 5.8 %collective-permute-start = (bf16[48,2176]{1,0:T(8,128)(2,1)S(1)}, bf16[48,2176]{1,0:T(8,128)(2,1)S(1)}, u32[]{:S(2)}, u32[]{:S(2)}) collective-permute-start(bf16[48,2176]{1,0:T(8,128)(2,1)S(1)} %shard_map.86.a), channel_id=1, source_target_pairs={{64,0},{17,1},{66,2},{19,3},{68,4},{21,5},{70,6},{23,7},{72,8},{25... | collective-permute-start | bytes 626696 | tf_op jit(solution)/shard_map/ppermute | solution.py:44
  34.8 2.3 %collective-permute-start.3 = (bf16[2,48,2176]{2,1,0:T(8,128)(2,1)S(1)}, bf16[2,48,2176]{2,1,0:T(8,128)(2,1)S(1)}, u32[]{:S(2)}, u32[]{:S(2)}) collective-permute-start(bf16[2,48,2176]{2,1,0:T(8,128)(2,1)S(1)} %get-tuple-element.39.low), channel_id=1, source_target_pairs={{1,0},{0,1},{3,2},{2,3},{5,4},{4,5},{7,6},{6,7},{9,8},{8,9},{11,10... | collective-permute-start | bytes 1253384 | tf_op jit(solution)/shard_map/ppermute | solution.py:44
  35.7 2.0 %collective-permute-start.4 = (bf16[2,48,2176]{2,1,0:T(8,128)(2,1)S(1)}, bf16[2,48,2176]{2,1,0:T(8,128)(2,1)S(1)}, u32[]{:S(2)}, u32[]{:S(2)}) collective-permute-start(bf16[2,48,2176]{2,1,0:T(8,128)(2,1)S(1)} %get-tuple-element.40.high), channel_id=1, source_target_pairs={{1,0},{0,1},{3,2},{2,3},{5,4},{4,5},{7,6},{6,7},{9,8},{8,9},{11,10... | collective-permute-start | bytes 1253384 | tf_op jit(solution)/shard_map/ppermute | solution.py:44
  37.8 8.8 %collective-permute-start.7 = (bf16[2,48,2176]{2,1,0:T(8,128)(2,1)S(1)}, bf16[2,48,2176]{2,1,0:T(8,128)(2,1)S(1)}, u32[]{:S(2)}, u32[]{:S(2)}) collective-permute-start(bf16[2,48,2176]{2,1,0:T(8,128)(2,1)S(1)} %get-tuple-element.41.refs_0_), channel_id=1, source_target_pairs={{48,0},{193,1},{50,2},{195,3},{52,4},{197,5},{54,6},{199,7},{56,8}... | collective-permute-start | bytes 1253384 | tf_op jit(solution)/shard_map/ppermute | solution.py:44
  38.7 8.8 %collective-permute-start.5 = (bf16[2,48,2176]{2,1,0:T(8,128)(2,1)S(1)}, bf16[2,48,2176]{2,1,0:T(8,128)(2,1)S(1)}, u32[]{:S(2)}, u32[]{:S(2)}) collective-permute-start(bf16[2,48,2176]{2,1,0:T(8,128)(2,1)S(1)} %get-tuple-element.41.refs_0_), channel_id=1, source_target_pairs={{16,0},{65,1},{18,2},{67,3},{20,4},{69,5},{22,6},{71,7},{24,8},{73... | collective-permute-start | bytes 1253384 | tf_op jit(solution)/shard_map/ppermute | solution.py:44
  40.9 10.1 %collective-permute-start.8 = (bf16[2,48,2176]{2,1,0:T(8,128)(2,1)S(1)}, bf16[2,48,2176]{2,1,0:T(8,128)(2,1)S(1)}, u32[]{:S(2)}, u32[]{:S(2)}) collective-permute-start(bf16[2,48,2176]{2,1,0:T(8,128)(2,1)S(1)} %get-tuple-element.42.refs_1_), channel_id=1, source_target_pairs={{48,0},{193,1},{50,2},{195,3},{52,4},{197,5},{54,6},{199,7},{56,8}... | collective-permute-start | bytes 1253384 | tf_op jit(solution)/shard_map/ppermute | solution.py:44
  40.9 11.3 %collective-permute-start.6 = (bf16[2,48,2176]{2,1,0:T(8,128)(2,1)S(1)}, bf16[2,48,2176]{2,1,0:T(8,128)(2,1)S(1)}, u32[]{:S(2)}, u32[]{:S(2)}) collective-permute-start(bf16[2,48,2176]{2,1,0:T(8,128)(2,1)S(1)} %get-tuple-element.42.refs_1_), channel_id=1, source_target_pairs={{16,0},{65,1},{18,2},{67,3},{20,4},{69,5},{22,6},{71,7},{24,8},{73... | collective-permute-start | bytes 1253384 | tf_op jit(solution)/shard_map/ppermute | solution.py:44
  46.5 5.7 %collective-permute-start.13 = (bf16[2,48,2176]{2,1,0:T(8,128)(2,1)S(1)}, bf16[2,48,2176]{2,1,0:T(8,128)(2,1)S(1)}, u32[]{:S(2)}, u32[]{:S(2)}) collective-permute-start(bf16[2,48,2176]{2,1,0:T(8,128)(2,1)S(1)} %collective-permute-done.7.refs_4_), channel_id=1, source_target_pairs={{1,0},{0,1},{3,2},{2,3},{5,4},{4,5},{7,6},{6,7},{9,8},{8,9},{11,10... | collective-permute-start | bytes 1253384 | tf_op jit(solution)/shard_map/ppermute | solution.py:44
  47.5 7.9 %collective-permute-start.9 = (bf16[2,48,2176]{2,1,0:T(8,128)(2,1)S(1)}, bf16[2,48,2176]{2,1,0:T(8,128)(2,1)S(1)}, u32[]{:S(2)}, u32[]{:S(2)}) collective-permute-start(bf16[2,48,2176]{2,1,0:T(8,128)(2,1)S(1)} %collective-permute-done.5.refs_2_), channel_id=1, source_target_pairs={{16,0},{65,1},{18,2},{67,3},{20,4},{69,5},{22,6},{71,7},{24,8},{73... | collective-permute-start | bytes 1253384 | tf_op jit(solution)/shard_map/ppermute | solution.py:44
  51.0 8.4 %collective-permute-start.10 = (bf16[2,48,2176]{2,1,0:T(8,128)(2,1)S(1)}, bf16[2,48,2176]{2,1,0:T(8,128)(2,1)S(1)}, u32[]{:S(2)}, u32[]{:S(2)}) collective-permute-start(bf16[2,48,2176]{2,1,0:T(8,128)(2,1)S(1)} %collective-permute-done.8.refs_5_), channel_id=1, source_target_pairs={{48,0},{193,1},{50,2},{195,3},{52,4},{197,5},{54,6},{199,7},{56,8}... | collective-permute-start | bytes 1253384 | tf_op jit(solution)/shard_map/ppermute | solution.py:44
  51.0 10.2 %collective-permute-start.11 = (bf16[2,48,2176]{2,1,0:T(8,128)(2,1)S(1)}, bf16[2,48,2176]{2,1,0:T(8,128)(2,1)S(1)}, u32[]{:S(2)}, u32[]{:S(2)}) collective-permute-start(bf16[2,48,2176]{2,1,0:T(8,128)(2,1)S(1)} %collective-permute-done.5.refs_2_), channel_id=1, source_target_pairs={{1,0},{0,1},{3,2},{2,3},{5,4},{4,5},{7,6},{6,7},{9,8},{8,9},{11,10... | collective-permute-start | bytes 1253384 | tf_op jit(solution)/shard_map/ppermute | solution.py:44
  52.3 9.0 %collective-permute-start.14 = (bf16[2,48,2176]{2,1,0:T(8,128)(2,1)S(1)}, bf16[2,48,2176]{2,1,0:T(8,128)(2,1)S(1)}, u32[]{:S(2)}, u32[]{:S(2)}) collective-permute-start(bf16[2,48,2176]{2,1,0:T(8,128)(2,1)S(1)} %collective-permute-done.8.refs_5_), channel_id=1, source_target_pairs={{1,0},{0,1},{3,2},{2,3},{5,4},{4,5},{7,6},{6,7},{9,8},{8,9},{11,10... | collective-permute-start | bytes 1253384 | tf_op jit(solution)/shard_map/ppermute | solution.py:44
  52.3 9.0 %collective-permute-start.12 = (bf16[2,48,2176]{2,1,0:T(8,128)(2,1)S(1)}, bf16[2,48,2176]{2,1,0:T(8,128)(2,1)S(1)}, u32[]{:S(2)}, u32[]{:S(2)}) collective-permute-start(bf16[2,48,2176]{2,1,0:T(8,128)(2,1)S(1)} %collective-permute-done.6.refs_3_), channel_id=1, source_target_pairs={{1,0},{0,1},{3,2},{2,3},{5,4},{4,5},{7,6},{6,7},{9,8},{8,9},{11,10... | collective-permute-start | bytes 1253384 | tf_op jit(solution)/shard_map/ppermute | solution.py:44
  55.4 5.8 %collective-permute-start.15 = (bf16[2,48,2176]{2,1,0:T(8,128)(2,1)S(1)}, bf16[2,48,2176]{2,1,0:T(8,128)(2,1)S(1)}, u32[]{:S(2)}, u32[]{:S(2)}) collective-permute-start(bf16[2,48,2176]{2,1,0:T(8,128)(2,1)S(1)} %collective-permute-done.9.refs_6_), channel_id=1, source_target_pairs={{1,0},{0,1},{3,2},{2,3},{5,4},{4,5},{7,6},{6,7},{9,8},{8,9},{11,10... | collective-permute-start | bytes 1253384 | tf_op jit(solution)/shard_map/ppermute | solution.py:44
  59.4 3.2 %collective-permute-start.16 = (bf16[2,48,2176]{2,1,0:T(8,128)(2,1)S(1)}, bf16[2,48,2176]{2,1,0:T(8,128)(2,1)S(1)}, u32[]{:S(2)}, u32[]{:S(2)}) collective-permute-start(bf16[2,48,2176]{2,1,0:T(8,128)(2,1)S(1)} %collective-permute-done.10.refs_7_), channel_id=1, source_target_pairs={{1,0},{0,1},{3,2},{2,3},{5,4},{4,5},{7,6},{6,7},{9,8},{8,9},{11,10... | collective-permute-start | bytes 1253384 | tf_op jit(solution)/shard_map/ppermute | solution.py:44
  62.6 31.3 %copy-start.4 = (f32[16]{0:T(128)S(1)}, f32[16]{0:T(128)}, u32[]{:S(2)}) copy-start(f32[16]{0:T(128)} %ref_logps.1) | copy-start | bytes 196
  62.6 31.3 %copy-start.5 = (s32[16]{0:T(128)S(1)}, s32[16]{0:T(128)}, u32[]{:S(2)}) copy-start(s32[16]{0:T(128)} %pairing.1) | copy-start | bytes 196
  97.3 6.4 %collective-permute-start.17 = (bf16[768,1024]{1,0:T(8,128)(2,1)S(1)}, bf16[768,1024]{1,0:T(8,128)(2,1)S(1)}, u32[]{:S(2)}, u32[]{:S(2)}) collective-permute-start(bf16[768,1024]{1,0:T(8,128)(2,1)S(1)} %get-tuple-element.50), channel_id=1, source_target_pairs={{1,0},{0,1},{3,2},{2,3},{5,4},{4,5},{7,6},{6,7},{9,8},{8,9},{11,10... | collective-permute-start | bytes 4718600 | tf_op jit(solution)/shard_map/ppermute | solution.py:44
  100.2 3.7 %collective-permute-start.18 = (bf16[768,1024]{1,0:T(8,128)(2,1)S(1)}, bf16[768,1024]{1,0:T(8,128)(2,1)S(1)}, u32[]{:S(2)}, u32[]{:S(2)}) collective-permute-start(bf16[768,1024]{1,0:T(8,128)(2,1)S(1)} %shard_map.95), channel_id=1, source_target_pairs={{1,0},{0,1},{3,2},{2,3},{5,4},{4,5},{7,6},{6,7},{9,8},{8,9},{11,10... | collective-permute-start | bytes 4718600 | tf_op jit(solution)/shard_map/ppermute | solution.py:44
  105.1 7.8 %collective-permute-start.23 = (bf16[2,48,2048]{2,1,0:T(8,128)(2,1)S(1)}, bf16[2,48,2048]{2,1,0:T(8,128)(2,1)S(1)}, u32[]{:S(2)}, u32[]{:S(2)}) collective-permute-start(bf16[2,48,2048]{2,1,0:T(8,128)(2,1)S(1)} %get-tuple-element.62), channel_id=1, source_target_pairs={{16,0},{65,1},{18,2},{67,3},{20,4},{69,5},{22,6},{71,7},{24,8},{73... | collective-permute-start | bytes 1179656 | tf_op jit(solution)/shard_map/ppermute | solution.py:44
  105.7 10.0 %collective-permute-start.19 = (bf16[2,48,2048]{2,1,0:T(8,128)(2,1)S(1)}, bf16[2,48,2048]{2,1,0:T(8,128)(2,1)S(1)}, u32[]{:S(2)}, u32[]{:S(2)}) collective-permute-start(bf16[2,48,2048]{2,1,0:T(8,128)(2,1)S(1)} %get-tuple-element.53), channel_id=1, source_target_pairs={{48,0},{193,1},{50,2},{195,3},{52,4},{197,5},{54,6},{199,7},{56,8}... | collective-permute-start | bytes 1179656 | tf_op jit(solution)/shard_map/ppermute | solution.py:44
  106.6 14.2 %collective-permute-start.21 = (bf16[2,48,2048]{2,1,0:T(8,128)(2,1)S(1)}, bf16[2,48,2048]{2,1,0:T(8,128)(2,1)S(1)}, u32[]{:S(2)}, u32[]{:S(2)}) collective-permute-start(bf16[2,48,2048]{2,1,0:T(8,128)(2,1)S(1)} %get-tuple-element.58), channel_id=1, source_target_pairs={{16,0},{65,1},{18,2},{67,3},{20,4},{69,5},{22,6},{71,7},{24,8},{73... | collective-permute-start | bytes 1179656 | tf_op jit(solution)/shard_map/ppermute | solution.py:44
  108.4 12.4 %collective-permute-start.22 = (bf16[2,48,2048]{2,1,0:T(8,128)(2,1)S(1)}, bf16[2,48,2048]{2,1,0:T(8,128)(2,1)S(1)}, u32[]{:S(2)}, u32[]{:S(2)}) collective-permute-start(bf16[2,48,2048]{2,1,0:T(8,128)(2,1)S(1)} %get-tuple-element.60), channel_id=1, source_target_pairs={{48,0},{193,1},{50,2},{195,3},{52,4},{197,5},{54,6},{199,7},{56,8}... | collective-permute-start | bytes 1179656 | tf_op jit(solution)/shard_map/ppermute | solution.py:44
  112.9 7.9 %collective-permute-start.24 = (bf16[2,48,2048]{2,1,0:T(8,128)(2,1)S(1)}, bf16[2,48,2048]{2,1,0:T(8,128)(2,1)S(1)}, u32[]{:S(2)}, u32[]{:S(2)}) collective-permute-start(bf16[2,48,2048]{2,1,0:T(8,128)(2,1)S(1)} %get-tuple-element.63), channel_id=1, source_target_pairs={{16,0},{65,1},{18,2},{67,3},{20,4},{69,5},{22,6},{71,7},{24,8},{73... | collective-permute-start | bytes 1179656 | tf_op jit(solution)/shard_map/ppermute | solution.py:44
  116.3 8.1 %collective-permute-start.20 = (bf16[2,48,2048]{2,1,0:T(8,128)(2,1)S(1)}, bf16[2,48,2048]{2,1,0:T(8,128)(2,1)S(1)}, u32[]{:S(2)}, u32[]{:S(2)}) collective-permute-start(bf16[2,48,2048]{2,1,0:T(8,128)(2,1)S(1)} %get-tuple-element.57), channel_id=1, source_target_pairs={{48,0},{193,1},{50,2},{195,3},{52,4},{197,5},{54,6},{199,7},{56,8}... | collective-permute-start | bytes 1179656 | tf_op jit(solution)/shard_map/ppermute | solution.py:44
  124.7 5.8 %collective-permute-start.25 = (bf16[48,2048]{1,0:T(8,128)(2,1)S(1)}, bf16[48,2048]{1,0:T(8,128)(2,1)S(1)}, u32[]{:S(2)}, u32[]{:S(2)}) collective-permute-start(bf16[48,2048]{1,0:T(8,128)(2,1)S(1)} %get-tuple-element.68), channel_id=1, source_target_pairs={{192,0},{49,1},{194,2},{51,3},{196,4},{53,5},{198,6},{55,7},{200,8... | collective-permute-start | bytes 589832 | tf_op jit(solution)/shard_map/ppermute | solution.py:44
  124.8 7.4 %collective-permute-start.26 = (bf16[48,2048]{1,0:T(8,128)(2,1)S(1)}, bf16[48,2048]{1,0:T(8,128)(2,1)S(1)}, u32[]{:S(2)}, u32[]{:S(2)}) collective-permute-start(bf16[48,2048]{1,0:T(8,128)(2,1)S(1)} %get-tuple-element.69), channel_id=1, source_target_pairs={{64,0},{17,1},{66,2},{19,3},{68,4},{21,5},{70,6},{23,7},{72,8},{25... | collective-permute-start | bytes 589832 | tf_op jit(solution)/shard_map/ppermute | solution.py:44
  127.5 6.0 %collective-permute-start.27 = (bf16[48,2048]{1,0:T(8,128)(2,1)S(1)}, bf16[48,2048]{1,0:T(8,128)(2,1)S(1)}, u32[]{:S(2)}, u32[]{:S(2)}) collective-permute-start(bf16[48,2048]{1,0:T(8,128)(2,1)S(1)} %get-tuple-element.70), channel_id=1, source_target_pairs={{128,0},{33,1},{130,2},{35,3},{132,4},{37,5},{134,6},{39,7},{136,8... | collective-permute-start | bytes 589832 | tf_op jit(solution)/shard_map/ppermute | solution.py:44
  134.4 17.9 %all-to-all-start.3 = ((bf16[16,48,128]{2,1,0:T(8,128)(2,1)}), bf16[16,48,128]{2,1,0:T(8,128)(2,1)S(1)}, u32[]{:S(2)}, u32[]{:S(2)}) async-start(bf16[16,48,128]{2,1,0:T(8,128)(2,1)} %shard_map.103), calls=%async_computation.3 | async-start | bytes 393216 | tf_op jit(solution)/shard_map/all_to_all | solution.py:519
  (4 other events, 35.2 us)

commit v5 on v4

--- a/solution.py
+++ b/solution.py
@@ -104,7 +104,7 @@
 
 def first_message(targets, hidden):
     return call(
-        first_message_kernel, shape((16, 64, 128), bf16), [SMEM, VMEM], [pltpu.VMEM((48, 128), f32)]
+        first_message_kernel, shape((16, 64, 128), bf16), [SMEM, VMEM], [pltpu.VMEM((48, 128), f32)], vmem=56
     )(targets, hidden)
 
 
@@ -127,21 +127,23 @@
     )(ids, parts)
 
 
-def join_blocks_kernel(a, b, c, d, after, low, high):
+def join_blocks_kernel(a, b, c, d, after, low, high, mark):
+    mark[...] = jnp.zeros_like(mark)
     low[0], low[1], high[0], high[1] = a[...], b[...], c[...], d[...]
 
 
 def join_blocks(*blocks):
-    return call(join_blocks_kernel, [shape((2, WIN, WIDE), bf16)] * 2, [VMEM] * 5)(*blocks)
-
-
-def gate_kernel(low, high, first, second, out_low, out_high):
+    outs = [shape((2, WIN, WIDE), bf16)] * 2 + [shape((8, 128), f32)]
+    return call(join_blocks_kernel, outs, [VMEM] * 5)(*blocks)
+
+
+def gate_kernel(low, high, after, out_low, out_high):
     out_low[...] = low[...]
     out_high[...] = high[...]
 
 
-def gate(low, high, *marks):
-    return call(gate_kernel, [shape(low.shape, low.dtype)] * 2, [VMEM] * 4)(low, high, *marks)
+def gate(low, high, after):
+    return call(gate_kernel, [shape(low.shape, low.dtype)] * 2, [VMEM] * 3)(low, high, after)
 
 
 def columns_of(rows):
@@ -486,14 +488,13 @@
     parts = lax.all_to_all(first_message(targets, hidden), ("z", "c"), 0, 0, tiled=True)
     block = join_window(ids, parts)
     head, mark = load_head(head_weight)
-    low, high = join_blocks(block, *(fetch(block, middle(o)) for o in OFF[1:]), mark)
-    other = [fetch(low, near), fetch(high, near)]
-    low, high = gate(low, high, *other)
+    low, high, mark = join_blocks(block, *(fetch(block, middle(o)) for o in OFF[1:]), mark)
+    low, high = gate(low, high, fetch(mark, near))
     ahead_low, back_high = fetch(low, final(1)), fetch(high, final(-1))
     ahead_high, back_low = fetch(high, final(1)), fetch(low, final(-1))
     far_low, far_high = fetch(ahead_low, final(1)), fetch(back_high, final(-1))
     own = [low, high, ahead_low, ahead_high, back_low, back_high, far_low, far_high]
-    other += [fetch(v, near) for v in own[2:]]
+    other = [fetch(v, near) for v in own]
 
     rows, logits, stats, target = local_logits(ids, own, other, head)
     stats = merge(exchange(stats, ("z", "c")))

time: 153 us -> 151 us (0.987)
  waiting for transfers between devices: 44.2 us -> 42.6 us
    ppermute x28 -> x29, waiting for transfers between devices: 22.7 us -> 21.2 us  [fetch(): return lax.ppermute(value, AXES, pairs)]
    unnamed x12 -> x8, local copies, waits for them, and re-layouts: 3.9 us -> 2.5 us
    ppermute x28 -> x29, starting transfers between devices: 31.2 us -> 31.7 us  [fetch(): return lax.ppermute(value, AXES, pairs)]
  transfers between devices with their start and end apart: 30 -> 31, of which waited for: 15 -> 14; matrix products, arithmetic and copies ran while one was open for 0% -> 0% of each run, Pallas kernels for 10% -> 10%
where the time goes in v5:
time: 151 us
  starting transfers between devices  49.3 us (33%)
  waiting for transfers between devices  42.6 us (28%)
  Pallas kernels  30.6 us (20%)
  blocking collectives  24.2 us (16%)
  local copies, waits for them, and re-layouts  3.11 us (2%)
    ppermute x29, starting transfers between devices, fetch(): return lax.ppermute(value, AXES, pairs)  31.7 us
    ppermute x29, waiting for transfers between devices, fetch(): return lax.ppermute(value, AXES, pairs)  21.2 us
    all_to_all x1, blocking collectives, exchange(): lax.all_to_all(jnp.broadcast_to(value[None], (16,) + value.shape), axes,...  12.7 us
    all_to_all x1, waiting for transfers between devices, local(): lax.all_to_all(first_message(targets, hidden), ('z', 'c'), 0, 0, tiled=True)  11.6 us
    all_to_all x1, blocking collectives, local(): stats = lax.all_to_all(stats, ('y', 'x'), 0, 0, tiled=True)  11.6 us
    all_to_all x1, starting transfers between devices, local(): lax.all_to_all(first_message(targets, hidden), ('z', 'c'), 0, 0, tiled=True)  9.98 us
    all_to_all x1, waiting for transfers between devices, local(): grad_hidden = finish(lax.all_to_all(parts, ('z', 'c'), 0, 0, tiled=True))  9.87 us
    pallas_call x2, Pallas kernels, grad_head_half(): pl.pallas_call(head_kernel, grid=(steps,), in_specs=[pl.BlockSpec((TOKENS...  8.76 us
  transfers between devices with their start and end apart: 31, of which 14 were waited for; matrix products, arithmetic and copies ran while one was open for 0% of the time, Pallas kernels for 10%

profile of v5, /device:TPU:1, one launch (start us, length us, event | category | flops | bytes accessed | tf_op | source)
XLA Modules:
  0.0 150.6 jit_solution(15137951935781703463)
XLA Ops:
  0.6 1.5 %shard_map.85 = bf16[16,64,128]{2,1,0:T(8,128)(2,1)} custom-call(s32[3]{0:T(128)} %targets.1, bf16[3,4096]{1,0:T(4,128)(2,1)} %hidden.1), custom_call_target="tpu_custom_call" | custom-call | tf_op jit(solution)/shard_map/pallas_call | solution.py:106
  2.1 10.0 %all-to-all-start = ((bf16[16,64,128]{2,1,0:T(8,128)(2,1)}), bf16[16,64,128]{2,1,0:T(8,128)(2,1)S(1)}, u32[]{:S(2)}, u32[]{:S(2)}) async-start(bf16[16,64,128]{2,1,0:T(8,128)(2,1)} %shard_map.85), calls=%async_computation | async-start | bytes 524288 | tf_op jit(solution)/shard_map/all_to_all | solution.py:488
  12.2 11.6 %all-to-all-done.parts = bf16[16,64,128]{2,1,0:T(8,128)(2,1)S(1)} async-done(((bf16[16,64,128]{2,1,0:T(8,128)(2,1)}), bf16[16,64,128]{2,1,0:T(8,128)(2,1)S(1)}, u32[]{:S(2)}, u32[]{:S(2)}) %all-to-all-start) | async-done | bytes 262176 | tf_op jit(solution)/shard_map/all_to_all | solution.py:488
  24.5 2.8 %collective-permute-start.2 = (bf16[48,2176]{1,0:T(8,128)(2,1)S(1)}, bf16[48,2176]{1,0:T(8,128)(2,1)S(1)}, u32[]{:S(2)}, u32[]{:S(2)}) collective-permute-start(bf16[48,2176]{1,0:T(8,128)(2,1)S(1)} %shard_map.86.a), channel_id=1, source_target_pairs={{128,0},{33,1},{130,2},{35,3},{132,4},{37,5},{134,6},{39,7},{136,8... | collective-permute-start | bytes 626696 | tf_op jit(solution)/shard_map/ppermute | solution.py:44
  27.7 2.4 %collective-permute-start = (bf16[48,2176]{1,0:T(8,128)(2,1)S(1)}, bf16[48,2176]{1,0:T(8,128)(2,1)S(1)}, u32[]{:S(2)}, u32[]{:S(2)}) collective-permute-start(bf16[48,2176]{1,0:T(8,128)(2,1)S(1)} %shard_map.86.a), channel_id=1, source_target_pairs={{64,0},{17,1},{66,2},{19,3},{68,4},{21,5},{70,6},{23,7},{72,8},{25... | collective-permute-start | bytes 626696 | tf_op jit(solution)/shard_map/ppermute | solution.py:44
  30.1 2.5 %copy-done = bf16[4096,640]{1,0:T(8,128)(2,1)S(1)} copy-done((bf16[4096,640]{1,0:T(8,128)(2,1)S(1)}, bf16[4096,640]{1,0:T(8,128)(2,1)}, u32[]{:S(2)}) %copy-start) | copy-done | bytes 5242904
  36.7 2.2 %collective-permute-start.4 = (bf16[2,48,2176]{2,1,0:T(8,128)(2,1)S(1)}, bf16[2,48,2176]{2,1,0:T(8,128)(2,1)S(1)}, u32[]{:S(2)}, u32[]{:S(2)}) collective-permute-start(bf16[2,48,2176]{2,1,0:T(8,128)(2,1)S(1)} %get-tuple-element.43.refs_0_), channel_id=1, source_target_pairs={{16,0},{65,1},{18,2},{67,3},{20,4},{69,5},{22,6},{71,7},{24,8},{73... | collective-permute-start | bytes 1253384 | tf_op jit(solution)/shard_map/ppermute | solution.py:44
  39.6 3.0 %collective-permute-start.5 = (bf16[2,48,2176]{2,1,0:T(8,128)(2,1)S(1)}, bf16[2,48,2176]{2,1,0:T(8,128)(2,1)S(1)}, u32[]{:S(2)}, u32[]{:S(2)}) collective-permute-start(bf16[2,48,2176]{2,1,0:T(8,128)(2,1)S(1)} %get-tuple-element.44.refs_1_), channel_id=1, source_target_pairs={{16,0},{65,1},{18,2},{67,3},{20,4},{69,5},{22,6},{71,7},{24,8},{73... | collective-permute-start | bytes 1253384 | tf_op jit(solution)/shard_map/ppermute | solution.py:44
  42.5 2.0 %collective-permute-done.6.refs_4_ = bf16[2,48,2176]{2,1,0:T(8,128)(2,1)S(1)} collective-permute-done((bf16[2,48,2176]{2,1,0:T(8,128)(2,1)S(1)}, bf16[2,48,2176]{2,1,0:T(8,128)(2,1)S(1)}, u32[]{:S(2)}, u32[]{:S(2)}) %collective-permute-start.6) | collective-permute-done | bytes 417824 | tf_op jit(solution)/shard_map/ppermute | solution.py:44
  45.3 3.0 %collective-permute-start.8 = (bf16[2,48,2176]{2,1,0:T(8,128)(2,1)S(1)}, bf16[2,48,2176]{2,1,0:T(8,128)(2,1)S(1)}, u32[]{:S(2)}, u32[]{:S(2)}) collective-permute-start(bf16[2,48,2176]{2,1,0:T(8,128)(2,1)S(1)} %collective-permute-done.4.refs_2_), channel_id=1, source_target_pairs={{16,0},{65,1},{18,2},{67,3},{20,4},{69,5},{22,6},{71,7},{24,8},{73... | collective-permute-start | bytes 1253384 | tf_op jit(solution)/shard_map/ppermute | solution.py:44
  50.6 2.7 %collective-permute-done.8.refs_6_ = bf16[2,48,2176]{2,1,0:T(8,128)(2,1)S(1)} collective-permute-done((bf16[2,48,2176]{2,1,0:T(8,128)(2,1)S(1)}, bf16[2,48,2176]{2,1,0:T(8,128)(2,1)S(1)}, u32[]{:S(2)}, u32[]{:S(2)}) %collective-permute-start.8) | collective-permute-done | bytes 417824 | tf_op jit(solution)/shard_map/ppermute | solution.py:44
  53.2 1.3 collective-permute-start.16
  54.5 2.9 %collective-permute-done.9.refs_7_ = bf16[2,48,2176]{2,1,0:T(8,128)(2,1)S(1)} collective-permute-done((bf16[2,48,2176]{2,1,0:T(8,128)(2,1)S(1)}, bf16[2,48,2176]{2,1,0:T(8,128)(2,1)S(1)}, u32[]{:S(2)}, u32[]{:S(2)}) %collective-permute-start.9) | collective-permute-done | bytes 417824 | tf_op jit(solution)/shard_map/ppermute | solution.py:44
  57.4 1.6 %collective-permute-start.17 = (bf16[2,48,2176]{2,1,0:T(8,128)(2,1)S(1)}, bf16[2,48,2176]{2,1,0:T(8,128)(2,1)S(1)}, u32[]{:S(2)}, u32[]{:S(2)}) collective-permute-start(bf16[2,48,2176]{2,1,0:T(8,128)(2,1)S(1)} %collective-permute-done.9.refs_7_), channel_id=1, source_target_pairs={{1,0},{0,1},{3,2},{2,3},{5,4},{4,5},{7,6},{6,7},{9,8},{8,9},{11,10... | collective-permute-start | bytes 1253384 | tf_op jit(solution)/shard_map/ppermute | solution.py:44
  59.0 1.4 collective-permute-done.17.refs_15_
  60.4 7.0 %shard_map.90 = (bf16[768,4096]{1,0:T(8,128)(2,1)S(1)}, f32[768,640]{1,0:T(8,128)S(1)}, f32[2,8,128]{2,1,0:T(8,128)S(1)}, f32[8,128]{1,0:T(8,128)S(1)}) custom-call(s32[5]{0:T(128)S(1)} %stack.23.ids, bf16[2,48,2176]{2,1,0:T(8,128)(2,1)S(1)} %get-tuple-element.43.refs_0_, bf16[2,48,2176]{2,1,0:T(8,128)(2,1)S(1)} %get-tuple-element.44.refs_1_, ...), custom_call_target="tpu_custom_call" | custom-call | flops 4026531840 | bytes 20971520 | tf_op jit(solution)/shard_map/pallas_call | solution.py:215
  67.4 12.7 %all_to_all.20.parts = f32[16,2,8,128]{3,2,1,0:T(8,128)S(1)} all-to-all(f32[16,2,8,128]{3,2,1,0:T(8,128)S(1)} %broadcast_in_dim.2), channel_id=1, replica_groups=mesh['y'=4,'x'=4,'z'=8,'c'=2] {'z','c'}, dimensions={0} | all-to-all | bytes 262144 | tf_op jit(solution)/shard_map/all_to_all | solution.py:235
  80.1 11.6 %all_to_all.21.parts = f32[16,2,8,128]{3,2,1,0:T(8,128)S(1)} all-to-all(f32[16,2,8,128]{3,2,1,0:T(8,128)S(1)} %shard_map.91), channel_id=1, replica_groups=mesh['y'=4,'x'=4,'z'=8,'c'=2] {'y','x'}, dimensions={0} | all-to-all | bytes 262144 | tf_op jit(solution)/shard_map/all_to_all | solution.py:501
  92.5 2.6 %shard_map.93 = (bf16[768,640]{1,0:T(8,128)(2,1)S(1)}, bf16[768,1024]{1,0:T(8,128)(2,1)S(1)}) custom-call(s32[5]{0:T(128)S(1)} %stack.23.ids, f32[768,640]{1,0:T(8,128)S(1)} %get-tuple-element.46.logits, f32[8,128]{1,0:T(8,128)S(1)} %get-tuple-element.48.norm, f32[8,128]{1,0:T(8,128)S(1)} %get-tuple-element.49.weight, ...), custom_call_target="tpu_custom_call" | custom-call | flops 1006632960 | bytes 6291456 | tf_op jit(solution)/shard_map/pallas_call | solution.py:326
  96.0 2.0 %shard_map.95 = bf16[768,1024]{1,0:T(8,128)(2,1)S(1)} custom-call(s32[5]{0:T(128)S(1)} %stack.23.ids, bf16[768,640]{1,0:T(8,128)(2,1)S(1)} %get-tuple-element.51.grad, bf16[4096,640]{1,0:T(8,128)(2,1)S(1)} %get-tuple-element.45.refs_16_.head), custom_call_target="tpu_custom_call" | custom-call | flops 2013265920 | bytes 16777216 | tf_op jit(solution)/shard_map/pallas_call | solution.py:337
  98.3 3.2 %shard_map.94.own = f32[768,2048]{1,0:T(8,128)S(1)} custom-call(s32[5]{0:T(128)S(1)} %stack.23.ids, bf16[768,640]{1,0:T(8,128)(2,1)S(1)} %get-tuple-element.51.grad, bf16[4096,640]{1,0:T(8,128)(2,1)S(1)} %get-tuple-element.45.refs_16_.head), custom_call_target="tpu_custom_call" | custom-call | flops 2013265920 | bytes 10485760 | tf_op jit(solution)/shard_map/pallas_call | solution.py:361
  104.3 1.8 %collective-permute-start.22 = (bf16[2,48,2048]{2,1,0:T(8,128)(2,1)S(1)}, bf16[2,48,2048]{2,1,0:T(8,128)(2,1)S(1)}, u32[]{:S(2)}, u32[]{:S(2)}) collective-permute-start(bf16[2,48,2048]{2,1,0:T(8,128)(2,1)S(1)} %get-tuple-element.60), channel_id=1, source_target_pairs={{16,0},{65,1},{18,2},{67,3},{20,4},{69,5},{22,6},{71,7},{24,8},{73... | collective-permute-start | bytes 1179656 | tf_op jit(solution)/shard_map/ppermute | solution.py:44
  106.1 4.4 %shard_map.98 = (bf16[4096,640]{1,0:T(8,128)(2,1)}, f32[8,128]{1,0:T(8,128)S(1)}) custom-call(bf16[768,4096]{1,0:T(8,128)(2,1)S(1)} %get-tuple-element.56.hidden, bf16[768,640]{1,0:T(8,128)(2,1)S(1)} %get-tuple-element.51.grad, f32[8,128]{1,0:T(8,128)S(1)} %get-tuple-element.57.refs_0_), custom_call_target="tpu_custom_call" | custom-call | flops 2013265920 | bytes 6291456 | tf_op jit(solution)/shard_map/pallas_call | solution.py:406
  110.6 2.8 %collective-permute-start.25 = (bf16[2,48,2048]{2,1,0:T(8,128)(2,1)S(1)}, bf16[2,48,2048]{2,1,0:T(8,128)(2,1)S(1)}, u32[]{:S(2)}, u32[]{:S(2)}) collective-permute-start(bf16[2,48,2048]{2,1,0:T(8,128)(2,1)S(1)} %get-tuple-element.65), channel_id=1, source_target_pairs={{16,0},{65,1},{18,2},{67,3},{20,4},{69,5},{22,6},{71,7},{24,8},{73... | collective-permute-start | bytes 1179656 | tf_op jit(solution)/shard_map/ppermute | solution.py:44
  114.0 4.4 %shard_map.101 = (bf16[4096,640]{1,0:T(8,128)(2,1)}, f32[8,128]{1,0:T(8,128)S(1)}) custom-call(bf16[768,4096]{1,0:T(8,128)(2,1)S(1)} %get-tuple-element.56.hidden, bf16[768,640]{1,0:T(8,128)(2,1)S(1)} %get-tuple-element.51.grad, f32[8,128]{1,0:T(8,128)S(1)} %get-tuple-element.66.refs_0_, ...), custom_call_target="tpu_custom_call", output_to_operand_aliasing={{0}: (3, {})} | custom-call | flops 2013265920 | bytes 6291456 | tf_op jit(solution)/shard_map/pallas_call | solution.py:406
  118.4 3.7 %collective-permute-done.21.refs_1_ = bf16[2,48,2048]{2,1,0:T(8,128)(2,1)S(1)} collective-permute-done((bf16[2,48,2048]{2,1,0:T(8,128)(2,1)S(1)}, bf16[2,48,2048]{2,1,0:T(8,128)(2,1)S(1)}, u32[]{:S(2)}, u32[]{:S(2)}) %collective-permute-start.21) | collective-permute-done | bytes 393248 | tf_op jit(solution)/shard_map/ppermute | solution.py:44
  122.4 2.7 %collective-permute-start.27 = (bf16[48,2048]{1,0:T(8,128)(2,1)S(1)}, bf16[48,2048]{1,0:T(8,128)(2,1)S(1)}, u32[]{:S(2)}, u32[]{:S(2)}) collective-permute-start(bf16[48,2048]{1,0:T(8,128)(2,1)S(1)} %get-tuple-element.71), channel_id=1, source_target_pairs={{64,0},{17,1},{66,2},{19,3},{68,4},{21,5},{70,6},{23,7},{72,8},{25... | collective-permute-start | bytes 589832 | tf_op jit(solution)/shard_map/ppermute | solution.py:44
  125.1 3.1 %collective-permute-done.26.b = bf16[48,2048]{1,0:T(8,128)(2,1)S(1)} collective-permute-done((bf16[48,2048]{1,0:T(8,128)(2,1)S(1)}, bf16[48,2048]{1,0:T(8,128)(2,1)S(1)}, u32[]{:S(2)}, u32[]{:S(2)}) %collective-permute-start.26) | collective-permute-done | bytes 196640 | tf_op jit(solution)/shard_map/ppermute | solution.py:44
  128.1 1.7 %collective-permute-done.27.c = bf16[48,2048]{1,0:T(8,128)(2,1)S(1)} collective-permute-done((bf16[48,2048]{1,0:T(8,128)(2,1)S(1)}, bf16[48,2048]{1,0:T(8,128)(2,1)S(1)}, u32[]{:S(2)}, u32[]{:S(2)}) %collective-permute-start.27) | collective-permute-done | bytes 196640 | tf_op jit(solution)/shard_map/ppermute | solution.py:44
  129.8 1.3 collective-permute-done.28.d
  132.0 7.6 %all-to-all-start.3 = ((bf16[16,48,128]{2,1,0:T(8,128)(2,1)}), bf16[16,48,128]{2,1,0:T(8,128)(2,1)S(1)}, u32[]{:S(2)}, u32[]{:S(2)}) async-start(bf16[16,48,128]{2,1,0:T(8,128)(2,1)} %shard_map.103), calls=%async_computation.3 | async-start | bytes 393216 | tf_op jit(solution)/shard_map/all_to_all | solution.py:520
  140.1 9.9 %all-to-all-done.3.parts = bf16[16,48,128]{2,1,0:T(8,128)(2,1)S(1)} async-done(((bf16[16,48,128]{2,1,0:T(8,128)(2,1)}), bf16[16,48,128]{2,1,0:T(8,128)(2,1)S(1)}, u32[]{:S(2)}, u32[]{:S(2)}) %all-to-all-start.3) | async-done | bytes 196640 | tf_op jit(solution)/shard_map/all_to_all | solution.py:520
  (63 shorter events, 17.0 us)
Async XLA Ops:
  2.1 21.7 %all-to-all-start = ((bf16[16,64,128]{2,1,0:T(8,128)(2,1)}), bf16[16,64,128]{2,1,0:T(8,128)(2,1)S(1)}, u32[]{:S(2)}, u32[]{:S(2)}) async-start(bf16[16,64,128]{2,1,0:T(8,128)(2,1)} %shard_map.85), calls=%async_computation | async-start | bytes 524288 | tf_op jit(solution)/shard_map/all_to_all | solution.py:488
  24.5 8.4 %collective-permute-start.2 = (bf16[48,2176]{1,0:T(8,128)(2,1)S(1)}, bf16[48,2176]{1,0:T(8,128)(2,1)S(1)}, u32[]{:S(2)}, u32[]{:S(2)}) collective-permute-start(bf16[48,2176]{1,0:T(8,128)(2,1)S(1)} %shard_map.86.a), channel_id=1, source_target_pairs={{128,0},{33,1},{130,2},{35,3},{132,4},{37,5},{134,6},{39,7},{136,8... | collective-permute-start | bytes 626696 | tf_op jit(solution)/shard_map/ppermute | solution.py:44
  27.4 6.2 %collective-permute-start.1 = (bf16[48,2176]{1,0:T(8,128)(2,1)S(1)}, bf16[48,2176]{1,0:T(8,128)(2,1)S(1)}, u32[]{:S(2)}, u32[]{:S(2)}) collective-permute-start(bf16[48,2176]{1,0:T(8,128)(2,1)S(1)} %shard_map.86.a), channel_id=1, source_target_pairs={{192,0},{49,1},{194,2},{51,3},{196,4},{53,5},{198,6},{55,7},{200,8... | collective-permute-start | bytes 626696 | tf_op jit(solution)/shard_map/ppermute | solution.py:44
  27.7 5.8 %collective-permute-start = (bf16[48,2176]{1,0:T(8,128)(2,1)S(1)}, bf16[48,2176]{1,0:T(8,128)(2,1)S(1)}, u32[]{:S(2)}, u32[]{:S(2)}) collective-permute-start(bf16[48,2176]{1,0:T(8,128)(2,1)S(1)} %shard_map.86.a), channel_id=1, source_target_pairs={{64,0},{17,1},{66,2},{19,3},{68,4},{21,5},{70,6},{23,7},{72,8},{25... | collective-permute-start | bytes 626696 | tf_op jit(solution)/shard_map/ppermute | solution.py:44
  33.6 1.8 %collective-permute-start.3 = (f32[8,128]{1,0:T(8,128)S(1)}, f32[8,128]{1,0:T(8,128)S(1)}, u32[]{:S(2)}, u32[]{:S(2)}) collective-permute-start(f32[8,128]{1,0:T(8,128)S(1)} %get-tuple-element.42), channel_id=1, source_target_pairs={{1,0},{0,1},{3,2},{2,3},{5,4},{4,5},{7,6},{6,7},{9,8},{8,9},{11,10... | collective-permute-start | bytes 12296 | tf_op jit(solution)/shard_map/ppermute | solution.py:44
  35.4 4.1 %collective-permute-start.10 = (bf16[2,48,2176]{2,1,0:T(8,128)(2,1)S(1)}, bf16[2,48,2176]{2,1,0:T(8,128)(2,1)S(1)}, u32[]{:S(2)}, u32[]{:S(2)}) collective-permute-start(bf16[2,48,2176]{2,1,0:T(8,128)(2,1)S(1)} %get-tuple-element.43.refs_0_), channel_id=1, source_target_pairs={{1,0},{0,1},{3,2},{2,3},{5,4},{4,5},{7,6},{6,7},{9,8},{8,9},{11,10... | collective-permute-start | bytes 1253384 | tf_op jit(solution)/shard_map/ppermute | solution.py:44
  35.9 8.7 %collective-permute-start.6 = (bf16[2,48,2176]{2,1,0:T(8,128)(2,1)S(1)}, bf16[2,48,2176]{2,1,0:T(8,128)(2,1)S(1)}, u32[]{:S(2)}, u32[]{:S(2)}) collective-permute-start(bf16[2,48,2176]{2,1,0:T(8,128)(2,1)S(1)} %get-tuple-element.43.refs_0_), channel_id=1, source_target_pairs={{48,0},{193,1},{50,2},{195,3},{52,4},{197,5},{54,6},{199,7},{56,8}... | collective-permute-start | bytes 1253384 | tf_op jit(solution)/shard_map/ppermute | solution.py:44
  36.7 8.6 %collective-permute-start.4 = (bf16[2,48,2176]{2,1,0:T(8,128)(2,1)S(1)}, bf16[2,48,2176]{2,1,0:T(8,128)(2,1)S(1)}, u32[]{:S(2)}, u32[]{:S(2)}) collective-permute-start(bf16[2,48,2176]{2,1,0:T(8,128)(2,1)S(1)} %get-tuple-element.43.refs_0_), channel_id=1, source_target_pairs={{16,0},{65,1},{18,2},{67,3},{20,4},{69,5},{22,6},{71,7},{24,8},{73... | collective-permute-start | bytes 1253384 | tf_op jit(solution)/shard_map/ppermute | solution.py:44
  38.8 10.2 %collective-permute-start.7 = (bf16[2,48,2176]{2,1,0:T(8,128)(2,1)S(1)}, bf16[2,48,2176]{2,1,0:T(8,128)(2,1)S(1)}, u32[]{:S(2)}, u32[]{:S(2)}) collective-permute-start(bf16[2,48,2176]{2,1,0:T(8,128)(2,1)S(1)} %get-tuple-element.44.refs_1_), channel_id=1, source_target_pairs={{48,0},{193,1},{50,2},{195,3},{52,4},{197,5},{54,6},{199,7},{56,8}... | collective-permute-start | bytes 1253384 | tf_op jit(solution)/shard_map/ppermute | solution.py:44
  38.8 10.2 %collective-permute-start.11 = (bf16[2,48,2176]{2,1,0:T(8,128)(2,1)S(1)}, bf16[2,48,2176]{2,1,0:T(8,128)(2,1)S(1)}, u32[]{:S(2)}, u32[]{:S(2)}) collective-permute-start(bf16[2,48,2176]{2,1,0:T(8,128)(2,1)S(1)} %get-tuple-element.44.refs_1_), channel_id=1, source_target_pairs={{1,0},{0,1},{3,2},{2,3},{5,4},{4,5},{7,6},{6,7},{9,8},{8,9},{11,10... | collective-permute-start | bytes 1253384 | tf_op jit(solution)/shard_map/ppermute | solution.py:44
  39.6 10.5 %collective-permute-start.5 = (bf16[2,48,2176]{2,1,0:T(8,128)(2,1)S(1)}, bf16[2,48,2176]{2,1,0:T(8,128)(2,1)S(1)}, u32[]{:S(2)}, u32[]{:S(2)}) collective-permute-start(bf16[2,48,2176]{2,1,0:T(8,128)(2,1)S(1)} %get-tuple-element.44.refs_1_), channel_id=1, source_target_pairs={{16,0},{65,1},{18,2},{67,3},{20,4},{69,5},{22,6},{71,7},{24,8},{73... | collective-permute-start | bytes 1253384 | tf_op jit(solution)/shard_map/ppermute | solution.py:44
  44.6 5.6 %collective-permute-start.14 = (bf16[2,48,2176]{2,1,0:T(8,128)(2,1)S(1)}, bf16[2,48,2176]{2,1,0:T(8,128)(2,1)S(1)}, u32[]{:S(2)}, u32[]{:S(2)}) collective-permute-start(bf16[2,48,2176]{2,1,0:T(8,128)(2,1)S(1)} %collective-permute-done.6.refs_4_), channel_id=1, source_target_pairs={{1,0},{0,1},{3,2},{2,3},{5,4},{4,5},{7,6},{6,7},{9,8},{8,9},{11,10... | collective-permute-start | bytes 1253384 | tf_op jit(solution)/shard_map/ppermute | solution.py:44
  45.3 7.9 %collective-permute-start.8 = (bf16[2,48,2176]{2,1,0:T(8,128)(2,1)S(1)}, bf16[2,48,2176]{2,1,0:T(8,128)(2,1)S(1)}, u32[]{:S(2)}, u32[]{:S(2)}) collective-permute-start(bf16[2,48,2176]{2,1,0:T(8,128)(2,1)S(1)} %collective-permute-done.4.refs_2_), channel_id=1, source_target_pairs={{16,0},{65,1},{18,2},{67,3},{20,4},{69,5},{22,6},{71,7},{24,8},{73... | collective-permute-start | bytes 1253384 | tf_op jit(solution)/shard_map/ppermute | solution.py:44
  49.0 8.4 %collective-permute-start.9 = (bf16[2,48,2176]{2,1,0:T(8,128)(2,1)S(1)}, bf16[2,48,2176]{2,1,0:T(8,128)(2,1)S(1)}, u32[]{:S(2)}, u32[]{:S(2)}) collective-permute-start(bf16[2,48,2176]{2,1,0:T(8,128)(2,1)S(1)} %collective-permute-done.7.refs_5_), channel_id=1, source_target_pairs={{48,0},{193,1},{50,2},{195,3},{52,4},{197,5},{54,6},{199,7},{56,8}... | collective-permute-start | bytes 1253384 | tf_op jit(solution)/shard_map/ppermute | solution.py:44
  49.0 10.0 %collective-permute-start.12 = (bf16[2,48,2176]{2,1,0:T(8,128)(2,1)S(1)}, bf16[2,48,2176]{2,1,0:T(8,128)(2,1)S(1)}, u32[]{:S(2)}, u32[]{:S(2)}) collective-permute-start(bf16[2,48,2176]{2,1,0:T(8,128)(2,1)S(1)} %collective-permute-done.4.refs_2_), channel_id=1, source_target_pairs={{1,0},{0,1},{3,2},{2,3},{5,4},{4,5},{7,6},{6,7},{9,8},{8,9},{11,10... | collective-permute-start | bytes 1253384 | tf_op jit(solution)/shard_map/ppermute | solution.py:44
  50.1 9.0 %collective-permute-start.15 = (bf16[2,48,2176]{2,1,0:T(8,128)(2,1)S(1)}, bf16[2,48,2176]{2,1,0:T(8,128)(2,1)S(1)}, u32[]{:S(2)}, u32[]{:S(2)}) collective-permute-start(bf16[2,48,2176]{2,1,0:T(8,128)(2,1)S(1)} %collective-permute-done.7.refs_5_), channel_id=1, source_target_pairs={{1,0},{0,1},{3,2},{2,3},{5,4},{4,5},{7,6},{6,7},{9,8},{8,9},{11,10... | collective-permute-start | bytes 1253384 | tf_op jit(solution)/shard_map/ppermute | solution.py:44
  50.2 8.9 %collective-permute-start.13 = (bf16[2,48,2176]{2,1,0:T(8,128)(2,1)S(1)}, bf16[2,48,2176]{2,1,0:T(8,128)(2,1)S(1)}, u32[]{:S(2)}, u32[]{:S(2)}) collective-permute-start(bf16[2,48,2176]{2,1,0:T(8,128)(2,1)S(1)} %collective-permute-done.5.refs_3_), channel_id=1, source_target_pairs={{1,0},{0,1},{3,2},{2,3},{5,4},{4,5},{7,6},{6,7},{9,8},{8,9},{11,10... | collective-permute-start | bytes 1253384 | tf_op jit(solution)/shard_map/ppermute | solution.py:44
  53.2 5.8 %collective-permute-start.16 = (bf16[2,48,2176]{2,1,0:T(8,128)(2,1)S(1)}, bf16[2,48,2176]{2,1,0:T(8,128)(2,1)S(1)}, u32[]{:S(2)}, u32[]{:S(2)}) collective-permute-start(bf16[2,48,2176]{2,1,0:T(8,128)(2,1)S(1)} %collective-permute-done.8.refs_6_), channel_id=1, source_target_pairs={{1,0},{0,1},{3,2},{2,3},{5,4},{4,5},{7,6},{6,7},{9,8},{8,9},{11,10... | collective-permute-start | bytes 1253384 | tf_op jit(solution)/shard_map/ppermute | solution.py:44
  57.4 3.0 %collective-permute-start.17 = (bf16[2,48,2176]{2,1,0:T(8,128)(2,1)S(1)}, bf16[2,48,2176]{2,1,0:T(8,128)(2,1)S(1)}, u32[]{:S(2)}, u32[]{:S(2)}) collective-permute-start(bf16[2,48,2176]{2,1,0:T(8,128)(2,1)S(1)} %collective-permute-done.9.refs_7_), channel_id=1, source_target_pairs={{1,0},{0,1},{3,2},{2,3},{5,4},{4,5},{7,6},{6,7},{9,8},{8,9},{11,10... | collective-permute-start | bytes 1253384 | tf_op jit(solution)/shard_map/ppermute | solution.py:44
  60.4 31.3 %copy-start.3 = (s32[16]{0:T(128)S(1)}, s32[16]{0:T(128)}, u32[]{:S(2)}) copy-start(s32[16]{0:T(128)} %pairing.1) | copy-start | bytes 196
  95.1 6.4 %collective-permute-start.18 = (bf16[768,1024]{1,0:T(8,128)(2,1)S(1)}, bf16[768,1024]{1,0:T(8,128)(2,1)S(1)}, u32[]{:S(2)}, u32[]{:S(2)}) collective-permute-start(bf16[768,1024]{1,0:T(8,128)(2,1)S(1)} %get-tuple-element.52), channel_id=1, source_target_pairs={{1,0},{0,1},{3,2},{2,3},{5,4},{4,5},{7,6},{6,7},{9,8},{8,9},{11,10... | collective-permute-start | bytes 4718600 | tf_op jit(solution)/shard_map/ppermute | solution.py:44
  98.0 3.7 %collective-permute-start.19 = (bf16[768,1024]{1,0:T(8,128)(2,1)S(1)}, bf16[768,1024]{1,0:T(8,128)(2,1)S(1)}, u32[]{:S(2)}, u32[]{:S(2)}) collective-permute-start(bf16[768,1024]{1,0:T(8,128)(2,1)S(1)} %shard_map.95), channel_id=1, source_target_pairs={{1,0},{0,1},{3,2},{2,3},{5,4},{4,5},{7,6},{6,7},{9,8},{8,9},{11,10... | collective-permute-start | bytes 4718600 | tf_op jit(solution)/shard_map/ppermute | solution.py:44
  102.8 7.7 %collective-permute-start.24 = (bf16[2,48,2048]{2,1,0:T(8,128)(2,1)S(1)}, bf16[2,48,2048]{2,1,0:T(8,128)(2,1)S(1)}, u32[]{:S(2)}, u32[]{:S(2)}) collective-permute-start(bf16[2,48,2048]{2,1,0:T(8,128)(2,1)S(1)} %get-tuple-element.64), channel_id=1, source_target_pairs={{16,0},{65,1},{18,2},{67,3},{20,4},{69,5},{22,6},{71,7},{24,8},{73... | collective-permute-start | bytes 1179656 | tf_op jit(solution)/shard_map/ppermute | solution.py:44
  103.4 9.9 %collective-permute-start.20 = (bf16[2,48,2048]{2,1,0:T(8,128)(2,1)S(1)}, bf16[2,48,2048]{2,1,0:T(8,128)(2,1)S(1)}, u32[]{:S(2)}, u32[]{:S(2)}) collective-permute-start(bf16[2,48,2048]{2,1,0:T(8,128)(2,1)S(1)} %get-tuple-element.55), channel_id=1, source_target_pairs={{48,0},{193,1},{50,2},{195,3},{52,4},{197,5},{54,6},{199,7},{56,8}... | collective-permute-start | bytes 1179656 | tf_op jit(solution)/shard_map/ppermute | solution.py:44
  104.3 14.0 %collective-permute-start.22 = (bf16[2,48,2048]{2,1,0:T(8,128)(2,1)S(1)}, bf16[2,48,2048]{2,1,0:T(8,128)(2,1)S(1)}, u32[]{:S(2)}, u32[]{:S(2)}) collective-permute-start(bf16[2,48,2048]{2,1,0:T(8,128)(2,1)S(1)} %get-tuple-element.60), channel_id=1, source_target_pairs={{16,0},{65,1},{18,2},{67,3},{20,4},{69,5},{22,6},{71,7},{24,8},{73... | collective-permute-start | bytes 1179656 | tf_op jit(solution)/shard_map/ppermute | solution.py:44
  106.1 12.3 %collective-permute-start.23 = (bf16[2,48,2048]{2,1,0:T(8,128)(2,1)S(1)}, bf16[2,48,2048]{2,1,0:T(8,128)(2,1)S(1)}, u32[]{:S(2)}, u32[]{:S(2)}) collective-permute-start(bf16[2,48,2048]{2,1,0:T(8,128)(2,1)S(1)} %get-tuple-element.62), channel_id=1, source_target_pairs={{48,0},{193,1},{50,2},{195,3},{52,4},{197,5},{54,6},{199,7},{56,8}... | collective-permute-start | bytes 1179656 | tf_op jit(solution)/shard_map/ppermute | solution.py:44
  110.6 7.8 %collective-permute-start.25 = (bf16[2,48,2048]{2,1,0:T(8,128)(2,1)S(1)}, bf16[2,48,2048]{2,1,0:T(8,128)(2,1)S(1)}, u32[]{:S(2)}, u32[]{:S(2)}) collective-permute-start(bf16[2,48,2048]{2,1,0:T(8,128)(2,1)S(1)} %get-tuple-element.65), channel_id=1, source_target_pairs={{16,0},{65,1},{18,2},{67,3},{20,4},{69,5},{22,6},{71,7},{24,8},{73... | collective-permute-start | bytes 1179656 | tf_op jit(solution)/shard_map/ppermute | solution.py:44
  114.0 8.1 %collective-permute-start.21 = (bf16[2,48,2048]{2,1,0:T(8,128)(2,1)S(1)}, bf16[2,48,2048]{2,1,0:T(8,128)(2,1)S(1)}, u32[]{:S(2)}, u32[]{:S(2)}) collective-permute-start(bf16[2,48,2048]{2,1,0:T(8,128)(2,1)S(1)} %get-tuple-element.59), channel_id=1, source_target_pairs={{48,0},{193,1},{50,2},{195,3},{52,4},{197,5},{54,6},{199,7},{56,8}... | collective-permute-start | bytes 1179656 | tf_op jit(solution)/shard_map/ppermute | solution.py:44
  122.3 5.8 %collective-permute-start.26 = (bf16[48,2048]{1,0:T(8,128)(2,1)S(1)}, bf16[48,2048]{1,0:T(8,128)(2,1)S(1)}, u32[]{:S(2)}, u32[]{:S(2)}) collective-permute-start(bf16[48,2048]{1,0:T(8,128)(2,1)S(1)} %get-tuple-element.70), channel_id=1, source_target_pairs={{192,0},{49,1},{194,2},{51,3},{196,4},{53,5},{198,6},{55,7},{200,8... | collective-permute-start | bytes 589832 | tf_op jit(solution)/shard_map/ppermute | solution.py:44
  122.4 7.4 %collective-permute-start.27 = (bf16[48,2048]{1,0:T(8,128)(2,1)S(1)}, bf16[48,2048]{1,0:T(8,128)(2,1)S(1)}, u32[]{:S(2)}, u32[]{:S(2)}) collective-permute-start(bf16[48,2048]{1,0:T(8,128)(2,1)S(1)} %get-tuple-element.71), channel_id=1, source_target_pairs={{64,0},{17,1},{66,2},{19,3},{68,4},{21,5},{70,6},{23,7},{72,8},{25... | collective-permute-start | bytes 589832 | tf_op jit(solution)/shard_map/ppermute | solution.py:44
  125.1 6.0 %collective-permute-start.28 = (bf16[48,2048]{1,0:T(8,128)(2,1)S(1)}, bf16[48,2048]{1,0:T(8,128)(2,1)S(1)}, u32[]{:S(2)}, u32[]{:S(2)}) collective-permute-start(bf16[48,2048]{1,0:T(8,128)(2,1)S(1)} %get-tuple-element.72), channel_id=1, source_target_pairs={{128,0},{33,1},{130,2},{35,3},{132,4},{37,5},{134,6},{39,7},{136,8... | collective-permute-start | bytes 589832 | tf_op jit(solution)/shard_map/ppermute | solution.py:44
  132.0 17.9 %all-to-all-start.3 = ((bf16[16,48,128]{2,1,0:T(8,128)(2,1)}), bf16[16,48,128]{2,1,0:T(8,128)(2,1)S(1)}, u32[]{:S(2)}, u32[]{:S(2)}) async-start(bf16[16,48,128]{2,1,0:T(8,128)(2,1)} %shard_map.103), calls=%async_computation.3 | async-start | bytes 393216 | tf_op jit(solution)/shard_map/all_to_all | solution.py:520
  (3 other events, 65.1 us)

commit v6 on v5

--- a/solution.py
+++ b/solution.py
@@ -127,23 +127,20 @@
     )(ids, parts)
 
 
-def join_blocks_kernel(a, b, c, d, after, low, high, mark):
+def all_arrived_kernel(a, b, c, mark):
     mark[...] = jnp.zeros_like(mark)
+
+
+def all_arrived(*values):
+    return call(all_arrived_kernel, shape((8, 128), f32), [VMEM] * 3)(*values)
+
+
+def join_blocks_kernel(a, b, c, d, loaded, swapped, low, high):
     low[0], low[1], high[0], high[1] = a[...], b[...], c[...], d[...]
 
 
 def join_blocks(*blocks):
-    outs = [shape((2, WIN, WIDE), bf16)] * 2 + [shape((8, 128), f32)]
-    return call(join_blocks_kernel, outs, [VMEM] * 5)(*blocks)
-
-
-def gate_kernel(low, high, after, out_low, out_high):
-    out_low[...] = low[...]
-    out_high[...] = high[...]
-
-
-def gate(low, high, after):
-    return call(gate_kernel, [shape(low.shape, low.dtype)] * 2, [VMEM] * 3)(low, high, after)
+    return call(join_blocks_kernel, [shape((2, WIN, WIDE), bf16)] * 2, [VMEM] * 6)(*blocks)
 
 
 def columns_of(rows):
@@ -488,8 +485,8 @@
     parts = lax.all_to_all(first_message(targets, hidden), ("z", "c"), 0, 0, tiled=True)
     block = join_window(ids, parts)
     head, mark = load_head(head_weight)
-    low, high, mark = join_blocks(block, *(fetch(block, middle(o)) for o in OFF[1:]), mark)
-    low, high = gate(low, high, fetch(mark, near))
+    around = [fetch(block, middle(o)) for o in OFF[1:]]
+    low, high = join_blocks(block, *around, mark, fetch(all_arrived(*around), near))
     ahead_low, back_high = fetch(low, final(1)), fetch(high, final(-1))
     ahead_high, back_low = fetch(high, final(1)), fetch(low, final(-1))
     far_low, far_high = fetch(ahead_low, final(1)), fetch(back_high, final(-1))

time: 151 us -> 153 us (1.013)
  no operation moved by 1% of the time
where the time goes in v6:
time: 153 us
  starting transfers between devices  49.9 us (33%)
  waiting for transfers between devices  43.9 us (29%)
  Pallas kernels  30.5 us (20%)
  blocking collectives  24.2 us (16%)
  local copies, waits for them, and re-layouts  3.11 us (2%)
    ppermute x29, starting transfers between devices, fetch(): return lax.ppermute(value, AXES, pairs)  32.4 us
    ppermute x29, waiting for transfers between devices, fetch(): return lax.ppermute(value, AXES, pairs)  22.5 us
    all_to_all x1, blocking collectives, exchange(): lax.all_to_all(jnp.broadcast_to(value[None], (16,) + value.shape), axes,...  12.7 us
    all_to_all x1, waiting for transfers between devices, local(): lax.all_to_all(first_message(targets, hidden), ('z', 'c'), 0, 0, tiled=True)  11.6 us
    all_to_all x1, blocking collectives, local(): stats = lax.all_to_all(stats, ('y', 'x'), 0, 0, tiled=True)  11.6 us
    all_to_all x1, starting transfers between devices, local(): lax.all_to_all(first_message(targets, hidden), ('z', 'c'), 0, 0, tiled=True)  9.98 us
    all_to_all x1, waiting for transfers between devices, local(): grad_hidden = finish(lax.all_to_all(parts, ('z', 'c'), 0, 0, tiled=True))  9.87 us
    pallas_call x2, Pallas kernels, grad_head_half(): pl.pallas_call(head_kernel, grid=(steps,), in_specs=[pl.BlockSpec((TOKENS...  8.76 us
  transfers between devices with their start and end apart: 31, of which 14 were waited for; matrix products, arithmetic and copies ran while one was open for 0% of the time, Pallas kernels for 10%

profile of v6, /device:TPU:1, one launch (start us, length us, event | category | flops | bytes accessed | tf_op | source)
XLA Modules:
  0.0 152.5 jit_solution(4448965879697814727)
XLA Ops:
  0.6 1.5 shard_map.85
  2.1 10.0 %all-to-all-start = ((bf16[16,64,128]{2,1,0:T(8,128)(2,1)}), bf16[16,64,128]{2,1,0:T(8,128)(2,1)S(1)}, u32[]{:S(2)}, u32[]{:S(2)}) async-start(bf16[16,64,128]{2,1,0:T(8,128)(2,1)} %shard_map.85), calls=%async_computation | async-start | bytes 524288 | tf_op jit(solution)/shard_map/all_to_all | solution.py:485
  12.2 11.6 %all-to-all-done.parts = bf16[16,64,128]{2,1,0:T(8,128)(2,1)S(1)} async-done(((bf16[16,64,128]{2,1,0:T(8,128)(2,1)}), bf16[16,64,128]{2,1,0:T(8,128)(2,1)S(1)}, u32[]{:S(2)}, u32[]{:S(2)}) %all-to-all-start) | async-done | bytes 262176 | tf_op jit(solution)/shard_map/all_to_all | solution.py:485
  24.5 2.8 %collective-permute-start.2 = (bf16[48,2176]{1,0:T(8,128)(2,1)S(1)}, bf16[48,2176]{1,0:T(8,128)(2,1)S(1)}, u32[]{:S(2)}, u32[]{:S(2)}) collective-permute-start(bf16[48,2176]{1,0:T(8,128)(2,1)S(1)} %shard_map.86.a), channel_id=1, source_target_pairs={{128,0},{33,1},{130,2},{35,3},{132,4},{37,5},{134,6},{39,7},{136,8... | collective-permute-start | bytes 626696 | tf_op jit(solution)/shard_map/ppermute | solution.py:44
  27.7 2.4 %collective-permute-start = (bf16[48,2176]{1,0:T(8,128)(2,1)S(1)}, bf16[48,2176]{1,0:T(8,128)(2,1)S(1)}, u32[]{:S(2)}, u32[]{:S(2)}) collective-permute-start(bf16[48,2176]{1,0:T(8,128)(2,1)S(1)} %shard_map.86.a), channel_id=1, source_target_pairs={{64,0},{17,1},{66,2},{19,3},{68,4},{21,5},{70,6},{23,7},{72,8},{25... | collective-permute-start | bytes 626696 | tf_op jit(solution)/shard_map/ppermute | solution.py:44
  31.1 2.5 %collective-permute-done.1.b.c = bf16[48,2176]{1,0:T(8,128)(2,1)S(1)} collective-permute-done((bf16[48,2176]{1,0:T(8,128)(2,1)S(1)}, bf16[48,2176]{1,0:T(8,128)(2,1)S(1)}, u32[]{:S(2)}, u32[]{:S(2)}) %collective-permute-start.1) | collective-permute-done | bytes 208928 | tf_op jit(solution)/shard_map/ppermute | solution.py:44
  34.4 2.5 %copy-done = bf16[4096,640]{1,0:T(8,128)(2,1)S(1)} copy-done((bf16[4096,640]{1,0:T(8,128)(2,1)S(1)}, bf16[4096,640]{1,0:T(8,128)(2,1)}, u32[]{:S(2)}) %copy-start) | copy-done | bytes 5242904
  38.3 2.2 %collective-permute-start.4 = (bf16[2,48,2176]{2,1,0:T(8,128)(2,1)S(1)}, bf16[2,48,2176]{2,1,0:T(8,128)(2,1)S(1)}, u32[]{:S(2)}, u32[]{:S(2)}) collective-permute-start(bf16[2,48,2176]{2,1,0:T(8,128)(2,1)S(1)} %get-tuple-element.37.refs_0_), channel_id=1, source_target_pairs={{16,0},{65,1},{18,2},{67,3},{20,4},{69,5},{22,6},{71,7},{24,8},{73... | collective-permute-start | bytes 1253384 | tf_op jit(solution)/shard_map/ppermute | solution.py:44
  41.5 3.0 %collective-permute-start.5 = (bf16[2,48,2176]{2,1,0:T(8,128)(2,1)S(1)}, bf16[2,48,2176]{2,1,0:T(8,128)(2,1)S(1)}, u32[]{:S(2)}, u32[]{:S(2)}) collective-permute-start(bf16[2,48,2176]{2,1,0:T(8,128)(2,1)S(1)} %get-tuple-element.38.refs_1_), channel_id=1, source_target_pairs={{16,0},{65,1},{18,2},{67,3},{20,4},{69,5},{22,6},{71,7},{24,8},{73... | collective-permute-start | bytes 1253384 | tf_op jit(solution)/shard_map/ppermute | solution.py:44
  44.4 1.8 %collective-permute-done.6.refs_4_ = bf16[2,48,2176]{2,1,0:T(8,128)(2,1)S(1)} collective-permute-done((bf16[2,48,2176]{2,1,0:T(8,128)(2,1)S(1)}, bf16[2,48,2176]{2,1,0:T(8,128)(2,1)S(1)}, u32[]{:S(2)}, u32[]{:S(2)}) %collective-permute-start.6) | collective-permute-done | bytes 417824 | tf_op jit(solution)/shard_map/ppermute | solution.py:44
  47.2 3.0 %collective-permute-start.8 = (bf16[2,48,2176]{2,1,0:T(8,128)(2,1)S(1)}, bf16[2,48,2176]{2,1,0:T(8,128)(2,1)S(1)}, u32[]{:S(2)}, u32[]{:S(2)}) collective-permute-start(bf16[2,48,2176]{2,1,0:T(8,128)(2,1)S(1)} %collective-permute-done.4.refs_2_), channel_id=1, source_target_pairs={{16,0},{65,1},{18,2},{67,3},{20,4},{69,5},{22,6},{71,7},{24,8},{73... | collective-permute-start | bytes 1253384 | tf_op jit(solution)/shard_map/ppermute | solution.py:44
  52.5 2.7 %collective-permute-done.8.refs_6_ = bf16[2,48,2176]{2,1,0:T(8,128)(2,1)S(1)} collective-permute-done((bf16[2,48,2176]{2,1,0:T(8,128)(2,1)S(1)}, bf16[2,48,2176]{2,1,0:T(8,128)(2,1)S(1)}, u32[]{:S(2)}, u32[]{:S(2)}) %collective-permute-start.8) | collective-permute-done | bytes 417824 | tf_op jit(solution)/shard_map/ppermute | solution.py:44
  56.4 2.6 %collective-permute-done.9.refs_7_ = bf16[2,48,2176]{2,1,0:T(8,128)(2,1)S(1)} collective-permute-done((bf16[2,48,2176]{2,1,0:T(8,128)(2,1)S(1)}, bf16[2,48,2176]{2,1,0:T(8,128)(2,1)S(1)}, u32[]{:S(2)}, u32[]{:S(2)}) %collective-permute-start.9) | collective-permute-done | bytes 417824 | tf_op jit(solution)/shard_map/ppermute | solution.py:44
  59.1 1.8 %collective-permute-start.17 = (bf16[2,48,2176]{2,1,0:T(8,128)(2,1)S(1)}, bf16[2,48,2176]{2,1,0:T(8,128)(2,1)S(1)}, u32[]{:S(2)}, u32[]{:S(2)}) collective-permute-start(bf16[2,48,2176]{2,1,0:T(8,128)(2,1)S(1)} %collective-permute-done.9.refs_7_), channel_id=1, source_target_pairs={{1,0},{0,1},{3,2},{2,3},{5,4},{4,5},{7,6},{6,7},{9,8},{8,9},{11,10... | collective-permute-start | bytes 1253384 | tf_op jit(solution)/shard_map/ppermute | solution.py:44
  60.9 1.4 collective-permute-done.17.refs_15_
  62.3 7.0 %shard_map.90 = (bf16[768,4096]{1,0:T(8,128)(2,1)S(1)}, f32[768,640]{1,0:T(8,128)S(1)}, f32[2,8,128]{2,1,0:T(8,128)S(1)}, f32[8,128]{1,0:T(8,128)S(1)}) custom-call(s32[5]{0:T(128)S(1)} %stack.23.ids, bf16[2,48,2176]{2,1,0:T(8,128)(2,1)S(1)} %get-tuple-element.37.refs_0_, bf16[2,48,2176]{2,1,0:T(8,128)(2,1)S(1)} %get-tuple-element.38.refs_1_, ...), custom_call_target="tpu_custom_call" | custom-call | flops 4026531840 | bytes 20971520 | tf_op jit(solution)/shard_map/pallas_call | solution.py:212
  69.3 12.7 %all_to_all.20.parts = f32[16,2,8,128]{3,2,1,0:T(8,128)S(1)} all-to-all(f32[16,2,8,128]{3,2,1,0:T(8,128)S(1)} %broadcast_in_dim.2), channel_id=1, replica_groups=mesh['y'=4,'x'=4,'z'=8,'c'=2] {'z','c'}, dimensions={0} | all-to-all | bytes 262144 | tf_op jit(solution)/shard_map/all_to_all | solution.py:232
  82.0 11.6 %all_to_all.21.parts = f32[16,2,8,128]{3,2,1,0:T(8,128)S(1)} all-to-all(f32[16,2,8,128]{3,2,1,0:T(8,128)S(1)} %shard_map.91), channel_id=1, replica_groups=mesh['y'=4,'x'=4,'z'=8,'c'=2] {'y','x'}, dimensions={0} | all-to-all | bytes 262144 | tf_op jit(solution)/shard_map/all_to_all | solution.py:498
  94.4 2.6 %shard_map.93 = (bf16[768,640]{1,0:T(8,128)(2,1)S(1)}, bf16[768,1024]{1,0:T(8,128)(2,1)S(1)}) custom-call(s32[5]{0:T(128)S(1)} %stack.23.ids, f32[768,640]{1,0:T(8,128)S(1)} %get-tuple-element.40.logits, f32[8,128]{1,0:T(8,128)S(1)} %get-tuple-element.42.norm, f32[8,128]{1,0:T(8,128)S(1)} %get-tuple-element.43.weight, ...), custom_call_target="tpu_custom_call" | custom-call | flops 1006632960 | bytes 6291456 | tf_op jit(solution)/shard_map/pallas_call | solution.py:323
  97.9 2.0 %shard_map.95 = bf16[768,1024]{1,0:T(8,128)(2,1)S(1)} custom-call(s32[5]{0:T(128)S(1)} %stack.23.ids, bf16[768,640]{1,0:T(8,128)(2,1)S(1)} %get-tuple-element.45.grad, bf16[4096,640]{1,0:T(8,128)(2,1)S(1)} %get-tuple-element.39.refs_16_.head), custom_call_target="tpu_custom_call" | custom-call | flops 2013265920 | bytes 16777216 | tf_op jit(solution)/shard_map/pallas_call | solution.py:334
  100.2 3.2 %shard_map.94.own = f32[768,2048]{1,0:T(8,128)S(1)} custom-call(s32[5]{0:T(128)S(1)} %stack.23.ids, bf16[768,640]{1,0:T(8,128)(2,1)S(1)} %get-tuple-element.45.grad, bf16[4096,640]{1,0:T(8,128)(2,1)S(1)} %get-tuple-element.39.refs_16_.head), custom_call_target="tpu_custom_call" | custom-call | flops 2013265920 | bytes 10485760 | tf_op jit(solution)/shard_map/pallas_call | solution.py:358
  106.2 1.8 %collective-permute-start.22 = (bf16[2,48,2048]{2,1,0:T(8,128)(2,1)S(1)}, bf16[2,48,2048]{2,1,0:T(8,128)(2,1)S(1)}, u32[]{:S(2)}, u32[]{:S(2)}) collective-permute-start(bf16[2,48,2048]{2,1,0:T(8,128)(2,1)S(1)} %get-tuple-element.54), channel_id=1, source_target_pairs={{16,0},{65,1},{18,2},{67,3},{20,4},{69,5},{22,6},{71,7},{24,8},{73... | collective-permute-start | bytes 1179656 | tf_op jit(solution)/shard_map/ppermute | solution.py:44
  108.0 4.4 %shard_map.98 = (bf16[4096,640]{1,0:T(8,128)(2,1)}, f32[8,128]{1,0:T(8,128)S(1)}) custom-call(bf16[768,4096]{1,0:T(8,128)(2,1)S(1)} %get-tuple-element.50.hidden, bf16[768,640]{1,0:T(8,128)(2,1)S(1)} %get-tuple-element.45.grad, f32[8,128]{1,0:T(8,128)S(1)} %get-tuple-element.51.refs_0_), custom_call_target="tpu_custom_call" | custom-call | flops 2013265920 | bytes 6291456 | tf_op jit(solution)/shard_map/pallas_call | solution.py:403
  112.5 2.8 %collective-permute-start.25 = (bf16[2,48,2048]{2,1,0:T(8,128)(2,1)S(1)}, bf16[2,48,2048]{2,1,0:T(8,128)(2,1)S(1)}, u32[]{:S(2)}, u32[]{:S(2)}) collective-permute-start(bf16[2,48,2048]{2,1,0:T(8,128)(2,1)S(1)} %get-tuple-element.59), channel_id=1, source_target_pairs={{16,0},{65,1},{18,2},{67,3},{20,4},{69,5},{22,6},{71,7},{24,8},{73... | collective-permute-start | bytes 1179656 | tf_op jit(solution)/shard_map/ppermute | solution.py:44
  115.9 4.4 %shard_map.101 = (bf16[4096,640]{1,0:T(8,128)(2,1)}, f32[8,128]{1,0:T(8,128)S(1)}) custom-call(bf16[768,4096]{1,0:T(8,128)(2,1)S(1)} %get-tuple-element.50.hidden, bf16[768,640]{1,0:T(8,128)(2,1)S(1)} %get-tuple-element.45.grad, f32[8,128]{1,0:T(8,128)S(1)} %get-tuple-element.60.refs_0_, ...), custom_call_target="tpu_custom_call", output_to_operand_aliasing={{0}: (3, {})} | custom-call | flops 2013265920 | bytes 6291456 | tf_op jit(solution)/shard_map/pallas_call | solution.py:403
  120.3 3.7 %collective-permute-done.21.refs_1_ = bf16[2,48,2048]{2,1,0:T(8,128)(2,1)S(1)} collective-permute-done((bf16[2,48,2048]{2,1,0:T(8,128)(2,1)S(1)}, bf16[2,48,2048]{2,1,0:T(8,128)(2,1)S(1)}, u32[]{:S(2)}, u32[]{:S(2)}) %collective-permute-start.21) | collective-permute-done | bytes 393248 | tf_op jit(solution)/shard_map/ppermute | solution.py:44
  124.3 2.7 %collective-permute-start.27 = (bf16[48,2048]{1,0:T(8,128)(2,1)S(1)}, bf16[48,2048]{1,0:T(8,128)(2,1)S(1)}, u32[]{:S(2)}, u32[]{:S(2)}) collective-permute-start(bf16[48,2048]{1,0:T(8,128)(2,1)S(1)} %get-tuple-element.65), channel_id=1, source_target_pairs={{64,0},{17,1},{66,2},{19,3},{68,4},{21,5},{70,6},{23,7},{72,8},{25... | collective-permute-start | bytes 589832 | tf_op jit(solution)/shard_map/ppermute | solution.py:44
  127.0 3.1 %collective-permute-done.26.b = bf16[48,2048]{1,0:T(8,128)(2,1)S(1)} collective-permute-done((bf16[48,2048]{1,0:T(8,128)(2,1)S(1)}, bf16[48,2048]{1,0:T(8,128)(2,1)S(1)}, u32[]{:S(2)}, u32[]{:S(2)}) %collective-permute-start.26) | collective-permute-done | bytes 196640 | tf_op jit(solution)/shard_map/ppermute | solution.py:44
  130.0 1.7 %collective-permute-done.27.c = bf16[48,2048]{1,0:T(8,128)(2,1)S(1)} collective-permute-done((bf16[48,2048]{1,0:T(8,128)(2,1)S(1)}, bf16[48,2048]{1,0:T(8,128)(2,1)S(1)}, u32[]{:S(2)}, u32[]{:S(2)}) %collective-permute-start.27) | collective-permute-done | bytes 196640 | tf_op jit(solution)/shard_map/ppermute | solution.py:44
  131.7 1.3 collective-permute-done.28.d
  133.9 7.6 %all-to-all-start.3 = ((bf16[16,48,128]{2,1,0:T(8,128)(2,1)}), bf16[16,48,128]{2,1,0:T(8,128)(2,1)S(1)}, u32[]{:S(2)}, u32[]{:S(2)}) async-start(bf16[16,48,128]{2,1,0:T(8,128)(2,1)} %shard_map.103), calls=%async_computation.3 | async-start | bytes 393216 | tf_op jit(solution)/shard_map/all_to_all | solution.py:517
  142.0 9.9 %all-to-all-done.3.parts = bf16[16,48,128]{2,1,0:T(8,128)(2,1)S(1)} async-done(((bf16[16,48,128]{2,1,0:T(8,128)(2,1)}), bf16[16,48,128]{2,1,0:T(8,128)(2,1)S(1)}, u32[]{:S(2)}, u32[]{:S(2)}) %all-to-all-start.3) | async-done | bytes 196640 | tf_op jit(solution)/shard_map/all_to_all | solution.py:517
  (63 shorter events, 18.0 us)
Async XLA Ops:
  2.1 21.7 %all-to-all-start = ((bf16[16,64,128]{2,1,0:T(8,128)(2,1)}), bf16[16,64,128]{2,1,0:T(8,128)(2,1)S(1)}, u32[]{:S(2)}, u32[]{:S(2)}) async-start(bf16[16,64,128]{2,1,0:T(8,128)(2,1)} %shard_map.85), calls=%async_computation | async-start | bytes 524288 | tf_op jit(solution)/shard_map/all_to_all | solution.py:485
  24.5 6.5 %collective-permute-start.2 = (bf16[48,2176]{1,0:T(8,128)(2,1)S(1)}, bf16[48,2176]{1,0:T(8,128)(2,1)S(1)}, u32[]{:S(2)}, u32[]{:S(2)}) collective-permute-start(bf16[48,2176]{1,0:T(8,128)(2,1)S(1)} %shard_map.86.a), channel_id=1, source_target_pairs={{128,0},{33,1},{130,2},{35,3},{132,4},{37,5},{134,6},{39,7},{136,8... | collective-permute-start | bytes 626696 | tf_op jit(solution)/shard_map/ppermute | solution.py:44
  27.4 6.2 %collective-permute-start.1 = (bf16[48,2176]{1,0:T(8,128)(2,1)S(1)}, bf16[48,2176]{1,0:T(8,128)(2,1)S(1)}, u32[]{:S(2)}, u32[]{:S(2)}) collective-permute-start(bf16[48,2176]{1,0:T(8,128)(2,1)S(1)} %shard_map.86.a), channel_id=1, source_target_pairs={{192,0},{49,1},{194,2},{51,3},{196,4},{53,5},{198,6},{55,7},{200,8... | collective-permute-start | bytes 626696 | tf_op jit(solution)/shard_map/ppermute | solution.py:44
  27.7 5.8 %collective-permute-start = (bf16[48,2176]{1,0:T(8,128)(2,1)S(1)}, bf16[48,2176]{1,0:T(8,128)(2,1)S(1)}, u32[]{:S(2)}, u32[]{:S(2)}) collective-permute-start(bf16[48,2176]{1,0:T(8,128)(2,1)S(1)} %shard_map.86.a), channel_id=1, source_target_pairs={{64,0},{17,1},{66,2},{19,3},{68,4},{21,5},{70,6},{23,7},{72,8},{25... | collective-permute-start | bytes 626696 | tf_op jit(solution)/shard_map/ppermute | solution.py:44
  33.5 3.7 %collective-permute-start.3 = (f32[8,128]{1,0:T(8,128)S(1)}, f32[8,128]{1,0:T(8,128)S(1)}, u32[]{:S(2)}, u32[]{:S(2)}) collective-permute-start(f32[8,128]{1,0:T(8,128)S(1)} %shard_map.88), channel_id=1, source_target_pairs={{1,0},{0,1},{3,2},{2,3},{5,4},{4,5},{7,6},{6,7},{9,8},{8,9},{11,10... | collective-permute-start | bytes 12296 | tf_op jit(solution)/shard_map/ppermute | solution.py:44
  37.3 4.1 %collective-permute-start.10 = (bf16[2,48,2176]{2,1,0:T(8,128)(2,1)S(1)}, bf16[2,48,2176]{2,1,0:T(8,128)(2,1)S(1)}, u32[]{:S(2)}, u32[]{:S(2)}) collective-permute-start(bf16[2,48,2176]{2,1,0:T(8,128)(2,1)S(1)} %get-tuple-element.37.refs_0_), channel_id=1, source_target_pairs={{1,0},{0,1},{3,2},{2,3},{5,4},{4,5},{7,6},{6,7},{9,8},{8,9},{11,10... | collective-permute-start | bytes 1253384 | tf_op jit(solution)/shard_map/ppermute | solution.py:44
  37.4 8.8 %collective-permute-start.6 = (bf16[2,48,2176]{2,1,0:T(8,128)(2,1)S(1)}, bf16[2,48,2176]{2,1,0:T(8,128)(2,1)S(1)}, u32[]{:S(2)}, u32[]{:S(2)}) collective-permute-start(bf16[2,48,2176]{2,1,0:T(8,128)(2,1)S(1)} %get-tuple-element.37.refs_0_), channel_id=1, source_target_pairs={{48,0},{193,1},{50,2},{195,3},{52,4},{197,5},{54,6},{199,7},{56,8}... | collective-permute-start | bytes 1253384 | tf_op jit(solution)/shard_map/ppermute | solution.py:44
  38.3 8.9 %collective-permute-start.4 = (bf16[2,48,2176]{2,1,0:T(8,128)(2,1)S(1)}, bf16[2,48,2176]{2,1,0:T(8,128)(2,1)S(1)}, u32[]{:S(2)}, u32[]{:S(2)}) collective-permute-start(bf16[2,48,2176]{2,1,0:T(8,128)(2,1)S(1)} %get-tuple-element.37.refs_0_), channel_id=1, source_target_pairs={{16,0},{65,1},{18,2},{67,3},{20,4},{69,5},{22,6},{71,7},{24,8},{73... | collective-permute-start | bytes 1253384 | tf_op jit(solution)/shard_map/ppermute | solution.py:44
  40.6 10.1 %collective-permute-start.7 = (bf16[2,48,2176]{2,1,0:T(8,128)(2,1)S(1)}, bf16[2,48,2176]{2,1,0:T(8,128)(2,1)S(1)}, u32[]{:S(2)}, u32[]{:S(2)}) collective-permute-start(bf16[2,48,2176]{2,1,0:T(8,128)(2,1)S(1)} %get-tuple-element.38.refs_1_), channel_id=1, source_target_pairs={{48,0},{193,1},{50,2},{195,3},{52,4},{197,5},{54,6},{199,7},{56,8}... | collective-permute-start | bytes 1253384 | tf_op jit(solution)/shard_map/ppermute | solution.py:44
  40.6 10.1 %collective-permute-start.11 = (bf16[2,48,2176]{2,1,0:T(8,128)(2,1)S(1)}, bf16[2,48,2176]{2,1,0:T(8,128)(2,1)S(1)}, u32[]{:S(2)}, u32[]{:S(2)}) collective-permute-start(bf16[2,48,2176]{2,1,0:T(8,128)(2,1)S(1)} %get-tuple-element.38.refs_1_), channel_id=1, source_target_pairs={{1,0},{0,1},{3,2},{2,3},{5,4},{4,5},{7,6},{6,7},{9,8},{8,9},{11,10... | collective-permute-start | bytes 1253384 | tf_op jit(solution)/shard_map/ppermute | solution.py:44
  41.5 10.5 %collective-permute-start.5 = (bf16[2,48,2176]{2,1,0:T(8,128)(2,1)S(1)}, bf16[2,48,2176]{2,1,0:T(8,128)(2,1)S(1)}, u32[]{:S(2)}, u32[]{:S(2)}) collective-permute-start(bf16[2,48,2176]{2,1,0:T(8,128)(2,1)S(1)} %get-tuple-element.38.refs_1_), channel_id=1, source_target_pairs={{16,0},{65,1},{18,2},{67,3},{20,4},{69,5},{22,6},{71,7},{24,8},{73... | collective-permute-start | bytes 1253384 | tf_op jit(solution)/shard_map/ppermute | solution.py:44
  46.2 5.9 %collective-permute-start.14 = (bf16[2,48,2176]{2,1,0:T(8,128)(2,1)S(1)}, bf16[2,48,2176]{2,1,0:T(8,128)(2,1)S(1)}, u32[]{:S(2)}, u32[]{:S(2)}) collective-permute-start(bf16[2,48,2176]{2,1,0:T(8,128)(2,1)S(1)} %collective-permute-done.6.refs_4_), channel_id=1, source_target_pairs={{1,0},{0,1},{3,2},{2,3},{5,4},{4,5},{7,6},{6,7},{9,8},{8,9},{11,10... | collective-permute-start | bytes 1253384 | tf_op jit(solution)/shard_map/ppermute | solution.py:44
  47.2 7.9 %collective-permute-start.8 = (bf16[2,48,2176]{2,1,0:T(8,128)(2,1)S(1)}, bf16[2,48,2176]{2,1,0:T(8,128)(2,1)S(1)}, u32[]{:S(2)}, u32[]{:S(2)}) collective-permute-start(bf16[2,48,2176]{2,1,0:T(8,128)(2,1)S(1)} %collective-permute-done.4.refs_2_), channel_id=1, source_target_pairs={{16,0},{65,1},{18,2},{67,3},{20,4},{69,5},{22,6},{71,7},{24,8},{73... | collective-permute-start | bytes 1253384 | tf_op jit(solution)/shard_map/ppermute | solution.py:44
  50.7 8.4 %collective-permute-start.9 = (bf16[2,48,2176]{2,1,0:T(8,128)(2,1)S(1)}, bf16[2,48,2176]{2,1,0:T(8,128)(2,1)S(1)}, u32[]{:S(2)}, u32[]{:S(2)}) collective-permute-start(bf16[2,48,2176]{2,1,0:T(8,128)(2,1)S(1)} %collective-permute-done.7.refs_5_), channel_id=1, source_target_pairs={{48,0},{193,1},{50,2},{195,3},{52,4},{197,5},{54,6},{199,7},{56,8}... | collective-permute-start | bytes 1253384 | tf_op jit(solution)/shard_map/ppermute | solution.py:44
  50.7 10.2 %collective-permute-start.12 = (bf16[2,48,2176]{2,1,0:T(8,128)(2,1)S(1)}, bf16[2,48,2176]{2,1,0:T(8,128)(2,1)S(1)}, u32[]{:S(2)}, u32[]{:S(2)}) collective-permute-start(bf16[2,48,2176]{2,1,0:T(8,128)(2,1)S(1)} %collective-permute-done.4.refs_2_), channel_id=1, source_target_pairs={{1,0},{0,1},{3,2},{2,3},{5,4},{4,5},{7,6},{6,7},{9,8},{8,9},{11,10... | collective-permute-start | bytes 1253384 | tf_op jit(solution)/shard_map/ppermute | solution.py:44
  52.0 9.0 %collective-permute-start.15 = (bf16[2,48,2176]{2,1,0:T(8,128)(2,1)S(1)}, bf16[2,48,2176]{2,1,0:T(8,128)(2,1)S(1)}, u32[]{:S(2)}, u32[]{:S(2)}) collective-permute-start(bf16[2,48,2176]{2,1,0:T(8,128)(2,1)S(1)} %collective-permute-done.7.refs_5_), channel_id=1, source_target_pairs={{1,0},{0,1},{3,2},{2,3},{5,4},{4,5},{7,6},{6,7},{9,8},{8,9},{11,10... | collective-permute-start | bytes 1253384 | tf_op jit(solution)/shard_map/ppermute | solution.py:44
  52.1 8.9 %collective-permute-start.13 = (bf16[2,48,2176]{2,1,0:T(8,128)(2,1)S(1)}, bf16[2,48,2176]{2,1,0:T(8,128)(2,1)S(1)}, u32[]{:S(2)}, u32[]{:S(2)}) collective-permute-start(bf16[2,48,2176]{2,1,0:T(8,128)(2,1)S(1)} %collective-permute-done.5.refs_3_), channel_id=1, source_target_pairs={{1,0},{0,1},{3,2},{2,3},{5,4},{4,5},{7,6},{6,7},{9,8},{8,9},{11,10... | collective-permute-start | bytes 1253384 | tf_op jit(solution)/shard_map/ppermute | solution.py:44
  55.1 5.8 %collective-permute-start.16 = (bf16[2,48,2176]{2,1,0:T(8,128)(2,1)S(1)}, bf16[2,48,2176]{2,1,0:T(8,128)(2,1)S(1)}, u32[]{:S(2)}, u32[]{:S(2)}) collective-permute-start(bf16[2,48,2176]{2,1,0:T(8,128)(2,1)S(1)} %collective-permute-done.8.refs_6_), channel_id=1, source_target_pairs={{1,0},{0,1},{3,2},{2,3},{5,4},{4,5},{7,6},{6,7},{9,8},{8,9},{11,10... | collective-permute-start | bytes 1253384 | tf_op jit(solution)/shard_map/ppermute | solution.py:44
  59.1 3.2 %collective-permute-start.17 = (bf16[2,48,2176]{2,1,0:T(8,128)(2,1)S(1)}, bf16[2,48,2176]{2,1,0:T(8,128)(2,1)S(1)}, u32[]{:S(2)}, u32[]{:S(2)}) collective-permute-start(bf16[2,48,2176]{2,1,0:T(8,128)(2,1)S(1)} %collective-permute-done.9.refs_7_), channel_id=1, source_target_pairs={{1,0},{0,1},{3,2},{2,3},{5,4},{4,5},{7,6},{6,7},{9,8},{8,9},{11,10... | collective-permute-start | bytes 1253384 | tf_op jit(solution)/shard_map/ppermute | solution.py:44
  62.3 31.3 %copy-start.3 = (s32[16]{0:T(128)S(1)}, s32[16]{0:T(128)}, u32[]{:S(2)}) copy-start(s32[16]{0:T(128)} %pairing.1) | copy-start | bytes 196
  97.0 6.4 %collective-permute-start.18 = (bf16[768,1024]{1,0:T(8,128)(2,1)S(1)}, bf16[768,1024]{1,0:T(8,128)(2,1)S(1)}, u32[]{:S(2)}, u32[]{:S(2)}) collective-permute-start(bf16[768,1024]{1,0:T(8,128)(2,1)S(1)} %get-tuple-element.46), channel_id=1, source_target_pairs={{1,0},{0,1},{3,2},{2,3},{5,4},{4,5},{7,6},{6,7},{9,8},{8,9},{11,10... | collective-permute-start | bytes 4718600 | tf_op jit(solution)/shard_map/ppermute | solution.py:44
  99.9 3.7 %collective-permute-start.19 = (bf16[768,1024]{1,0:T(8,128)(2,1)S(1)}, bf16[768,1024]{1,0:T(8,128)(2,1)S(1)}, u32[]{:S(2)}, u32[]{:S(2)}) collective-permute-start(bf16[768,1024]{1,0:T(8,128)(2,1)S(1)} %shard_map.95), channel_id=1, source_target_pairs={{1,0},{0,1},{3,2},{2,3},{5,4},{4,5},{7,6},{6,7},{9,8},{8,9},{11,10... | collective-permute-start | bytes 4718600 | tf_op jit(solution)/shard_map/ppermute | solution.py:44
  104.7 7.7 %collective-permute-start.24 = (bf16[2,48,2048]{2,1,0:T(8,128)(2,1)S(1)}, bf16[2,48,2048]{2,1,0:T(8,128)(2,1)S(1)}, u32[]{:S(2)}, u32[]{:S(2)}) collective-permute-start(bf16[2,48,2048]{2,1,0:T(8,128)(2,1)S(1)} %get-tuple-element.58), channel_id=1, source_target_pairs={{16,0},{65,1},{18,2},{67,3},{20,4},{69,5},{22,6},{71,7},{24,8},{73... | collective-permute-start | bytes 1179656 | tf_op jit(solution)/shard_map/ppermute | solution.py:44
  105.3 9.9 %collective-permute-start.20 = (bf16[2,48,2048]{2,1,0:T(8,128)(2,1)S(1)}, bf16[2,48,2048]{2,1,0:T(8,128)(2,1)S(1)}, u32[]{:S(2)}, u32[]{:S(2)}) collective-permute-start(bf16[2,48,2048]{2,1,0:T(8,128)(2,1)S(1)} %get-tuple-element.49), channel_id=1, source_target_pairs={{48,0},{193,1},{50,2},{195,3},{52,4},{197,5},{54,6},{199,7},{56,8}... | collective-permute-start | bytes 1179656 | tf_op jit(solution)/shard_map/ppermute | solution.py:44
  106.2 14.0 %collective-permute-start.22 = (bf16[2,48,2048]{2,1,0:T(8,128)(2,1)S(1)}, bf16[2,48,2048]{2,1,0:T(8,128)(2,1)S(1)}, u32[]{:S(2)}, u32[]{:S(2)}) collective-permute-start(bf16[2,48,2048]{2,1,0:T(8,128)(2,1)S(1)} %get-tuple-element.54), channel_id=1, source_target_pairs={{16,0},{65,1},{18,2},{67,3},{20,4},{69,5},{22,6},{71,7},{24,8},{73... | collective-permute-start | bytes 1179656 | tf_op jit(solution)/shard_map/ppermute | solution.py:44
  108.0 12.3 %collective-permute-start.23 = (bf16[2,48,2048]{2,1,0:T(8,128)(2,1)S(1)}, bf16[2,48,2048]{2,1,0:T(8,128)(2,1)S(1)}, u32[]{:S(2)}, u32[]{:S(2)}) collective-permute-start(bf16[2,48,2048]{2,1,0:T(8,128)(2,1)S(1)} %get-tuple-element.56), channel_id=1, source_target_pairs={{48,0},{193,1},{50,2},{195,3},{52,4},{197,5},{54,6},{199,7},{56,8}... | collective-permute-start | bytes 1179656 | tf_op jit(solution)/shard_map/ppermute | solution.py:44
  112.5 7.8 %collective-permute-start.25 = (bf16[2,48,2048]{2,1,0:T(8,128)(2,1)S(1)}, bf16[2,48,2048]{2,1,0:T(8,128)(2,1)S(1)}, u32[]{:S(2)}, u32[]{:S(2)}) collective-permute-start(bf16[2,48,2048]{2,1,0:T(8,128)(2,1)S(1)} %get-tuple-element.59), channel_id=1, source_target_pairs={{16,0},{65,1},{18,2},{67,3},{20,4},{69,5},{22,6},{71,7},{24,8},{73... | collective-permute-start | bytes 1179656 | tf_op jit(solution)/shard_map/ppermute | solution.py:44
  115.9 8.1 %collective-permute-start.21 = (bf16[2,48,2048]{2,1,0:T(8,128)(2,1)S(1)}, bf16[2,48,2048]{2,1,0:T(8,128)(2,1)S(1)}, u32[]{:S(2)}, u32[]{:S(2)}) collective-permute-start(bf16[2,48,2048]{2,1,0:T(8,128)(2,1)S(1)} %get-tuple-element.53), channel_id=1, source_target_pairs={{48,0},{193,1},{50,2},{195,3},{52,4},{197,5},{54,6},{199,7},{56,8}... | collective-permute-start | bytes 1179656 | tf_op jit(solution)/shard_map/ppermute | solution.py:44
  124.2 5.8 %collective-permute-start.26 = (bf16[48,2048]{1,0:T(8,128)(2,1)S(1)}, bf16[48,2048]{1,0:T(8,128)(2,1)S(1)}, u32[]{:S(2)}, u32[]{:S(2)}) collective-permute-start(bf16[48,2048]{1,0:T(8,128)(2,1)S(1)} %get-tuple-element.64), channel_id=1, source_target_pairs={{192,0},{49,1},{194,2},{51,3},{196,4},{53,5},{198,6},{55,7},{200,8... | collective-permute-start | bytes 589832 | tf_op jit(solution)/shard_map/ppermute | solution.py:44
  124.3 7.4 %collective-permute-start.27 = (bf16[48,2048]{1,0:T(8,128)(2,1)S(1)}, bf16[48,2048]{1,0:T(8,128)(2,1)S(1)}, u32[]{:S(2)}, u32[]{:S(2)}) collective-permute-start(bf16[48,2048]{1,0:T(8,128)(2,1)S(1)} %get-tuple-element.65), channel_id=1, source_target_pairs={{64,0},{17,1},{66,2},{19,3},{68,4},{21,5},{70,6},{23,7},{72,8},{25... | collective-permute-start | bytes 589832 | tf_op jit(solution)/shard_map/ppermute | solution.py:44
  127.0 6.0 %collective-permute-start.28 = (bf16[48,2048]{1,0:T(8,128)(2,1)S(1)}, bf16[48,2048]{1,0:T(8,128)(2,1)S(1)}, u32[]{:S(2)}, u32[]{:S(2)}) collective-permute-start(bf16[48,2048]{1,0:T(8,128)(2,1)S(1)} %get-tuple-element.66), channel_id=1, source_target_pairs={{128,0},{33,1},{130,2},{35,3},{132,4},{37,5},{134,6},{39,7},{136,8... | collective-permute-start | bytes 589832 | tf_op jit(solution)/shard_map/ppermute | solution.py:44
  133.9 17.9 %all-to-all-start.3 = ((bf16[16,48,128]{2,1,0:T(8,128)(2,1)}), bf16[16,48,128]{2,1,0:T(8,128)(2,1)S(1)}, u32[]{:S(2)}, u32[]{:S(2)}) async-start(bf16[16,48,128]{2,1,0:T(8,128)(2,1)} %shard_map.103), calls=%async_computation.3 | async-start | bytes 393216 | tf_op jit(solution)/shard_map/all_to_all | solution.py:517
  (3 other events, 65.1 us)
